TPU v7x, 1024 devices: a whole 8x8x8 slice. The times are simulated.
1024 devices in a mesh: expert: 32 (over z_hi, x), dp: 32 (over y, z_lo, core).
Axes of the slice: x: 8, y: 8, z: 8 (z_hi: 4, z_lo: 2; z = z_hi * 2 + z_lo), core: 2. Of those that a mesh axis runs over, the one named last changes fastest.
Arguments:
- grad_output: bfloat16 [131072, 2048], P(('expert', 'dp')), may hold values from -1.5 to 1.5
- logits: float32 [131072, 8], P(('expert', 'dp')), may hold values from -6 to 6
- chosen: int32 [131072, 8], P(('expert', 'dp')), may hold values from 0 to 127, as said below
- slots: int32 [131072, 8], P(('expert', 'dp')), may hold values from 0 to 10, as said below
- other_scores: float32 [131072, 8], P(('expert', 'dp')), may hold values from -48 to 48
- hidden: bfloat16 [32, 32, 32, 10, 768], P('expert', 'dp'), may hold values from -6 to 6
- down_weight: bfloat16 [32, 768, 2048], P('expert', 'dp'), may hold values from -0.21875 to 0.21875
Outputs:
- grad_hidden: bfloat16 [32, 32, 32, 10, 768], P('expert', 'dp')
- grad_down: float32 [32, 768, 2048], P('expert', 'dp')
- grad_logits: float32 [131072, 8], P(('expert', 'dp'))
Inputs may be any that keep to these rules, and one draw needn't show every extreme that they name: `chosen`: each row names 8 different experts. 10 marks a choice with no slot: its expert is 32 or above, or it comes after 10 earlier choices of the same expert among the rows of one device in row-major order. The live choices of one expert on one device hold slots 0, 1, 2, ... in that order. Some expert fills all 10 slots on some device.
All inputs are finite; a program needn't handle non-finite values.
Results may differ from a plain program's by a relative error of at most 0.023.
Values may be sent and summed in bfloat16 or wider, within the bound.
No kernel may reach another device: no remote copies, remote signals or barrier semaphores. Data moves between devices by JAX's collectives and lax.ppermute only.
A program may use at most 32 MiB of HBM per device.

v0:
```python
import math

import jax
import jax.numpy as jnp
from jax import lax
from jax.sharding import Mesh
from jax.sharding import PartitionSpec as P

DP = ("dp_0", "dp_1", "dp_2")
EXPERT_DP = ("expert", "dp_0", "dp_1", "dp_2")


def sent_together(arrays, axis, split_dim, concat_dim, along):
    widths = [math.prod(a.shape[along:]) for a in arrays]
    both = jnp.concatenate(
        [a.reshape(*a.shape[:along], w) for a, w in zip(arrays, widths)], axis=along
    )
    result = lax.all_to_all(both, axis, split_axis=split_dim, concat_axis=concat_dim, tiled=True)
    tiles = jnp.split(result, [sum(widths[:k]) for k in range(1, len(widths))], axis=along)
    return tuple(
        (b.reshape(*result.shape[:along], *a.shape[along:]) for a, b in zip(arrays, tiles))
    )


def laid_out(tiles, dim):
    tiles = jnp.moveaxis(tiles, 0, dim)
    lengths = tiles.shape
    return tiles.reshape(*lengths[:dim], lengths[dim] * lengths[dim + 1], *lengths[dim + 2 :])


def all_blocks(array, axes, turns):
    tiles = array
    for k in turns:
        tiles = lax.all_gather(tiles, axes[k])
    done = turns[::-1]
    back = [done.index(k) for k in range(len(axes))]
    tiles = tiles.transpose(*back, *range(len(axes), tiles.ndim))
    return tiles.reshape(-1, *array.shape)


def gathered_by_axis(array, axes, turns, dim):
    return laid_out(all_blocks(array, axes, turns), dim)


def split_up(array, dim, length):
    lengths = array.shape
    tiles = array.reshape(*lengths[:dim], length, lengths[dim] // length, *lengths[dim + 1 :])
    return jnp.moveaxis(tiles, dim, 0)


def sum_at_owner(array, axis, dim):
    tiles = split_up(array, dim, lax.axis_size(axis))
    arrived = lax.all_to_all(tiles, axis, split_axis=0, concat_axis=0, tiled=True)
    return arrived.astype(jnp.float32).sum(axis=0)


def body(grad_output, logits, chosen, slots, other_scores, hidden, down_weight):
    window = lax.axis_size("expert")
    capacity = hidden.shape[3]
    hidden_units = hidden.shape[4]
    model_width = grad_output.shape[1]
    shard_rows = down_weight.shape[1]
    raised = jnp.exp(logits)
    gating = raised / jnp.sum(raised, axis=1, keepdims=True)
    gate_sent = gating.astype(jnp.bfloat16)
    live_slot = slots < capacity
    target = jnp.where(live_slot, chosen * capacity + slots, window * capacity)
    columns = jnp.arange(window * capacity, dtype=jnp.int32)
    placing = (target[:, :, None] == columns[None, None, :]).astype(jnp.bfloat16)
    dispatch = jnp.sum(placing, axis=1)
    send_rows = jnp.einsum(
        "tr,td->rd", dispatch, grad_output, preferred_element_type=jnp.float32
    ).astype(jnp.bfloat16)
    send_gate = jnp.einsum(
        "tkr,tk->r", placing, gate_sent, preferred_element_type=jnp.float32
    ).astype(jnp.bfloat16)
    placing_float = placing.astype(jnp.float32)
    send_rows = send_rows.reshape(window, capacity, model_width)
    send_gate = send_gate.reshape(window, capacity)
    recv_rows, recv_gate = sent_together((send_rows, send_gate), "expert", 0, 0, 2)
    slot_rows = recv_rows.reshape(-1, model_width)
    slot_gate = recv_gate.reshape(-1).astype(jnp.float32)
    local_hidden = hidden.reshape(-1, hidden_units)
    scaled = (slot_gate[:, None] * slot_rows.astype(jnp.float32)).astype(jnp.bfloat16)
    weights = down_weight.reshape(shard_rows, model_width)
    product = lax.dot_general(
        slot_rows,
        gathered_by_axis(weights, DP, (1, 0, 2), 0),
        (((1,), (1,)), ((), ())),
        preferred_element_type=jnp.float32,
    )
    grad_rows = sum_at_owner(
        lax.dot_general(
            local_hidden, scaled, (((0,), (0,)), ((), ())), preferred_element_type=jnp.float32
        ).astype(jnp.bfloat16),
        DP,
        0,
    )
    slot_scores = jnp.sum(local_hidden.astype(jnp.float32) * product, axis=1)
    grad_hidden = (slot_gate[:, None] * product).astype(jnp.bfloat16).reshape(hidden.shape)
    returned = lax.all_to_all(
        slot_scores.reshape(window, capacity), "expert", split_axis=0, concat_axis=0, tiled=True
    )
    token_scores = jnp.einsum(
        "tkr,r->tk", placing_float, returned.reshape(-1), precision=lax.Precision.HIGHEST
    )
    outside = jnp.where(chosen >= window, other_scores, jnp.float32(0.0))
    scores_all = jnp.where(live_slot, token_scores, outside)
    mean_score = jnp.sum(gating * scores_all, axis=1, keepdims=True)
    grad_logits = gating * (scores_all - mean_score)
    return (grad_hidden, grad_rows.reshape(1, shard_rows, model_width), grad_logits)


def solution(mesh):
    torus = Mesh(
        mesh.devices.reshape(mesh.shape["expert"], 8, 2, 2), ("expert", "dp_0", "dp_1", "dp_2")
    )
    in_specs = (
        P(EXPERT_DP, None),
        P(EXPERT_DP, None),
        P(EXPERT_DP, None),
        P(EXPERT_DP, None),
        P(EXPERT_DP, None),
        P("expert", DP, None, None, None),
        P("expert", DP, None),
    )
    out_specs = (P("expert", DP, None, None, None), P("expert", DP, None), P(EXPERT_DP, None))
    return jax.shard_map(body, mesh=torus, in_specs=in_specs, out_specs=out_specs, check_vma=False)
```

profile of v0, /device:TPU:1, one launch (start us, length us, event | category | flops | bytes accessed | tf_op | source)
XLA Modules:
  0.0 240.8 jit_solution(10185277235059642956)
XLA Ops:
  7.2 8.4 %all_gather.15 = bf16[2,24,2048]{2,1,0:T(8,128)(2,1)} all-gather(bf16[1,24,2048]{2,1,0:T(8,128)(2,1)} %param.13), channel_id=1, replica_groups=mesh['expert'=32,'dp_0'=8,'dp_1'=2,'dp_2'=2] {'dp_1'}, dimensions={0}, use_global_device_ids=true | all-gather | bytes 294912 | tf_op jit(solution)/shard_map/all_gather | solution.py:34
  17.1 0.7 add_select_fusion
  18.5 1.6 convolution_convert_fusion.1
  20.1 2.3 reshape.51
  22.4 1.7 pad_maximum_fusion
  24.1 20.4 %all-to-all-start = ((bf16[32,10,2049]{2,1,0:T(8,128)(2,1)}), bf16[32,10,2049]{2,1,0:T(8,128)(2,1)S(1)}, u32[]{:S(2)}, u32[]{:S(2)}) async-start(bf16[32,10,2049]{2,1,0:T(8,128)(2,1)} %pad_maximum_fusion), calls=%async_computation | async-start | bytes 4456448 | tf_op jit(solution)/shard_map/all_to_all | solution.py:18
  44.5 23.0 %all-gather.5.cloned.1.call-done = bf16[16,24,2048]{2,1,0:T(8,128)(2,1)} async-done(((bf16[2,24,2048]{2,1,0:T(8,128)(2,1)}), bf16[16,24,2048]{2,1,0:T(8,128)(2,1)}) %all-gather.5.cloned.1.call-update) | async-done | bytes 1572880 | tf_op jit(solution)/shard_map/all_gather | solution.py:34
  67.6 1.3 copy.38
  68.9 1.0 reshape.54
  69.8 42.9 %all-to-all-done = bf16[32,10,2049]{2,1,0:T(8,128)(2,1)S(1)} async-done(((bf16[32,10,2049]{2,1,0:T(8,128)(2,1)}), bf16[32,10,2049]{2,1,0:T(8,128)(2,1)S(1)}, u32[]{:S(2)}, u32[]{:S(2)}) %all-to-all-start) | async-done | bytes 1311392 | tf_op jit(solution)/shard_map/all_to_all | solution.py:18
  113.3 1.7 multiply_convert_fusion
  115.0 3.6 %convert_element_type.67 = bf16[320,2048]{1,0:T(8,128)(2,1)} reshape(bf16[32,10,2048]{2,1,0:T(8,128)(2,1)} %multiply_convert_fusion) | data formatting | bytes 2621440 | tf_op jit(solution)/shard_map/convert_element_type | solution.py:84
  118.6 1.6 split.9
  120.2 2.5 %reshape.52 = bf16[320,2048]{1,0:T(8,128)(2,1)S(1)} reshape(bf16[32,10,2048]{2,1,0:T(8,128)(2,1)} %split.9) | data formatting | bytes 2621440 | tf_op jit(solution)/shard_map/reshape | solution.py:81
  122.7 2.3 copy.35
  125.1 2.0 multiply_reduce_fusion
  127.1 0.7 all_to_all.14
  127.8 7.3 %all-to-all-start.2 = ((f32[32,1,10]{2,1,0:T(1,128)}), f32[32,1,10]{2,1,0:T(1,128)S(1)}, u32[]{:S(2)}, u32[]{:S(2)}) async-start(f32[32,1,10]{2,1,0:T(1,128)} %bitcast.10), calls=%async_computation.2 | async-start | bytes 32768 | tf_op jit(solution)/shard_map/all_to_all | solution.py:101
  135.2 4.6 %convolution_convert_fusion = bf16[2048,768]{0,1:T(8,128)(2,1)} fusion(bf16[320,2048]{1,0:T(8,128)(2,1)S(1)} %copy-done.1, bf16[320,768]{1,0:T(8,128)(2,1)} %reshape.54), kind=kOutput, calls=%fused_computation.2 | convolution fusion | flops 1008205824 | bytes 4947968 | tf_op jit(solution)/shard_map/dot_general | solution.py:93
  139.7 6.4 %all-to-all-done.2 = f32[32,1,10]{2,1,0:T(1,128)S(1)} async-done(((f32[32,1,10]{2,1,0:T(1,128)}), f32[32,1,10]{2,1,0:T(1,128)S(1)}, u32[]{:S(2)}, u32[]{:S(2)}) %all-to-all-start.2) | async-done | bytes 1312 | tf_op jit(solution)/shard_map/all_to_all | solution.py:101
  146.1 10.6 %all-to-all-start.1 = ((bf16[32,24,2048]{2,1,0:T(8,128)(2,1)}), bf16[32,24,2048]{2,1,0:T(8,128)(2,1)}, u32[]{:S(2)}, u32[]{:S(2)}) async-start(bf16[32,24,2048]{2,1,0:T(8,128)(2,1)} %bitcast.24), calls=%async_computation.1 | async-start | bytes 6291456 | tf_op jit(solution)/shard_map/all_to_all | solution.py:53
  156.9 0.9 copy.40
  160.3 70.5 %all-to-all-done.1 = bf16[32,24,2048]{2,1,0:T(8,128)(2,1)} async-done(((bf16[32,24,2048]{2,1,0:T(8,128)(2,1)}), bf16[32,24,2048]{2,1,0:T(8,128)(2,1)}, u32[]{:S(2)}, u32[]{:S(2)}) %all-to-all-start.1) | async-done | bytes 3145760 | tf_op jit(solution)/shard_map/all_to_all | solution.py:53
  230.8 3.2 %convert_reduce_fusion = f32[24,2048]{1,0:T(8,128)} fusion(bf16[32,24,2048]{2,1,0:T(8,128)(2,1)} %all-to-all-done.1), kind=kLoop, calls=%fused_computation | loop fusion | flops 3096576 | bytes 3342336 | tf_op jit(solution)/shard_map/reduce_sum | solution.py:54
  (37 shorter events, 5.4 us)
Async XLA Ops:
  7.2 11.4 %copy-start = (bf16[128,2048]{1,0:T(8,128)(2,1)S(1)}, bf16[128,2048]{1,0:T(8,128)(2,1)}, u32[]{:S(2)}) copy-start(bf16[128,2048]{1,0:T(8,128)(2,1)} %param.7) | copy-start | bytes 1572868
  7.2 60.3 %all-gather.5.cloned.1.call-start = ((), (), s32[]{:S(2)}) async-start(), calls=%async_computation.3 | async-start | bytes 1769472 | tf_op jit(solution)/shard_map/all_gather | solution.py:34
  24.1 88.6 %all-to-all-start = ((bf16[32,10,2049]{2,1,0:T(8,128)(2,1)}), bf16[32,10,2049]{2,1,0:T(8,128)(2,1)S(1)}, u32[]{:S(2)}, u32[]{:S(2)}) async-start(bf16[32,10,2049]{2,1,0:T(8,128)(2,1)} %pad_maximum_fusion), calls=%async_computation | async-start | bytes 4456448 | tf_op jit(solution)/shard_map/all_to_all | solution.py:18
  44.5 78.2 %all-gather.7.cloned.1.call-start = ((), (), s32[]{:S(2)}) async-start(), calls=%async_computation.4 | async-start | bytes 4718592 | tf_op jit(solution)/shard_map/all_gather | solution.py:34
  122.7 2.4 copy-start.2
  125.1 10.1 %copy-start.1 = (bf16[320,2048]{1,0:T(8,128)(2,1)S(1)}, bf16[320,2048]{1,0:T(8,128)(2,1)}, u32[]{:S(2)}) copy-start(bf16[320,2048]{1,0:T(8,128)(2,1)} %convert_element_type.67) | copy-start | bytes 3932164
  127.8 18.3 %all-to-all-start.2 = ((f32[32,1,10]{2,1,0:T(1,128)}), f32[32,1,10]{2,1,0:T(1,128)S(1)}, u32[]{:S(2)}, u32[]{:S(2)}) async-start(f32[32,1,10]{2,1,0:T(1,128)} %bitcast.10), calls=%async_computation.2 | async-start | bytes 32768 | tf_op jit(solution)/shard_map/all_to_all | solution.py:101
  146.1 10.6 %copy-start.3 = (bf16[320,768]{1,0:T(8,128)(2,1)S(1)}, bf16[320,768]{1,0:T(8,128)(2,1)}, u32[]{:S(2)}) copy-start(bf16[320,768]{1,0:T(8,128)(2,1)} %get-tuple-element.21) | copy-start | bytes 1474564
  146.1 84.7 %all-to-all-start.1 = ((bf16[32,24,2048]{2,1,0:T(8,128)(2,1)}), bf16[32,24,2048]{2,1,0:T(8,128)(2,1)}, u32[]{:S(2)}, u32[]{:S(2)}) async-start(bf16[32,24,2048]{2,1,0:T(8,128)(2,1)} %bitcast.24), calls=%async_computation.1 | async-start | bytes 6291456 | tf_op jit(solution)/shard_map/all_to_all | solution.py:53
  156.7 2.9 %copy-start.4 = (f32[128,8]{0,1:T(8,128)S(1)}, f32[128,8]{0,1:T(8,128)}, u32[]{:S(2)}) copy-start(f32[128,8]{0,1:T(8,128)} %param.8) | copy-start | bytes 12292
  156.7 2.9 %copy-start.5 = (s32[128,8]{0,1:T(8,128)S(1)}, s32[128,8]{0,1:T(8,128)}, u32[]{:S(2)}) copy-start(s32[128,8]{0,1:T(8,128)} %param.10) | copy-start | bytes 12292
  156.7 2.9 %copy-start.6 = (s32[128,8]{0,1:T(8,128)S(1)}, s32[128,8]{0,1:T(8,128)}, u32[]{:S(2)}) copy-start(s32[128,8]{0,1:T(8,128)} %param.9) | copy-start | bytes 12292
  156.7 2.9 %copy-start.7 = (f32[128,8]{0,1:T(8,128)S(1)}, f32[128,8]{0,1:T(8,128)}, u32[]{:S(2)}) copy-start(f32[128,8]{0,1:T(8,128)} %param.11) | copy-start | bytes 12292
Sparse Core Ops, SparseCore 0:
  15.8 51.7 all-gather.4
  70.2 29.2 all-gather.6
where the time goes:
time: 242 us; the launch traced here: 241 us
  waiting for transfers between devices  143 us (59%)
  starting transfers between devices  38.4 us (16%)
  local copies, waits for them, and re-layouts  17.7 us (7%)
  between operations  14.3 us (6%)
  other arithmetic  10.3 us (4%)
  matrix products  8.94 us (4%)
  blocking collectives  8.41 us (3%)
    all_to_all x1, waiting for transfers between devices, sum_at_owner(): lax.all_to_all(tiles, axis, split_axis=0, concat_axis=0, tiled=True)  70.5 us
    all_to_all x1, waiting for transfers between devices, sent_together(): lax.all_to_all(both, axis, split_axis=split_dim, concat_axis=concat_dim,...  42.9 us
    all_gather x2, waiting for transfers between devices, all_blocks(): tiles = lax.all_gather(tiles, axes[k])  23 us
    all_to_all x1, starting transfers between devices, sent_together(): lax.all_to_all(both, axis, split_axis=split_dim, concat_axis=concat_dim,...  20.4 us
    all_to_all x1, starting transfers between devices, sum_at_owner(): lax.all_to_all(tiles, axis, split_axis=0, concat_axis=0, tiled=True)  10.6 us
    all_gather x1, blocking collectives, all_blocks(): tiles = lax.all_gather(tiles, axes[k])  8.41 us
    all_to_all x1, starting transfers between devices, body(): lax.all_to_all(slot_scores.reshape(window, capacity), 'expert', split_axi...  7.33 us
    all_to_all x1, waiting for transfers between devices, body(): lax.all_to_all(slot_scores.reshape(window, capacity), 'expert', split_axi...  6.4 us
  transfers between devices with their start and end apart: 5, of which 4 were waited for; matrix products, arithmetic and copies ran while one was open for 12% of the time, Pallas kernels for 0%

commit v1 on v0

v1 whole, which is shorter than its diff:
```python
import functools

import jax
import jax.numpy as jnp
from jax import lax
from jax.experimental import pallas as pl
from jax.experimental.pallas import tpu as pltpu
from jax.sharding import Mesh
from jax.sharding import PartitionSpec as P

EXPERT = ("zh", "x")
RING = ("y", "zl")
DP = ("y", "zl", "core")
ALL = EXPERT + DP
CHUNKS = 2
FOLD = 4
F32 = jnp.float32
BF16 = jnp.bfloat16
VMEM = pl.BlockSpec(memory_space=pltpu.VMEM)
SMEM = pl.BlockSpec(memory_space=pltpu.SMEM)
PARAMS = pltpu.CompilerParams(vmem_limit_bytes=48 * 1024 * 1024)


def cost(flops, size):
    return pl.CostEstimate(flops=flops, bytes_accessed=size, transcendentals=0)


def iota(shape, dim):
    return lax.broadcasted_iota(jnp.int32, shape, dim)


def onehot(mask):
    return jnp.where(mask, 1.0, 0.0).astype(BF16)


def dot(a, b, ca=1, cb=0):
    return lax.dot_general(a, b, (((ca,), (cb,)), ((), ())), preferred_element_type=F32)


def softmax_rows(logits):
    raised = jnp.exp(logits)
    return raised / jnp.sum(raised, axis=0, keepdims=True)


def pack_kernel(logits_ref, chosen_ref, slots_ref, rows_ref, *out_refs):
    gate = softmax_rows(logits_ref[...]).astype(BF16).astype(F32)
    chosen, slots = chosen_ref[...], slots_ref[...]
    topk, tokens = chosen.shape
    rows = out_refs[0].shape[0]
    main = jnp.where(slots < 8, chosen * 8 + slots, -1)
    extra = jnp.where((slots >= 8) & (slots < 10), chosen * 2 + slots - 8, -1)
    row = iota((rows, tokens), 0)
    place = jnp.zeros((rows, tokens), F32)
    fold = jnp.zeros((rows, tokens), F32)
    for k in range(topk):
        place = jnp.where(row == main[k : k + 1, :], gate[k : k + 1, :], place)
        fold = jnp.where(row // FOLD == extra[k : k + 1, :], gate[k : k + 1, :], fold)
    place = place.astype(BF16)
    folds = [jnp.where(row % FOLD == m, fold, 0.0).astype(BF16) for m in range(FOLD)]
    width = rows_ref.shape[1] // len(out_refs)
    part = width // FOLD
    for j, out in enumerate(out_refs):
        block = rows_ref[:, j * width : (j + 1) * width]
        out[:, :width] = dot(place, block).astype(BF16)
        total = sum(dot(folds[m], block[:, m * part : (m + 1) * part]) for m in range(FOLD))
        out[:, width:] = total.astype(BF16)


def permuted_units(core, units, shard):
    half = units // 2
    place = iota((1, units), 1)
    other = (place >= half).astype(jnp.int32)
    inner = place - other * half
    side = jnp.where(other == 1, 1 - core, core)
    block = inner // shard
    return block * (2 * shard) + side * shard + (inner - block * shard)


def hidden_kernel(shard, core_ref, hidden_ref, main_ref, extra_ref, main_t_ref, extra_t_ref):
    rows, units = main_ref.shape
    to_unit = permuted_units(core_ref[0], units, shard)
    column = onehot(iota((units, units), 0) == to_unit)
    source = rows // 8
    here = iota((rows, rows), 0)
    there = iota((rows, rows), 1)
    turn = onehot(there == (here % 8) * source + here // 8)
    turned = dot(turn, hidden_ref[:rows, :]).astype(BF16)
    last = hidden_ref[rows:, :]
    main_ref[...] = dot(turned, column).astype(BF16)
    extra_ref[...] = dot(last, column).astype(BF16)
    main_t_ref[...] = dot(column, turned, 0, 1).astype(BF16)
    extra_t_ref[...] = dot(column, last, 0, 1).astype(BF16)


def unfolded(block, m):
    rows = block.shape[0]
    few = rows // FOLD
    source = rows // 8
    here = iota((few, rows), 0)
    there = iota((few, rows), 1)
    pick = onehot(there == (here % source) * 8 + (here // source) * FOLD + m)
    return dot(pick, block).astype(BF16)


def partial_kernel(main_t_ref, extra_t_ref, rows_ref, fold_ref, own_ref, other_ref):
    m = pl.program_id(0)
    half = own_ref.shape[0]
    total = dot(main_t_ref[...], rows_ref[...])
    total = total + dot(extra_t_ref[...], unfolded(fold_ref[...], m))
    own_ref[...] = total[:half, :].astype(BF16)
    other_ref[...] = total[half:, :].astype(BF16)


def partial_sums(main_t, extra_t, payload):
    units = main_t.shape[0]
    rows = payload.shape[0]
    width = payload.shape[1] * FOLD // (FOLD + 1)
    part = width // FOLD
    few = rows // FOLD
    out = jax.ShapeDtypeStruct((units // 2, width), BF16)
    return pl.pallas_call(
        partial_kernel,
        grid=(FOLD,),
        in_specs=[
            pl.BlockSpec((units, rows), lambda m: (0, 0)),
            pl.BlockSpec((units, few), lambda m: (0, 0)),
            pl.BlockSpec((rows, part), lambda m: (0, m)),
            pl.BlockSpec((rows, part), lambda m: (0, FOLD)),
        ],
        out_specs=[pl.BlockSpec((units // 2, part), lambda m: (0, m))] * 2,
        out_shape=[out, out],
        compiler_params=PARAMS,
        cost_estimate=cost(2 * units * (rows + few) * width, 4 * units * width),
        name="partial_sums",
    )(main_t, extra_t, payload, payload)


def product_kernel(shard, core_ref, main_ref, extra_ref, own_ref, other_ref, *refs):
    chunks = (len(refs) - 4) // 2
    payloads, (grad_ref, score_ref, acc_main, acc_extra) = refs[: 2 * chunks], refs[2 * chunks :]
    g = pl.program_id(0)
    rows, units = main_ref.shape
    half = units // 2
    few = rows // FOLD

    @pl.when(g == 0)
    def _():
        acc_main[...] = jnp.zeros_like(acc_main)
        acc_extra[...] = jnp.zeros_like(acc_extra)

    for j in range(chunks):

        @pl.when(g // FOLD == j)
        def _():
            block = payloads[2 * j][...]
            more = unfolded(payloads[2 * j + 1][...], g % FOLD)
            for h, weight in enumerate((own_ref[...], other_ref[...])):
                span = slice(h * half, (h + 1) * half)
                acc_main[:, span] += dot(block, weight, 1, 1)
                acc_extra[:, span] += dot(more, weight, 1, 1)

    @pl.when(g == chunks * FOLD - 1)
    def _():
        main, extra = acc_main[...], acc_extra[...]
        main_score = jnp.sum(main * main_ref[...].astype(F32), axis=1, keepdims=True)
        extra_score = jnp.sum(extra * extra_ref[...].astype(F32), axis=1, keepdims=True)
        source = rows // 8
        lane = iota((rows, 128), 1)
        spread = jnp.where(lane == iota((rows, 128), 0) % 8, main_score, 0.0)
        scores = jnp.sum(spread.reshape(source, 8, 128), axis=1)
        lane = iota((source, 128), 1)
        for c in range(2):
            scores = jnp.where(lane == 8 + c, extra_score[c * source : (c + 1) * source, :], scores)
        score_ref[...] = scores
        to_unit = permuted_units(core_ref[0], units, shard)
        column = onehot(iota((units, units), 0) == to_unit)
        here = iota((rows, rows), 0)
        there = iota((rows, rows), 1)
        turn = onehot(there == (here % source) * 8 + here // source)
        turned = dot(turn, main.astype(BF16)).astype(BF16)
        grad_ref[:rows, :] = dot(turned, column, 1, 1).astype(BF16)
        grad_ref[rows:, :] = dot(extra.astype(BF16), column, 1, 1).astype(BF16)


def products(core, shard, main, extra, own, other, payloads):
    rows, units = main.shape
    few = rows // FOLD
    chunks = len(payloads)
    width = payloads[0].shape[1] * FOLD // (FOLD + 1)
    part = width // FOLD

    def block_of(j):
        return lambda g: (0, jnp.clip(g - FOLD * j, 0, FOLD - 1))

    fixed = lambda g: (0, 0)
    specs = [
        SMEM,
        pl.BlockSpec((rows, units), fixed),
        pl.BlockSpec((few, units), fixed),
        pl.BlockSpec((units // 2, part), lambda g: (0, g)),
        pl.BlockSpec((units // 2, part), lambda g: (0, g)),
    ]
    operands = []
    for j, payload in enumerate(payloads):
        specs.append(pl.BlockSpec((rows, part), block_of(j)))
        specs.append(pl.BlockSpec((rows, part), lambda g: (0, FOLD)))
        operands += [payload, payload]
    return pl.pallas_call(
        functools.partial(product_kernel, shard),
        grid=(chunks * FOLD,),
        in_specs=specs,
        out_specs=[
            pl.BlockSpec((rows + few, units), fixed),
            pl.BlockSpec((rows // 8, 128), fixed),
        ],
        out_shape=[
            jax.ShapeDtypeStruct((rows + few, units), BF16),
            jax.ShapeDtypeStruct((rows // 8, 128), F32),
        ],
        scratch_shapes=[pltpu.VMEM((rows, units), F32), pltpu.VMEM((few, units), F32)],
        compiler_params=PARAMS,
        cost_estimate=cost(2 * units * (rows + few) * width * chunks, 4 * units * width * chunks),
        name="products",
    )(core, main, extra, own, other, *operands)


def logits_kernel(logits_ref, chosen_ref, slots_ref, outside_ref, score_ref, out_ref):
    gating = softmax_rows(logits_ref[...])
    sent = gating.astype(BF16).astype(F32)
    chosen, slots = chosen_ref[...], slots_ref[...]
    topk, tokens = chosen.shape
    experts = score_ref.shape[0]
    returned = score_ref[...]
    found = []
    for k in range(topk):
        hit = jnp.where(iota((experts, tokens), 0) == chosen[k : k + 1, :], 1.0, 0.0)
        by_slot = lax.dot_general(
            returned,
            hit,
            (((0,), (0,)), ((), ())),
            precision=lax.Precision.HIGHEST,
            preferred_element_type=F32,
        )[:16, :]
        at_slot = iota((16, tokens), 0) == slots[k : k + 1, :]
        found.append(jnp.sum(jnp.where(at_slot, by_slot, 0.0), axis=0, keepdims=True))
    inside = jnp.concatenate(found, axis=0) / sent
    outside = jnp.where(chosen >= experts, outside_ref[...], 0.0)
    scores = jnp.where(slots < 10, inside, outside)
    mean = jnp.sum(gating * scores, axis=0, keepdims=True)
    out_ref[...] = gating * (scores - mean)


def body(grad_output, logits, chosen, slots, other_scores, hidden, down_weight):
    tokens, topk = logits.shape
    window, capacity, units = hidden.shape[2], hidden.shape[3], hidden.shape[4]
    model = grad_output.shape[1]
    shard = down_weight.shape[1]
    width = model // CHUNKS
    core = lax.axis_index("core").astype(jnp.int32).reshape(1)
    logits_t, chosen_t, slots_t = logits.T, chosen.T, slots.T

    weights = down_weight.reshape(shard, model)
    own_weights = lax.all_gather(weights, RING).reshape(-1, model)
    other_weights = lax.ppermute(own_weights, "core", [(0, 1), (1, 0)])

    packed = pl.pallas_call(
        pack_kernel,
        in_specs=[VMEM] * 4,
        out_specs=[VMEM] * CHUNKS,
        out_shape=[jax.ShapeDtypeStruct((window * 8, width + width // FOLD), BF16)] * CHUNKS,
        compiler_params=PARAMS,
        cost_estimate=cost(2 * 320 * tokens * model * 2, 4 * 320 * model),
        name="pack",
    )(logits_t, chosen_t, slots_t, grad_output)
    payloads = []
    for part in packed:
        part = part.reshape(window, 8, part.shape[1])
        part = lax.all_to_all(part, EXPERT, split_axis=0, concat_axis=0, tiled=True)
        payloads.append(part.reshape(window * 8, part.shape[2]))

    by_slot = hidden.transpose(0, 1, 3, 2, 4).reshape(capacity * window, units)
    main, extra, main_t, extra_t = pl.pallas_call(
        functools.partial(hidden_kernel, shard),
        in_specs=[SMEM, VMEM],
        out_specs=[VMEM] * 4,
        out_shape=[
            jax.ShapeDtypeStruct((window * 8, units), BF16),
            jax.ShapeDtypeStruct((window * 2, units), BF16),
            jax.ShapeDtypeStruct((units, window * 8), BF16),
            jax.ShapeDtypeStruct((units, window * 2), BF16),
        ],
        compiler_params=PARAMS,
        cost_estimate=cost(4 * 320 * units * units, 8 * 320 * units),
        name="hidden_order",
    )(core, by_slot)

    sums = []
    for payload in payloads:
        own, other = partial_sums(main_t, extra_t, payload)
        arrived = lax.ppermute(other, "core", [(0, 1), (1, 0)])
        both = (own.astype(F32) + arrived.astype(F32)).astype(BF16)
        pieces = both.reshape(-1, shard, width)
        pieces = lax.all_to_all(pieces, RING, split_axis=0, concat_axis=0, tiled=True)
        sums.append(jnp.sum(pieces.astype(F32), axis=0))
    grad_down = jnp.concatenate(sums, axis=1).reshape(1, shard, model)

    grad, score = products(core, shard, main, extra, own_weights, other_weights, payloads)
    grad_hidden = grad.reshape(1, 1, capacity, window, units).transpose(0, 1, 3, 2, 4)
    returned = lax.all_to_all(
        score.reshape(window, 1, 128), EXPERT, split_axis=0, concat_axis=0, tiled=True
    ).reshape(window, 128)
    grad_logits = pl.pallas_call(
        logits_kernel,
        in_specs=[VMEM] * 5,
        out_specs=VMEM,
        out_shape=jax.ShapeDtypeStruct((topk, tokens), F32),
        compiler_params=PARAMS,
        name="logits",
    )(logits_t, chosen_t, slots_t, other_scores.T, returned)
    return grad_hidden, grad_down, grad_logits.T


def solution(mesh):
    torus = Mesh(mesh.devices.reshape(4, 8, 8, 2, 2), ALL)
    in_specs = (
        P(ALL, None),
        P(ALL, None),
        P(ALL, None),
        P(ALL, None),
        P(ALL, None),
        P(EXPERT, DP, None, None, None),
        P(EXPERT, DP, None),
    )
    out_specs = (P(EXPERT, DP, None, None, None), P(EXPERT, DP, None), P(ALL, None))
    return jax.shard_map(body, mesh=torus, in_specs=in_specs, out_specs=out_specs, check_vma=False)
```

time: 242 us -> 190 us (0.79)
  the two profiles are of different devices: /device:TPU:1 before, /device:TPU:16 now
where the time goes in v1:
time: 190 us; the launch traced here: 189 us
  waiting for transfers between devices  80.4 us (42%)
  starting transfers between devices  67.3 us (35%)
  Pallas kernels  17.2 us (9%)
  between operations  14.2 us (7%)
  other arithmetic  7.14 us (4%)
  local copies, waits for them, and re-layouts  3.12 us (2%)
    all_to_all x2, waiting for transfers between devices, body(): part = lax.all_to_all(part, EXPERT, split_axis=0, concat_axis=0, tiled=True)  35 us
    all_to_all x2, starting transfers between devices, body(): part = lax.all_to_all(part, EXPERT, split_axis=0, concat_axis=0, tiled=True)  27.2 us
    all_to_all x1, starting transfers between devices, body(): lax.all_to_all(score.reshape(window, 1, 128), EXPERT, split_axis=0, conca...  18.7 us
    all_gather x1, waiting for transfers between devices, body(): own_weights = lax.all_gather(weights, RING).reshape(-1, model)  17 us
    all_to_all x2, starting transfers between devices, body(): lax.all_to_all(pieces, RING, split_axis=0, concat_axis=0, tiled=True)  15.5 us
    all_to_all x2, waiting for transfers between devices, body(): lax.all_to_all(pieces, RING, split_axis=0, concat_axis=0, tiled=True)  12 us
    all_to_all x1, waiting for transfers between devices, body(): lax.all_to_all(score.reshape(window, 1, 128), EXPERT, split_axis=0, conca...  10.6 us
    pallas_call x1, Pallas kernels, products(): pl.pallas_call(functools.partial(product_kernel, shard), grid=(chunks * F...  8.13 us
  transfers between devices with their start and end apart: 9, of which 8 were waited for; matrix products, arithmetic and copies ran while one was open for 4% of the time, Pallas kernels for 3%

profile of v1, /device:TPU:16, one launch (start us, length us, event | category | flops | bytes accessed | tf_op | source)
XLA Modules:
  0.0 189.4 jit_solution(17585203017551878402)
XLA Ops:
  10.3 1.7 pack.1
  11.9 21.2 %all-to-all-start = ((bf16[32,8,1280]{2,1,0:T(8,128)(2,1)}), bf16[32,8,1280]{2,1,0:T(8,128)(2,1)S(1)}, u32[]{:S(2)}, u32[]{:S(2)}) async-start(bf16[32,8,1280]{2,1,0:T(8,128)(2,1)} %bitcast.7), calls=%async_computation | async-start | bytes 1310720 | tf_op jit(solution)/shard_map/all_to_all | solution.py:278
  33.9 20.9 %all-to-all-done = bf16[32,8,1280]{2,1,0:T(8,128)(2,1)S(1)} async-done(((bf16[32,8,1280]{2,1,0:T(8,128)(2,1)}), bf16[32,8,1280]{2,1,0:T(8,128)(2,1)S(1)}, u32[]{:S(2)}, u32[]{:S(2)}) %all-to-all-start) | async-done | bytes 655392 | tf_op jit(solution)/shard_map/all_to_all | solution.py:278
  54.8 6.0 %all-to-all-start.1 = ((bf16[32,8,1280]{2,1,0:T(8,128)(2,1)}), bf16[32,8,1280]{2,1,0:T(8,128)(2,1)S(1)}, u32[]{:S(2)}, u32[]{:S(2)}) async-start(bf16[32,8,1280]{2,1,0:T(8,128)(2,1)} %bitcast.9), calls=%async_computation.1 | async-start | bytes 1310720 | tf_op jit(solution)/shard_map/all_to_all | solution.py:278
  60.9 1.5 hidden_order.1
  62.4 2.4 %partial_sums.2 = (bf16[384,1024]{1,0:T(8,128)(2,1)S(1)}, bf16[384,1024]{1,0:T(8,128)(2,1)S(1)}) custom-call(bf16[768,256]{1,0:T(8,128)(2,1)S(1)} %get-tuple-element.20.main_t_ref, bf16[768,64]{1,0:T(8,128)(2,1)S(1)} %get-tuple-element.21.extra_t_ref, bf16[256,1280]{1,0:T(8,128)(2,1)S(1)} %bitcast.25, bf16[256,1280]{1,0:T(8,128)(2,1)S(1)} %bitcast.26), custom_call_target="tpu_custom_call" | custom-call | flops 503316480 | bytes 3145728 | tf_op jit(solution)/shard_map/partial_sums/pallas_call | solution.py:121
  64.7 1.9 %collective-permute-start.1 = (bf16[384,1024]{1,0:T(8,128)(2,1)S(1)}, bf16[384,1024]{1,0:T(8,128)(2,1)S(1)}, u32[]{:S(2)}, u32[]{:S(2)}) collective-permute-start(bf16[384,1024]{1,0:T(8,128)(2,1)S(1)} %get-tuple-element.23), channel_id=1, source_target_pairs={{0,1},{1,0},{2,3},{3,2},{4,5},{5,4},{6,7},{7,6},{8,9},{9,8},{10,11... | collective-permute-start | bytes 2359304 | tf_op jit(solution)/shard_map/ppermute | solution.py:300
  66.6 2.3 %collective-permute-done.1 = bf16[384,1024]{1,0:T(8,128)(2,1)S(1)} collective-permute-done((bf16[384,1024]{1,0:T(8,128)(2,1)S(1)}, bf16[384,1024]{1,0:T(8,128)(2,1)S(1)}, u32[]{:S(2)}, u32[]{:S(2)}) %collective-permute-start.1) | collective-permute-done | bytes 786464 | tf_op jit(solution)/shard_map/ppermute | solution.py:300
  70.1 14.1 %all-to-all-done.1 = bf16[32,8,1280]{2,1,0:T(8,128)(2,1)S(1)} async-done(((bf16[32,8,1280]{2,1,0:T(8,128)(2,1)}), bf16[32,8,1280]{2,1,0:T(8,128)(2,1)S(1)}, u32[]{:S(2)}, u32[]{:S(2)}) %all-to-all-start.1) | async-done | bytes 655392 | tf_op jit(solution)/shard_map/all_to_all | solution.py:278
  84.2 8.2 %all-to-all-start.2 = ((bf16[16,24,1024]{2,1,0:T(8,128)(2,1)}), bf16[16,24,1024]{2,1,0:T(8,128)(2,1)}, u32[]{:S(2)}, u32[]{:S(2)}) async-start(bf16[16,24,1024]{2,1,0:T(8,128)(2,1)} %bitcast.13), calls=%async_computation.2 | async-start | bytes 1572864 | tf_op jit(solution)/shard_map/all_to_all | solution.py:303
  92.5 2.3 %partial_sums.3 = (bf16[384,1024]{1,0:T(8,128)(2,1)S(1)}, bf16[384,1024]{1,0:T(8,128)(2,1)S(1)}) custom-call(bf16[768,256]{1,0:T(8,128)(2,1)S(1)} %get-tuple-element.20.main_t_ref, bf16[768,64]{1,0:T(8,128)(2,1)S(1)} %get-tuple-element.21.extra_t_ref, bf16[256,1280]{1,0:T(8,128)(2,1)S(1)} %bitcast.29, bf16[256,1280]{1,0:T(8,128)(2,1)S(1)} %bitcast.30), custom_call_target="tpu_custom_call" | custom-call | flops 503316480 | bytes 3145728 | tf_op jit(solution)/shard_map/partial_sums/pallas_call | solution.py:121
  94.8 1.9 %collective-permute-start.2 = (bf16[384,1024]{1,0:T(8,128)(2,1)S(1)}, bf16[384,1024]{1,0:T(8,128)(2,1)S(1)}, u32[]{:S(2)}, u32[]{:S(2)}) collective-permute-start(bf16[384,1024]{1,0:T(8,128)(2,1)S(1)} %get-tuple-element.25), channel_id=1, source_target_pairs={{0,1},{1,0},{2,3},{3,2},{4,5},{5,4},{6,7},{7,6},{8,9},{9,8},{10,11... | collective-permute-start | bytes 2359304 | tf_op jit(solution)/shard_map/ppermute | solution.py:300
  96.7 2.3 %collective-permute-done.2 = bf16[384,1024]{1,0:T(8,128)(2,1)S(1)} collective-permute-done((bf16[384,1024]{1,0:T(8,128)(2,1)S(1)}, bf16[384,1024]{1,0:T(8,128)(2,1)S(1)}, u32[]{:S(2)}, u32[]{:S(2)}) %collective-permute-start.2) | collective-permute-done | bytes 786464 | tf_op jit(solution)/shard_map/ppermute | solution.py:300
  100.2 12.0 %all-to-all-done.2 = bf16[16,24,1024]{2,1,0:T(8,128)(2,1)} async-done(((bf16[16,24,1024]{2,1,0:T(8,128)(2,1)}), bf16[16,24,1024]{2,1,0:T(8,128)(2,1)}, u32[]{:S(2)}, u32[]{:S(2)}) %all-to-all-start.2) | async-done | bytes 786464 | tf_op jit(solution)/shard_map/all_to_all | solution.py:303
  112.2 7.3 %all-to-all-start.3 = ((bf16[16,24,1024]{2,1,0:T(8,128)(2,1)}), bf16[16,24,1024]{2,1,0:T(8,128)(2,1)}, u32[]{:S(2)}, u32[]{:S(2)}) async-start(bf16[16,24,1024]{2,1,0:T(8,128)(2,1)} %bitcast.14), calls=%async_computation.3 | async-start | bytes 1572864 | tf_op jit(solution)/shard_map/all_to_all | solution.py:303
  119.5 17.0 %all-gather.2.cloned.1.call-done = bf16[16,24,2048]{2,1,0:T(8,128)(2,1)} async-done(((bf16[1,24,2048]{2,1,0:T(8,128)(2,1)}), bf16[16,24,2048]{2,1,0:T(8,128)(2,1)}) %all-gather.2.cloned.1.call-update) | async-done | bytes 1572880 | tf_op jit(solution)/shard_map/all_gather | solution.py:263
  136.5 2.0 %collective-permute-start = (bf16[384,2048]{1,0:T(8,128)(2,1)}, bf16[384,2048]{1,0:T(8,128)(2,1)}, u32[]{:S(2)}, u32[]{:S(2)}) collective-permute-start(bf16[384,2048]{1,0:T(8,128)(2,1)} %bitcast.33), channel_id=1, source_target_pairs={{0,1},{1,0},{2,3},{3,2},{4,5},{5,4},{6,7},{7,6},{8,9},{9,8},{10,11... | collective-permute-start | bytes 4718600 | tf_op jit(solution)/shard_map/ppermute | solution.py:264
  138.5 1.3 convert_reduce_fusion.1
  139.8 1.9 %convert_reduce_fusion = f32[24,1024]{1,0:T(8,128)} fusion(bf16[16,24,1024]{2,1,0:T(8,128)(2,1)} %all-to-all-done.3), kind=kLoop, calls=%fused_computation | loop fusion | flops 761856 | bytes 884736 | tf_op jit(solution)/shard_map/reduce_sum | solution.py:304
  142.3 8.1 %products.1 = (bf16[320,768]{1,0:T(8,128)(2,1)}, f32[32,128]{1,0:T(8,128)}) custom-call(s32[1]{0:T(128)} %bitcast.core_ref, bf16[256,768]{1,0:T(8,128)(2,1)S(1)} %get-tuple-element.15.main_ref, bf16[64,768]{1,0:T(8,128)(2,1)S(1)} %get-tuple-element.16.extra_ref, bf16[384,2048]{1,0:T(8,128)(2,1)S(1)} %bitcast.34, ...), custom_call_target="tpu_custom_call" | custom-call | flops 1006632960 | bytes 6291456 | tf_op jit(solution)/shard_map/products/pallas_call | solution.py:208
  150.4 18.7 %all-to-all-start.4 = ((f32[32,1,128]{2,1,0:T(1,128)}), f32[32,1,128]{2,1,0:T(1,128)S(1)}, u32[]{:S(2)}, u32[]{:S(2)}) async-start(f32[32,1,128]{2,1,0:T(1,128)} %bitcast.18), calls=%async_computation.4 | async-start | bytes 32768 | tf_op jit(solution)/shard_map/all_to_all | solution.py:309
  169.1 1.6 maximum_bitcast_fusion
  170.7 10.6 %all-to-all-done.4 = f32[32,1,128]{2,1,0:T(1,128)S(1)} async-done(((f32[32,1,128]{2,1,0:T(1,128)}), f32[32,1,128]{2,1,0:T(1,128)S(1)}, u32[]{:S(2)}, u32[]{:S(2)}) %all-to-all-start.4) | async-done | bytes 16416 | tf_op jit(solution)/shard_map/all_to_all | solution.py:309
  181.3 1.2 logits.1
  (26 shorter events, 6.8 us)
Async XLA Ops:
  7.2 0.7 copy-start.1
  7.9 0.7 copy-start.3
  8.5 0.7 copy-start.5
  9.2 1.0 copy-start.8
  11.9 48.9 %copy-start.9 = (bf16[1,1,32,10,768]{4,2,3,1,0:T(8,128)(2,1)S(1)}, bf16[1,1,32,10,768]{4,2,3,1,0:T(8,128)(2,1)}, u32[]{:S(2)}) copy-start(bf16[1,1,32,10,768]{4,2,3,1,0:T(8,128)(2,1)} %param.12) | copy-start | bytes 1474564
  11.9 42.9 %all-to-all-start = ((bf16[32,8,1280]{2,1,0:T(8,128)(2,1)}), bf16[32,8,1280]{2,1,0:T(8,128)(2,1)S(1)}, u32[]{:S(2)}, u32[]{:S(2)}) async-start(bf16[32,8,1280]{2,1,0:T(8,128)(2,1)} %bitcast.7), calls=%async_computation | async-start | bytes 1310720 | tf_op jit(solution)/shard_map/all_to_all | solution.py:278
  33.1 103.4 %all-gather.2.cloned.1.call-start = ((), (), s32[]{:S(2)}) async-start(), calls=%async_computation.5 | async-start | bytes 1671168 | tf_op jit(solution)/shard_map/all_gather | solution.py:263
  54.8 29.4 %all-to-all-start.1 = ((bf16[32,8,1280]{2,1,0:T(8,128)(2,1)}), bf16[32,8,1280]{2,1,0:T(8,128)(2,1)S(1)}, u32[]{:S(2)}, u32[]{:S(2)}) async-start(bf16[32,8,1280]{2,1,0:T(8,128)(2,1)} %bitcast.9), calls=%async_computation.1 | async-start | bytes 1310720 | tf_op jit(solution)/shard_map/all_to_all | solution.py:278
  64.7 4.2 %collective-permute-start.1 = (bf16[384,1024]{1,0:T(8,128)(2,1)S(1)}, bf16[384,1024]{1,0:T(8,128)(2,1)S(1)}, u32[]{:S(2)}, u32[]{:S(2)}) collective-permute-start(bf16[384,1024]{1,0:T(8,128)(2,1)S(1)} %get-tuple-element.23), channel_id=1, source_target_pairs={{0,1},{1,0},{2,3},{3,2},{4,5},{5,4},{6,7},{7,6},{8,9},{9,8},{10,11... | collective-permute-start | bytes 2359304 | tf_op jit(solution)/shard_map/ppermute | solution.py:300
  84.2 28.0 %all-to-all-start.2 = ((bf16[16,24,1024]{2,1,0:T(8,128)(2,1)}), bf16[16,24,1024]{2,1,0:T(8,128)(2,1)}, u32[]{:S(2)}, u32[]{:S(2)}) async-start(bf16[16,24,1024]{2,1,0:T(8,128)(2,1)} %bitcast.13), calls=%async_computation.2 | async-start | bytes 1572864 | tf_op jit(solution)/shard_map/all_to_all | solution.py:303
  94.8 4.2 %collective-permute-start.2 = (bf16[384,1024]{1,0:T(8,128)(2,1)S(1)}, bf16[384,1024]{1,0:T(8,128)(2,1)S(1)}, u32[]{:S(2)}, u32[]{:S(2)}) collective-permute-start(bf16[384,1024]{1,0:T(8,128)(2,1)S(1)} %get-tuple-element.25), channel_id=1, source_target_pairs={{0,1},{1,0},{2,3},{3,2},{4,5},{5,4},{6,7},{7,6},{8,9},{9,8},{10,11... | collective-permute-start | bytes 2359304 | tf_op jit(solution)/shard_map/ppermute | solution.py:300
  112.2 27.6 %all-to-all-start.3 = ((bf16[16,24,1024]{2,1,0:T(8,128)(2,1)}), bf16[16,24,1024]{2,1,0:T(8,128)(2,1)}, u32[]{:S(2)}, u32[]{:S(2)}) async-start(bf16[16,24,1024]{2,1,0:T(8,128)(2,1)} %bitcast.14), calls=%async_computation.3 | async-start | bytes 1572864 | tf_op jit(solution)/shard_map/all_to_all | solution.py:303
  136.5 5.8 %copy-start = (bf16[16,24,2048]{2,1,0:T(8,128)(2,1)S(1)}, bf16[16,24,2048]{2,1,0:T(8,128)(2,1)}, u32[]{:S(2)}) copy-start(bf16[16,24,2048]{2,1,0:T(8,128)(2,1)} %all-gather.2.cloned.1.call-done) | copy-start | bytes 4718596
  136.5 5.8 %collective-permute-start = (bf16[384,2048]{1,0:T(8,128)(2,1)}, bf16[384,2048]{1,0:T(8,128)(2,1)}, u32[]{:S(2)}, u32[]{:S(2)}) collective-permute-start(bf16[384,2048]{1,0:T(8,128)(2,1)} %bitcast.33), channel_id=1, source_target_pairs={{0,1},{1,0},{2,3},{3,2},{4,5},{5,4},{6,7},{7,6},{8,9},{9,8},{10,11... | collective-permute-start | bytes 4718600 | tf_op jit(solution)/shard_map/ppermute | solution.py:264
  142.3 39.0 %copy-start.2 = (f32[128,8]{0,1:T(8,128)S(1)}, f32[128,8]{0,1:T(8,128)}, u32[]{:S(2)}) copy-start(f32[128,8]{0,1:T(8,128)} %param.8) | copy-start | bytes 12292
  142.3 39.0 %copy-start.4 = (s32[128,8]{0,1:T(8,128)S(1)}, s32[128,8]{0,1:T(8,128)}, u32[]{:S(2)}) copy-start(s32[128,8]{0,1:T(8,128)} %param.9) | copy-start | bytes 12292
  142.3 39.0 %copy-start.6 = (s32[128,8]{0,1:T(8,128)S(1)}, s32[128,8]{0,1:T(8,128)}, u32[]{:S(2)}) copy-start(s32[128,8]{0,1:T(8,128)} %param.10) | copy-start | bytes 12292
  142.3 39.0 %copy-start.7 = (f32[128,8]{0,1:T(8,128)S(1)}, f32[128,8]{0,1:T(8,128)}, u32[]{:S(2)}) copy-start(f32[128,8]{0,1:T(8,128)} %param.11) | copy-start | bytes 12292
  150.4 30.9 %all-to-all-start.4 = ((f32[32,1,128]{2,1,0:T(1,128)}), f32[32,1,128]{2,1,0:T(1,128)S(1)}, u32[]{:S(2)}, u32[]{:S(2)}) async-start(f32[32,1,128]{2,1,0:T(1,128)} %bitcast.18), calls=%async_computation.4 | async-start | bytes 32768 | tf_op jit(solution)/shard_map/all_to_all | solution.py:309
Sparse Core Ops, SparseCore 0:
  36.6 99.8 all-gather.1

commit v2 on v1

v2 whole, which is shorter than its diff:
```python
import functools

import jax
import jax.numpy as jnp
from jax import lax
from jax.experimental import pallas as pl
from jax.experimental.pallas import tpu as pltpu
from jax.sharding import Mesh
from jax.sharding import PartitionSpec as P

EXPERT = ("zh", "x")
RING = ("y", "zl")
DP = ("y", "zl", "core")
ALL = EXPERT + DP
FOLD = 4
F32 = jnp.float32
BF16 = jnp.bfloat16
VMEM = pl.BlockSpec(memory_space=pltpu.VMEM)
HBM = pl.BlockSpec(memory_space=pltpu.HBM)
SMEM = pl.BlockSpec(memory_space=pltpu.SMEM)
PARAMS = pltpu.CompilerParams(vmem_limit_bytes=48 * 1024 * 1024)


def cost(flops, size):
    return pl.CostEstimate(flops=flops, bytes_accessed=size, transcendentals=0)


def iota(shape, dim):
    return lax.broadcasted_iota(jnp.int32, shape, dim)


def onehot(mask):
    return jnp.where(mask, 1.0, 0.0).astype(BF16)


def dot(a, b, ca=1, cb=0):
    return lax.dot_general(a, b, (((ca,), (cb,)), ((), ())), preferred_element_type=F32)


def softmax_rows(logits):
    raised = jnp.exp(logits)
    return raised / jnp.sum(raised, axis=0, keepdims=True)


def pack_kernel(logits_in, chosen_in, slots_in, rows_in, first_in, out_ref, *scratch):
    held, sems = scratch[:4], scratch[4]
    copies = [
        pltpu.make_async_copy(src, dst, sems.at[k])
        for k, (src, dst) in enumerate(zip((logits_in, chosen_in, slots_in, rows_in), held))
    ]
    for copy in copies:
        copy.start()
    for copy in copies:
        copy.wait()
    logits_ref, chosen_ref, slots_ref, rows_ref = held
    gate = softmax_rows(logits_ref[...]).astype(BF16).astype(F32)
    chosen, slots = chosen_ref[...], slots_ref[...]
    topk, tokens = chosen.shape
    rows = out_ref.shape[0]
    main = jnp.where(slots < 8, chosen * 8 + slots, -1)
    extra = jnp.where((slots >= 8) & (slots < 10), chosen * 2 + slots - 8, -1)
    row = iota((rows, tokens), 0)
    place = jnp.zeros((rows, tokens), F32)
    fold = jnp.zeros((rows, tokens), F32)
    for k in range(topk):
        place = jnp.where(row == main[k : k + 1, :], gate[k : k + 1, :], place)
        fold = jnp.where(row // FOLD == extra[k : k + 1, :], gate[k : k + 1, :], fold)
    place = place.astype(BF16)
    width = rows_ref.shape[1]
    part = width // FOLD
    total = jnp.zeros((rows, part), F32)
    for m in range(FOLD):
        block = rows_ref[:, m * part : (m + 1) * part]
        out_ref[:, m * part : (m + 1) * part] = dot(place, block).astype(BF16)
        total = total + dot(jnp.where(row % FOLD == m, fold, 0.0).astype(BF16), block)
    out_ref[:, width:] = total.astype(BF16)


def permuted_units(core, units, shard):
    half = units // 2
    place = iota((1, units), 1)
    other = (place >= half).astype(jnp.int32)
    inner = place - other * half
    side = jnp.where(other == 1, 1 - core, core)
    block = inner // shard
    return block * (2 * shard) + side * shard + (inner - block * shard)


def hidden_kernel(shard, core_ref, hidden_ref, main_ref, extra_ref, main_t_ref, extra_t_ref):
    rows, units = main_ref.shape
    to_unit = permuted_units(core_ref[0], units, shard)
    column = onehot(iota((units, units), 0) == to_unit)
    source = rows // 8
    here = iota((rows, rows), 0)
    there = iota((rows, rows), 1)
    turn = onehot(there == (here % 8) * source + here // 8)
    turned = dot(turn, hidden_ref[:rows, :]).astype(BF16)
    last = hidden_ref[rows:, :]
    main_ref[...] = dot(turned, column).astype(BF16)
    extra_ref[...] = dot(last, column).astype(BF16)
    main_t_ref[...] = dot(column, turned, 0, 1).astype(BF16)
    extra_t_ref[...] = dot(column, last, 0, 1).astype(BF16)


def unfolded(block, m):
    rows = block.shape[0]
    few = rows // FOLD
    source = rows // 8
    here = iota((few, rows), 0)
    there = iota((few, rows), 1)
    pick = onehot(there == (here % source) * 8 + (here // source) * FOLD + m)
    return dot(pick, block).astype(BF16)


def half_product(main_t_ref, extra_t_ref, rows_ref, fold_ref):
    total = dot(main_t_ref[...], rows_ref[...])
    return total + dot(extra_t_ref[...], unfolded(fold_ref[...], pl.program_id(0)))


def send_kernel(main_t_ref, extra_t_ref, rows_ref, fold_ref, out_ref):
    out_ref[...] = half_product(main_t_ref, extra_t_ref, rows_ref, fold_ref).astype(BF16)


def keep_kernel(main_t_ref, extra_t_ref, rows_ref, fold_ref, arrived_ref, out_ref):
    total = half_product(main_t_ref, extra_t_ref, rows_ref, fold_ref)
    out_ref[...] = (total + arrived_ref[...].astype(F32)).astype(BF16)


def half_partial(main_t, extra_t, payload, half, arrived=None):
    units, rows = main_t.shape
    few = extra_t.shape[1]
    width = payload.shape[1] * FOLD // (FOLD + 1)
    part = width // FOLD
    in_specs = [
        pl.BlockSpec((units // 2, rows), lambda m: (half, 0)),
        pl.BlockSpec((units // 2, few), lambda m: (half, 0)),
        pl.BlockSpec((rows, part), lambda m: (0, m)),
        pl.BlockSpec((rows, part), lambda m: (0, FOLD)),
    ]
    operands = [main_t, extra_t, payload, payload]
    tile = pl.BlockSpec((units // 2, part), lambda m: (0, m))
    if arrived is not None:
        in_specs.append(tile)
        operands.append(arrived)
    return pl.pallas_call(
        send_kernel if arrived is None else keep_kernel,
        grid=(FOLD,),
        in_specs=in_specs,
        out_specs=tile,
        out_shape=pltpu.HBM((units // 2, width), BF16),
        compiler_params=PARAMS,
        cost_estimate=cost(units * (rows + few) * width, 3 * units * width),
        name="half_sent" if arrived is None else "half_kept",
    )(*operands)


def product_kernel(
    shard,
    core_ref,
    main_ref,
    extra_ref,
    own_ref,
    other_ref,
    rows_ref,
    fold_ref,
    grad_ref,
    score_ref,
    acc_main,
    acc_extra,
):
    g = pl.program_id(0)
    rows, units = main_ref.shape
    half = units // 2

    @pl.when(g == 0)
    def _():
        acc_main[...] = jnp.zeros_like(acc_main)
        acc_extra[...] = jnp.zeros_like(acc_extra)

    block = rows_ref[...]
    more = unfolded(fold_ref[...], g)
    for h, weight in enumerate((own_ref[...], other_ref[...])):
        span = slice(h * half, (h + 1) * half)
        acc_main[:, span] += dot(block, weight, 1, 1)
        acc_extra[:, span] += dot(more, weight, 1, 1)

    @pl.when(g == FOLD - 1)
    def _():
        main, extra = acc_main[...], acc_extra[...]
        main_score = jnp.sum(main * main_ref[...].astype(F32), axis=1, keepdims=True)
        extra_score = jnp.sum(extra * extra_ref[...].astype(F32), axis=1, keepdims=True)
        source = rows // 8
        lane = iota((rows, 128), 1)
        spread = jnp.where(lane == iota((rows, 128), 0) % 8, main_score, 0.0)
        scores = jnp.sum(spread.reshape(source, 8, 128), axis=1)
        lane = iota((source, 128), 1)
        for c in range(2):
            scores = jnp.where(lane == 8 + c, extra_score[c * source : (c + 1) * source, :], scores)
        pick = (iota((source, source), 0) ^ core_ref[1]) == iota((source, source), 1)
        score_ref[...] = exact_dot(jnp.where(pick, 1.0, 0.0), scores)
        to_unit = permuted_units(core_ref[0], units, shard)
        column = onehot(iota((units, units), 0) == to_unit)
        here = iota((rows, rows), 0)
        there = iota((rows, rows), 1)
        turn = onehot(there == (here % source) * 8 + here // source)
        turned = dot(turn, main.astype(BF16)).astype(BF16)
        grad_ref[:rows, :] = dot(turned, column, 1, 1).astype(BF16)
        grad_ref[rows:, :] = dot(extra.astype(BF16), column, 1, 1).astype(BF16)


def exact_dot(a, b, ca=1, cb=0):
    return lax.dot_general(
        a,
        b,
        (((ca,), (cb,)), ((), ())),
        precision=lax.Precision.HIGHEST,
        preferred_element_type=F32,
    )


def products(place, shard, main, extra, own, other, payload):
    rows, units = main.shape
    few = rows // FOLD
    width = payload.shape[1] * FOLD // (FOLD + 1)
    part = width // FOLD
    fixed = lambda g: (0, 0)
    moving = lambda g: (0, g)
    return pl.pallas_call(
        functools.partial(product_kernel, shard),
        grid=(FOLD,),
        in_specs=[
            SMEM,
            pl.BlockSpec((rows, units), fixed),
            pl.BlockSpec((few, units), fixed),
            pl.BlockSpec((units // 2, part), moving),
            pl.BlockSpec((units // 2, part), moving),
            pl.BlockSpec((rows, part), moving),
            pl.BlockSpec((rows, part), lambda g: (0, FOLD)),
        ],
        out_specs=[
            pl.BlockSpec((rows + few, units), fixed),
            pl.BlockSpec((rows // 8, 128), fixed),
        ],
        out_shape=[
            jax.ShapeDtypeStruct((rows + few, units), BF16),
            jax.ShapeDtypeStruct((rows // 8, 128), F32),
        ],
        scratch_shapes=[pltpu.VMEM((rows, units), F32), pltpu.VMEM((few, units), F32)],
        compiler_params=PARAMS,
        cost_estimate=cost(0, 0),
        name="products",
    )(place, main, extra, own, other, payload, payload)


def exchanged_by_bits(blocks):
    count, lanes = blocks.shape
    inner = lax.axis_size("x")
    bit = 1
    while bit < count:
        axis, step = ("x", bit) if bit < inner else ("zh", bit // inner)
        size = lax.axis_size(axis)
        pairs = blocks.reshape(count // (2 * bit), 2, bit, lanes)
        came = lax.ppermute(pairs[:, 1], axis, [(i, i ^ step) for i in range(size)])
        blocks = jnp.stack([pairs[:, 0], came], axis=1).reshape(count, lanes)
        bit *= 2
    return blocks


def in_hbm(array):
    return pltpu.with_memory_space_constraint(array, pltpu.HBM)


def after(array, first):
    return pl.pallas_call(
        lambda a, b, c: None,
        in_specs=[HBM, HBM],
        out_specs=HBM,
        out_shape=pltpu.HBM(array.shape, array.dtype),
        input_output_aliases={0: 0},
        cost_estimate=cost(0, 0),
        name="after",
    )(array, first)


def sum_kernel(pieces_ref, out_ref):
    total = pieces_ref[0].astype(F32)
    for k in range(1, pieces_ref.shape[0]):
        total = total + pieces_ref[k].astype(F32)
    out_ref[...] = total


def summed(pieces):
    count, shard, width = pieces.shape
    part = width // 4
    return pl.pallas_call(
        sum_kernel,
        grid=(4,),
        in_specs=[pl.BlockSpec((count, shard, part), lambda g: (0, 0, g))],
        out_specs=pl.BlockSpec((shard, part), lambda g: (0, g)),
        out_shape=jax.ShapeDtypeStruct((shard, width), F32),
        compiler_params=PARAMS,
        cost_estimate=cost(count * shard * width, 2 * count * shard * width),
        name="summed",
    )(pieces)


def logits_kernel(place_ref, logits_ref, chosen_ref, slots_ref, outside_ref, score_ref, out_ref):
    gating = softmax_rows(logits_ref[...])
    sent = gating.astype(BF16).astype(F32)
    chosen, slots = chosen_ref[...], slots_ref[...]
    topk, tokens = chosen.shape
    experts = score_ref.shape[0]
    returned = score_ref[...]
    found = []
    here = chosen ^ place_ref[1]
    for k in range(topk):
        hit = jnp.where(iota((experts, tokens), 0) == here[k : k + 1, :], 1.0, 0.0)
        by_slot = exact_dot(returned, hit, 0, 0)[:16, :]
        at_slot = iota((16, tokens), 0) == slots[k : k + 1, :]
        found.append(jnp.sum(jnp.where(at_slot, by_slot, 0.0), axis=0, keepdims=True))
    inside = jnp.concatenate(found, axis=0) / sent
    outside = jnp.where(chosen >= experts, outside_ref[...], 0.0)
    scores = jnp.where(slots < 10, inside, outside)
    mean = jnp.sum(gating * scores, axis=0, keepdims=True)
    out_ref[...] = gating * (scores - mean)


def body(grad_output, logits, chosen, slots, other_scores, hidden, down_weight):
    tokens, topk = logits.shape
    window, capacity, units = hidden.shape[2], hidden.shape[3], hidden.shape[4]
    model = grad_output.shape[1]
    shard = down_weight.shape[1]
    expert = lax.axis_index(EXPERT)
    place = jnp.stack([lax.axis_index("core"), expert]).astype(jnp.int32)
    logits_t, chosen_t, slots_t = logits.T, chosen.T, slots.T
    swap = [(0, 1), (1, 0)]

    weights = down_weight.reshape(shard, model)
    beside = lax.ppermute(weights, "zl", swap)
    low = lax.axis_index("zl") == 0
    pair = jnp.stack([jnp.where(low, weights, beside), jnp.where(low, beside, weights)])
    own_weights = lax.all_gather(pair, "y").reshape(-1, model)

    packed = pl.pallas_call(
        pack_kernel,
        in_specs=[HBM] * 5,
        out_specs=VMEM,
        out_shape=jax.ShapeDtypeStruct((window * 8, model + model // FOLD), BF16),
        scratch_shapes=[
            pltpu.VMEM((topk, tokens), F32),
            pltpu.VMEM((topk, tokens), jnp.int32),
            pltpu.VMEM((topk, tokens), jnp.int32),
            pltpu.VMEM((tokens, model), BF16),
            pltpu.SemaphoreType.DMA((4,)),
        ],
        compiler_params=PARAMS,
        cost_estimate=cost(2 * 320 * tokens * model * 2, 4 * 320 * model),
        name="pack",
    )(*map(in_hbm, (logits_t, chosen_t, slots_t, grad_output, pair)))
    payload = lax.all_to_all(
        packed.reshape(window, 8, packed.shape[1]), EXPERT, split_axis=0, concat_axis=0, tiled=True
    ).reshape(packed.shape)

    by_slot = hidden.transpose(0, 1, 3, 2, 4).reshape(capacity * window, units)
    main, extra, main_t, extra_t = pl.pallas_call(
        functools.partial(hidden_kernel, shard),
        in_specs=[SMEM, VMEM],
        out_specs=[VMEM] * 4,
        out_shape=[
            jax.ShapeDtypeStruct((window * 8, units), BF16),
            jax.ShapeDtypeStruct((window * 2, units), BF16),
            jax.ShapeDtypeStruct((units, window * 8), BF16),
            jax.ShapeDtypeStruct((units, window * 2), BF16),
        ],
        compiler_params=PARAMS,
        cost_estimate=cost(4 * 320 * units * units, 8 * 320 * units),
        name="hidden_order",
    )(place, by_slot)

    arrived = lax.ppermute(half_partial(main_t, extra_t, payload, 1), "core", swap)
    both = half_partial(main_t, extra_t, payload, 0, arrived)
    pieces = lax.all_to_all(
        both.reshape(-1, shard, model), RING, split_axis=0, concat_axis=0, tiled=True
    )
    grad_down = summed(pieces).reshape(1, shard, model)

    own_weights = after(own_weights, both)
    other_weights = lax.ppermute(own_weights, "core", swap)
    grad, score = products(place, shard, main, extra, own_weights, other_weights, payload)
    grad_hidden = grad.reshape(1, 1, capacity, window, units).transpose(0, 1, 3, 2, 4)
    returned = exchanged_by_bits(score)
    grad_logits = pl.pallas_call(
        logits_kernel,
        in_specs=[SMEM] + [VMEM] * 5,
        out_specs=VMEM,
        out_shape=jax.ShapeDtypeStruct((topk, tokens), F32),
        compiler_params=PARAMS,
        cost_estimate=cost(0, 0),
        name="logits",
    )(place, logits_t, chosen_t, slots_t, other_scores.T, returned)
    return grad_hidden, grad_down, grad_logits.T


def solution(mesh):
    torus = Mesh(mesh.devices.reshape(4, 8, 8, 2, 2), ALL)
    in_specs = (
        P(ALL, None),
        P(ALL, None),
        P(ALL, None),
        P(ALL, None),
        P(ALL, None),
        P(EXPERT, DP, None, None, None),
        P(EXPERT, DP, None),
    )
    out_specs = (P(EXPERT, DP, None, None, None), P(EXPERT, DP, None), P(ALL, None))
    return jax.shard_map(body, mesh=torus, in_specs=in_specs, out_specs=out_specs, check_vma=False)
```

time: 190 us -> 158 us (0.83)
  the two profiles are of different devices: /device:TPU:16 before, /device:TPU:128 now
where the time goes in v2:
time: 158 us
  waiting for transfers between devices  61.7 us (39%)
  starting transfers between devices  57.8 us (37%)
  Pallas kernels  21 us (13%)
  between operations  14.2 us (9%)
  other arithmetic  1.71 us (1%)
    all_to_all x1, waiting for transfers between devices, body(): lax.all_to_all(packed.reshape(window, 8, packed.shape[1]), EXPERT, split_...  30.9 us
    ppermute x5, starting transfers between devices, exchanged_by_bits(): came = lax.ppermute(pairs[:, 1], axis, [(i, i ^ step) for i in range(size)])  24 us
    ppermute x5, waiting for transfers between devices, exchanged_by_bits(): came = lax.ppermute(pairs[:, 1], axis, [(i, i ^ step) for i in range(size)])  18.1 us
    ppermute x1, starting transfers between devices, body(): beside = lax.ppermute(weights, 'zl', swap)  13.3 us
    all_to_all x1, starting transfers between devices, body(): lax.all_to_all(packed.reshape(window, 8, packed.shape[1]), EXPERT, split_...  10.9 us
    pallas_call x2, Pallas kernels, half_partial(): pl.pallas_call(send_kernel if arrived is None else keep_kernel, grid=(FOL...  6.49 us
    pallas_call x1, Pallas kernels, products(): pl.pallas_call(functools.partial(product_kernel, shard), grid=(FOLD,), in...  6.26 us
    all_to_all x1, starting transfers between devices, body(): lax.all_to_all(both.reshape(-1, shard, model), RING, split_axis=0, concat...  5.74 us
  transfers between devices with their start and end apart: 11, of which 9 were waited for; matrix products, arithmetic and copies ran while one was open for 0% of the time, Pallas kernels for 10%

profile of v2, /device:TPU:128, one launch (start us, length us, event | category | flops | bytes accessed | tf_op | source)
XLA Modules:
  0.0 157.9 jit_solution(5733189147092671778)
XLA Ops:
  7.2 13.3 %collective-permute-start = (bf16[24,2048]{1,0:T(8,128)(2,1)}, bf16[24,2048]{1,0:T(8,128)(2,1)S(1)}, u32[]{:S(2)}, u32[]{:S(2)}) collective-permute-start(bf16[24,2048]{1,0:T(8,128)(2,1)} %bitcast.71), channel_id=1, source_target_pairs={{0,2},{2,0},{1,3},{3,1},{4,6},{6,4},{5,7},{7,5},{8,10},{10,8},{9,1... | collective-permute-start | bytes 294920 | tf_op jit(solution)/shard_map/ppermute | solution.py:339
  20.5 2.8 %collective-permute-done = bf16[24,2048]{1,0:T(8,128)(2,1)S(1)} collective-permute-done((bf16[24,2048]{1,0:T(8,128)(2,1)}, bf16[24,2048]{1,0:T(8,128)(2,1)S(1)}, u32[]{:S(2)}, u32[]{:S(2)}) %collective-permute-start) | collective-permute-done | bytes 98336 | tf_op jit(solution)/shard_map/ppermute | solution.py:339
  24.9 3.0 %pack.1 = bf16[256,2560]{1,0:T(8,128)(2,1)} custom-call(f32[8,128]{1,0:T(8,128)} %bitcast.60, s32[8,128]{1,0:T(8,128)} %bitcast.62, s32[8,128]{1,0:T(8,128)} %bitcast.64, bf16[128,2048]{1,0:T(8,128)(2,1)} %rows_in.1, bf16[2,24,2048]{2,1,0:T(8,128)(2,1)} %pad_maximum_fusion.first_in), custom_call_target="tpu_custom_call" | custom-call | flops 335544320 | bytes 2621440 | tf_op jit(solution)/shard_map/pack/pallas_call | solution.py:344
  27.9 10.9 %all-to-all-start = ((bf16[32,8,2560]{2,1,0:T(8,128)(2,1)}), bf16[32,8,2560]{2,1,0:T(8,128)(2,1)S(1)}, u32[]{:S(2)}, u32[]{:S(2)}) async-start(bf16[32,8,2560]{2,1,0:T(8,128)(2,1)} %bitcast.11), calls=%async_computation | async-start | bytes 2621440 | tf_op jit(solution)/shard_map/all_to_all | solution.py:360
  39.6 2.0 %hidden_order.1 = (bf16[256,768]{1,0:T(8,128)(2,1)S(1)}, bf16[64,768]{1,0:T(8,128)(2,1)S(1)}, bf16[768,256]{1,0:T(8,128)(2,1)S(1)}, bf16[768,64]{1,0:T(8,128)(2,1)S(1)}) custom-call(s32[2]{0:T(128)S(1)} %pad_add_fusion.core_ref.place_ref, bf16[320,768]{1,0:T(8,128)(2,1)S(1)} %bitcast.68), custom_call_target="tpu_custom_call" | custom-call | flops 754974720 | bytes 1966080 | tf_op jit(solution)/shard_map/hidden_order/pallas_call | solution.py:365
  41.6 30.9 %all-to-all-done = bf16[32,8,2560]{2,1,0:T(8,128)(2,1)S(1)} async-done(((bf16[32,8,2560]{2,1,0:T(8,128)(2,1)}), bf16[32,8,2560]{2,1,0:T(8,128)(2,1)S(1)}, u32[]{:S(2)}, u32[]{:S(2)}) %all-to-all-start) | async-done | bytes 1310752 | tf_op jit(solution)/shard_map/all_to_all | solution.py:360
  72.6 3.2 %half_sent.1 = bf16[384,2048]{1,0:T(8,128)(2,1)} custom-call(bf16[768,256]{1,0:T(8,128)(2,1)S(1)} %get-tuple-element.11.main_t_ref, bf16[768,64]{1,0:T(8,128)(2,1)S(1)} %get-tuple-element.12.extra_t_ref, bf16[256,2560]{1,0:T(8,128)(2,1)S(1)} %bitcast.52, bf16[256,2560]{1,0:T(8,128)(2,1)S(1)} %bitcast.53), custom_call_target="tpu_custom_call" | custom-call | flops 503316480 | bytes 4718592 | tf_op jit(solution)/shard_map/half_sent/pallas_call | solution.py:145
  75.8 1.9 %collective-permute-start.1 = (bf16[384,2048]{1,0:T(8,128)(2,1)}, bf16[384,2048]{1,0:T(8,128)(2,1)S(1)}, u32[]{:S(2)}, u32[]{:S(2)}) collective-permute-start(bf16[384,2048]{1,0:T(8,128)(2,1)} %half_sent.1), channel_id=1, source_target_pairs={{0,1},{1,0},{2,3},{3,2},{4,5},{5,4},{6,7},{7,6},{8,9},{9,8},{10,11... | collective-permute-start | bytes 4718600 | tf_op jit(solution)/shard_map/ppermute | solution.py:380
  77.7 3.6 %collective-permute-done.1.arrived_ref = bf16[384,2048]{1,0:T(8,128)(2,1)S(1)} collective-permute-done((bf16[384,2048]{1,0:T(8,128)(2,1)}, bf16[384,2048]{1,0:T(8,128)(2,1)S(1)}, u32[]{:S(2)}, u32[]{:S(2)}) %collective-permute-start.1) | collective-permute-done | bytes 1572896 | tf_op jit(solution)/shard_map/ppermute | solution.py:380
  81.3 3.3 %half_kept.1.b = bf16[384,2048]{1,0:T(8,128)(2,1)} custom-call(bf16[768,256]{1,0:T(8,128)(2,1)S(1)} %get-tuple-element.11.main_t_ref, bf16[768,64]{1,0:T(8,128)(2,1)S(1)} %get-tuple-element.12.extra_t_ref, bf16[256,2560]{1,0:T(8,128)(2,1)S(1)} %bitcast.54, bf16[256,2560]{1,0:T(8,128)(2,1)S(1)} %bitcast.55, ...), custom_call_target="tpu_custom_call" | custom-call | flops 503316480 | bytes 4718592 | tf_op jit(solution)/shard_map/half_kept/pallas_call | solution.py:145
  84.6 5.5 %all-gather.3.cloned.1.call-done = bf16[16,24,2048]{2,1,0:T(8,128)(2,1)} async-done(((bf16[2,24,2048]{2,1,0:T(8,128)(2,1)}), bf16[16,24,2048]{2,1,0:T(8,128)(2,1)}) %all-gather.3.cloned.1.call-update) | async-done | bytes 1572880 | tf_op jit(solution)/shard_map/all_gather | solution.py:342
  90.1 1.9 %collective-permute-start.2 = (bf16[384,2048]{1,0:T(8,128)(2,1)}, bf16[384,2048]{1,0:T(8,128)(2,1)}, u32[]{:S(2)}, u32[]{:S(2)}) collective-permute-start(bf16[384,2048]{1,0:T(8,128)(2,1)} %after.1.own_ref), channel_id=1, source_target_pairs={{0,1},{1,0},{2,3},{3,2},{4,5},{5,4},{6,7},{7,6},{8,9},{9,8},{10,11... | collective-permute-start | bytes 4718600 | tf_op jit(solution)/shard_map/ppermute | solution.py:388
  92.0 5.7 %all-to-all-start.1 = ((bf16[16,24,2048]{2,1,0:T(8,128)(2,1)}), bf16[16,24,2048]{2,1,0:T(8,128)(2,1)S(1)}, u32[]{:S(2)}, u32[]{:S(2)}) async-start(bf16[16,24,2048]{2,1,0:T(8,128)(2,1)} %bitcast.69), calls=%async_computation.1 | async-start | bytes 3145728 | tf_op jit(solution)/shard_map/all_to_all | solution.py:382
  99.2 6.3 %products.1 = (bf16[320,768]{1,0:T(8,128)(2,1)}, f32[32,128]{1,0:T(8,128)S(1)}) custom-call(s32[2]{0:T(128)S(1)} %pad_add_fusion.core_ref.place_ref, bf16[256,768]{1,0:T(8,128)(2,1)S(1)} %get-tuple-element.9.main_ref, bf16[64,768]{1,0:T(8,128)(2,1)S(1)} %get-tuple-element.10.extra_ref, bf16[384,2048]{1,0:T(8,128)(2,1)S(1)} %copy-done, ...), custom_call_target="tpu_custom_call" | custom-call | tf_op jit(solution)/shard_map/products/pallas_call | solution.py:228
  105.5 3.5 %collective-permute-start.3 = (f32[16,1,128]{2,0,1:T(8,128)S(1)}, f32[16,1,128]{2,0,1:T(8,128)S(1)}, u32[]{:S(2)}, u32[]{:S(2)}) collective-permute-start(f32[16,1,128]{2,0,1:T(8,128)S(1)} %bitcast.79), channel_id=1, source_target_pairs={{0,32},{32,0},{64,96},{96,64},{128,160},{160,128},{192,224},{224,1... | collective-permute-start | bytes 24584 | tf_op jit(solution)/shard_map/ppermute | solution.py:263
  109.0 2.0 %collective-permute-done.3 = f32[16,1,128]{2,0,1:T(8,128)S(1)} collective-permute-done((f32[16,1,128]{2,0,1:T(8,128)S(1)}, f32[16,1,128]{2,0,1:T(8,128)S(1)}, u32[]{:S(2)}, u32[]{:S(2)}) %collective-permute-start.3) | collective-permute-done | bytes 8224 | tf_op jit(solution)/shard_map/ppermute | solution.py:263
  111.0 4.2 %collective-permute-start.4 = (f32[8,2,128]{2,0,1:T(8,128)S(1)}, f32[8,2,128]{2,0,1:T(8,128)S(1)}, u32[]{:S(2)}, u32[]{:S(2)}) collective-permute-start(f32[8,2,128]{2,0,1:T(8,128)S(1)} %bitcast.78), channel_id=1, source_target_pairs={{0,64},{32,96},{64,0},{96,32},{128,192},{160,224},{192,128},{224,1... | collective-permute-start | bytes 24584 | tf_op jit(solution)/shard_map/ppermute | solution.py:263
  115.3 2.2 %collective-permute-done.4 = f32[8,2,128]{2,0,1:T(8,128)S(1)} collective-permute-done((f32[8,2,128]{2,0,1:T(8,128)S(1)}, f32[8,2,128]{2,0,1:T(8,128)S(1)}, u32[]{:S(2)}, u32[]{:S(2)}) %collective-permute-start.4) | collective-permute-done | bytes 8224 | tf_op jit(solution)/shard_map/ppermute | solution.py:263
  117.5 7.4 %collective-permute-start.5 = (f32[4,4,128]{2,0,1:T(4,128)S(1)}, f32[4,4,128]{2,0,1:T(4,128)S(1)}, u32[]{:S(2)}, u32[]{:S(2)}) collective-permute-start(f32[4,4,128]{2,0,1:T(4,128)S(1)} %bitcast.81), channel_id=1, source_target_pairs={{0,128},{32,160},{64,192},{96,224},{128,0},{160,32},{192,64},{224,... | collective-permute-start | bytes 24584 | tf_op jit(solution)/shard_map/ppermute | solution.py:263
  124.9 2.1 %collective-permute-done.5 = f32[4,4,128]{2,0,1:T(4,128)S(1)} collective-permute-done((f32[4,4,128]{2,0,1:T(4,128)S(1)}, f32[4,4,128]{2,0,1:T(4,128)S(1)}, u32[]{:S(2)}, u32[]{:S(2)}) %collective-permute-start.5) | collective-permute-done | bytes 8224 | tf_op jit(solution)/shard_map/ppermute | solution.py:263
  127.0 4.9 %collective-permute-start.6 = (f32[2,8,128]{2,1,0:T(8,128)S(1)}, f32[2,8,128]{2,1,0:T(8,128)S(1)}, u32[]{:S(2)}, u32[]{:S(2)}) collective-permute-start(f32[2,8,128]{2,1,0:T(8,128)S(1)} %get-tuple-element.20), channel_id=1, source_target_pairs={{0,256},{256,0},{512,768},{768,512},{1,257},{257,1},{513,769},{769... | collective-permute-start | bytes 24584 | tf_op jit(solution)/shard_map/ppermute | solution.py:263
  132.0 6.3 %collective-permute-done.6 = f32[2,8,128]{2,1,0:T(8,128)S(1)} collective-permute-done((f32[2,8,128]{2,1,0:T(8,128)S(1)}, f32[2,8,128]{2,1,0:T(8,128)S(1)}, u32[]{:S(2)}, u32[]{:S(2)}) %collective-permute-start.6) | collective-permute-done | bytes 8224 | tf_op jit(solution)/shard_map/ppermute | solution.py:263
  138.3 3.9 %collective-permute-start.7 = (f32[1,16,128]{2,1,0:T(8,128)S(1)}, f32[1,16,128]{2,1,0:T(8,128)S(1)}, u32[]{:S(2)}, u32[]{:S(2)}) collective-permute-start(f32[1,16,128]{2,1,0:T(8,128)S(1)} %get-tuple-element.18), channel_id=1, source_target_pairs={{0,512},{256,768},{512,0},{768,256},{1,513},{257,769},{513,1},{769... | collective-permute-start | bytes 24584 | tf_op jit(solution)/shard_map/ppermute | solution.py:263
  142.1 5.6 %collective-permute-done.7 = f32[1,16,128]{2,1,0:T(8,128)S(1)} collective-permute-done((f32[1,16,128]{2,1,0:T(8,128)S(1)}, f32[1,16,128]{2,1,0:T(8,128)S(1)}, u32[]{:S(2)}, u32[]{:S(2)}) %collective-permute-start.7) | collective-permute-done | bytes 8224 | tf_op jit(solution)/shard_map/ppermute | solution.py:263
  (32 shorter events, 7.2 us)
Async XLA Ops:
  7.2 16.1 %collective-permute-start = (bf16[24,2048]{1,0:T(8,128)(2,1)}, bf16[24,2048]{1,0:T(8,128)(2,1)S(1)}, u32[]{:S(2)}, u32[]{:S(2)}) collective-permute-start(bf16[24,2048]{1,0:T(8,128)(2,1)} %bitcast.71), channel_id=1, source_target_pairs={{0,2},{2,0},{1,3},{3,1},{4,6},{6,4},{5,7},{7,5},{8,10},{10,8},{9,1... | collective-permute-start | bytes 294920 | tf_op jit(solution)/shard_map/ppermute | solution.py:339
  27.9 11.8 %copy-start.5 = (bf16[1,1,32,10,768]{4,2,3,1,0:T(8,128)(2,1)S(1)}, bf16[1,1,32,10,768]{4,2,3,1,0:T(8,128)(2,1)}, u32[]{:S(2)}) copy-start(bf16[1,1,32,10,768]{4,2,3,1,0:T(8,128)(2,1)} %param.12) | copy-start | bytes 1474564
  27.9 44.7 %all-to-all-start = ((bf16[32,8,2560]{2,1,0:T(8,128)(2,1)}), bf16[32,8,2560]{2,1,0:T(8,128)(2,1)S(1)}, u32[]{:S(2)}, u32[]{:S(2)}) async-start(bf16[32,8,2560]{2,1,0:T(8,128)(2,1)} %bitcast.11), calls=%async_computation | async-start | bytes 2621440 | tf_op jit(solution)/shard_map/all_to_all | solution.py:360
  38.8 51.3 %all-gather.3.cloned.1.call-start = ((), (), s32[]{:S(2)}) async-start(), calls=%async_computation.2 | async-start | bytes 1769472 | tf_op jit(solution)/shard_map/all_gather | solution.py:342
  75.8 5.5 %collective-permute-start.1 = (bf16[384,2048]{1,0:T(8,128)(2,1)}, bf16[384,2048]{1,0:T(8,128)(2,1)S(1)}, u32[]{:S(2)}, u32[]{:S(2)}) collective-permute-start(bf16[384,2048]{1,0:T(8,128)(2,1)} %half_sent.1), channel_id=1, source_target_pairs={{0,1},{1,0},{2,3},{3,2},{4,5},{5,4},{6,7},{7,6},{8,9},{9,8},{10,11... | collective-permute-start | bytes 4718600 | tf_op jit(solution)/shard_map/ppermute | solution.py:380
  90.1 7.7 %collective-permute-start.2 = (bf16[384,2048]{1,0:T(8,128)(2,1)}, bf16[384,2048]{1,0:T(8,128)(2,1)}, u32[]{:S(2)}, u32[]{:S(2)}) collective-permute-start(bf16[384,2048]{1,0:T(8,128)(2,1)} %after.1.own_ref), channel_id=1, source_target_pairs={{0,1},{1,0},{2,3},{3,2},{4,5},{5,4},{6,7},{7,6},{8,9},{9,8},{10,11... | collective-permute-start | bytes 4718600 | tf_op jit(solution)/shard_map/ppermute | solution.py:388
  92.0 57.5 %all-to-all-start.1 = ((bf16[16,24,2048]{2,1,0:T(8,128)(2,1)}), bf16[16,24,2048]{2,1,0:T(8,128)(2,1)S(1)}, u32[]{:S(2)}, u32[]{:S(2)}) async-start(bf16[16,24,2048]{2,1,0:T(8,128)(2,1)} %bitcast.69), calls=%async_computation.1 | async-start | bytes 3145728 | tf_op jit(solution)/shard_map/all_to_all | solution.py:382
  97.8 1.4 copy-start
  99.2 48.5 %copy-start.1 = (f32[128,8]{0,1:T(8,128)S(1)}, f32[128,8]{0,1:T(8,128)}, u32[]{:S(2)}) copy-start(f32[128,8]{0,1:T(8,128)} %param.8) | copy-start | bytes 12292
  99.2 48.5 %copy-start.2 = (s32[128,8]{0,1:T(8,128)S(1)}, s32[128,8]{0,1:T(8,128)}, u32[]{:S(2)}) copy-start(s32[128,8]{0,1:T(8,128)} %param.9) | copy-start | bytes 12292
  99.2 48.5 %copy-start.3 = (s32[128,8]{0,1:T(8,128)S(1)}, s32[128,8]{0,1:T(8,128)}, u32[]{:S(2)}) copy-start(s32[128,8]{0,1:T(8,128)} %param.10) | copy-start | bytes 12292
  99.2 48.5 %copy-start.4 = (f32[128,8]{0,1:T(8,128)S(1)}, f32[128,8]{0,1:T(8,128)}, u32[]{:S(2)}) copy-start(f32[128,8]{0,1:T(8,128)} %param.11) | copy-start | bytes 12292
  105.5 5.5 %collective-permute-start.3 = (f32[16,1,128]{2,0,1:T(8,128)S(1)}, f32[16,1,128]{2,0,1:T(8,128)S(1)}, u32[]{:S(2)}, u32[]{:S(2)}) collective-permute-start(f32[16,1,128]{2,0,1:T(8,128)S(1)} %bitcast.79), channel_id=1, source_target_pairs={{0,32},{32,0},{64,96},{96,64},{128,160},{160,128},{192,224},{224,1... | collective-permute-start | bytes 24584 | tf_op jit(solution)/shard_map/ppermute | solution.py:263
  111.0 6.4 %collective-permute-start.4 = (f32[8,2,128]{2,0,1:T(8,128)S(1)}, f32[8,2,128]{2,0,1:T(8,128)S(1)}, u32[]{:S(2)}, u32[]{:S(2)}) collective-permute-start(f32[8,2,128]{2,0,1:T(8,128)S(1)} %bitcast.78), channel_id=1, source_target_pairs={{0,64},{32,96},{64,0},{96,32},{128,192},{160,224},{192,128},{224,1... | collective-permute-start | bytes 24584 | tf_op jit(solution)/shard_map/ppermute | solution.py:263
  117.5 9.5 %collective-permute-start.5 = (f32[4,4,128]{2,0,1:T(4,128)S(1)}, f32[4,4,128]{2,0,1:T(4,128)S(1)}, u32[]{:S(2)}, u32[]{:S(2)}) collective-permute-start(f32[4,4,128]{2,0,1:T(4,128)S(1)} %bitcast.81), channel_id=1, source_target_pairs={{0,128},{32,160},{64,192},{96,224},{128,0},{160,32},{192,64},{224,... | collective-permute-start | bytes 24584 | tf_op jit(solution)/shard_map/ppermute | solution.py:263
  127.0 11.2 %collective-permute-start.6 = (f32[2,8,128]{2,1,0:T(8,128)S(1)}, f32[2,8,128]{2,1,0:T(8,128)S(1)}, u32[]{:S(2)}, u32[]{:S(2)}) collective-permute-start(f32[2,8,128]{2,1,0:T(8,128)S(1)} %get-tuple-element.20), channel_id=1, source_target_pairs={{0,256},{256,0},{512,768},{768,512},{1,257},{257,1},{513,769},{769... | collective-permute-start | bytes 24584 | tf_op jit(solution)/shard_map/ppermute | solution.py:263
  138.3 9.4 %collective-permute-start.7 = (f32[1,16,128]{2,1,0:T(8,128)S(1)}, f32[1,16,128]{2,1,0:T(8,128)S(1)}, u32[]{:S(2)}, u32[]{:S(2)}) collective-permute-start(f32[1,16,128]{2,1,0:T(8,128)S(1)} %get-tuple-element.18), channel_id=1, source_target_pairs={{0,512},{256,768},{512,0},{768,256},{1,513},{257,769},{513,1},{769... | collective-permute-start | bytes 24584 | tf_op jit(solution)/shard_map/ppermute | solution.py:263
Sparse Core Ops, SparseCore 0:
  42.9 47.1 all-gather.2

commit v3 on v2

--- a/solution.py
+++ b/solution.py
@@ -42,7 +42,7 @@
     return raised / jnp.sum(raised, axis=0, keepdims=True)
 
 
-def pack_kernel(logits_in, chosen_in, slots_in, rows_in, first_in, out_ref, *scratch):
+def pack_kernel(logits_in, chosen_in, slots_in, rows_in, out_ref, *scratch):
     held, sems = scratch[:4], scratch[4]
     copies = [
         pltpu.make_async_copy(src, dst, sems.at[k])
@@ -86,20 +86,17 @@
     return block * (2 * shard) + side * shard + (inner - block * shard)
 
 
-def hidden_kernel(shard, core_ref, hidden_ref, main_ref, extra_ref, main_t_ref, extra_t_ref):
-    rows, units = main_ref.shape
-    to_unit = permuted_units(core_ref[0], units, shard)
+def hidden_kernel(shard, place_ref, hidden_ref, main_t_ref, extra_t_ref):
+    units, rows = main_t_ref.shape
+    to_unit = permuted_units(place_ref[0], units, shard)
     column = onehot(iota((units, units), 0) == to_unit)
     source = rows // 8
     here = iota((rows, rows), 0)
     there = iota((rows, rows), 1)
     turn = onehot(there == (here % 8) * source + here // 8)
     turned = dot(turn, hidden_ref[:rows, :]).astype(BF16)
-    last = hidden_ref[rows:, :]
-    main_ref[...] = dot(turned, column).astype(BF16)
-    extra_ref[...] = dot(last, column).astype(BF16)
     main_t_ref[...] = dot(column, turned, 0, 1).astype(BF16)
-    extra_t_ref[...] = dot(column, last, 0, 1).astype(BF16)
+    extra_t_ref[...] = dot(column, hidden_ref[rows:, :], 0, 1).astype(BF16)
 
 
 def unfolded(block, m):
@@ -112,53 +109,48 @@
     return dot(pick, block).astype(BF16)
 
 
-def half_product(main_t_ref, extra_t_ref, rows_ref, fold_ref):
-    total = dot(main_t_ref[...], rows_ref[...])
-    return total + dot(extra_t_ref[...], unfolded(fold_ref[...], pl.program_id(0)))
-
-
-def send_kernel(main_t_ref, extra_t_ref, rows_ref, fold_ref, out_ref):
-    out_ref[...] = half_product(main_t_ref, extra_t_ref, rows_ref, fold_ref).astype(BF16)
-
-
-def keep_kernel(main_t_ref, extra_t_ref, rows_ref, fold_ref, arrived_ref, out_ref):
-    total = half_product(main_t_ref, extra_t_ref, rows_ref, fold_ref)
-    out_ref[...] = (total + arrived_ref[...].astype(F32)).astype(BF16)
-
-
-def half_partial(main_t, extra_t, payload, half, arrived=None):
+def half_kernel(half, adds, main_t_ref, extra_t_ref, payload_ref, *refs):
+    *given, out_ref, held, sems = refs
+    units, width = held.shape
+    part = width // FOLD
+    span = slice(half * units, (half + 1) * units)
+    main_t, extra_t = main_t_ref[span, :], extra_t_ref[span, :]
+    fold = payload_ref[:, width:]
+    copies = []
+    for m in range(FOLD):
+        cols = slice(m * part, (m + 1) * part)
+        total = dot(main_t, payload_ref[:, cols]) + dot(extra_t, unfolded(fold, m))
+        if adds:
+            total = total + given[0][:, cols].astype(F32)
+        held[:, cols] = total.astype(BF16)
+        copies.append(pltpu.make_async_copy(held.at[:, cols], out_ref.at[:, cols], sems.at[m]))
+        copies[-1].start()
+    for copy in copies:
+        copy.wait()
+
+
+def half_partial(main_t, extra_t, payload, half, arrived=None, first=()):
+    given = [] if arrived is None else [arrived]
     units, rows = main_t.shape
     few = extra_t.shape[1]
     width = payload.shape[1] * FOLD // (FOLD + 1)
-    part = width // FOLD
-    in_specs = [
-        pl.BlockSpec((units // 2, rows), lambda m: (half, 0)),
-        pl.BlockSpec((units // 2, few), lambda m: (half, 0)),
-        pl.BlockSpec((rows, part), lambda m: (0, m)),
-        pl.BlockSpec((rows, part), lambda m: (0, FOLD)),
-    ]
-    operands = [main_t, extra_t, payload, payload]
-    tile = pl.BlockSpec((units // 2, part), lambda m: (0, m))
-    if arrived is not None:
-        in_specs.append(tile)
-        operands.append(arrived)
-    return pl.pallas_call(
-        send_kernel if arrived is None else keep_kernel,
-        grid=(FOLD,),
-        in_specs=in_specs,
-        out_specs=tile,
+    return pl.pallas_call(
+        functools.partial(half_kernel, half, bool(given)),
+        in_specs=[VMEM] * (3 + len(given)) + [HBM] * len(first),
+        out_specs=HBM,
         out_shape=pltpu.HBM((units // 2, width), BF16),
+        scratch_shapes=[pltpu.VMEM((units // 2, width), BF16), pltpu.SemaphoreType.DMA((FOLD,))],
         compiler_params=PARAMS,
         cost_estimate=cost(units * (rows + few) * width, 3 * units * width),
-        name="half_sent" if arrived is None else "half_kept",
-    )(*operands)
+        name="half_kept" if given else "half_sent",
+    )(main_t, extra_t, payload, *given, *map(in_hbm, first))
 
 
 def product_kernel(
     shard,
-    core_ref,
-    main_ref,
-    extra_ref,
+    place_ref,
+    main_t_ref,
+    extra_t_ref,
     own_ref,
     other_ref,
     rows_ref,
@@ -169,8 +161,10 @@
     acc_extra,
 ):
     g = pl.program_id(0)
-    rows, units = main_ref.shape
+    units, rows = main_t_ref.shape
+    few = extra_t_ref.shape[1]
     half = units // 2
+    source = rows // 8
 
     @pl.when(g == 0)
     def _():
@@ -181,31 +175,31 @@
     more = unfolded(fold_ref[...], g)
     for h, weight in enumerate((own_ref[...], other_ref[...])):
         span = slice(h * half, (h + 1) * half)
-        acc_main[:, span] += dot(block, weight, 1, 1)
-        acc_extra[:, span] += dot(more, weight, 1, 1)
+        acc_main[span, :] += dot(weight, block, 1, 1)
+        acc_extra[span, :] += dot(weight, more, 1, 1)
 
     @pl.when(g == FOLD - 1)
     def _():
         main, extra = acc_main[...], acc_extra[...]
-        main_score = jnp.sum(main * main_ref[...].astype(F32), axis=1, keepdims=True)
-        extra_score = jnp.sum(extra * extra_ref[...].astype(F32), axis=1, keepdims=True)
-        source = rows // 8
-        lane = iota((rows, 128), 1)
-        spread = jnp.where(lane == iota((rows, 128), 0) % 8, main_score, 0.0)
-        scores = jnp.sum(spread.reshape(source, 8, 128), axis=1)
-        lane = iota((source, 128), 1)
-        for c in range(2):
-            scores = jnp.where(lane == 8 + c, extra_score[c * source : (c + 1) * source, :], scores)
-        pick = (iota((source, source), 0) ^ core_ref[1]) == iota((source, source), 1)
-        score_ref[...] = exact_dot(jnp.where(pick, 1.0, 0.0), scores)
-        to_unit = permuted_units(core_ref[0], units, shard)
+        main_score = jnp.sum(main * main_t_ref[...].astype(F32), axis=0, keepdims=True)
+        extra_score = jnp.sum(extra * extra_t_ref[...].astype(F32), axis=0, keepdims=True)
+        to_main = (iota((source, rows), 0) ^ place_ref[1]) == iota((source, rows), 1) // 8
+        at_main = iota((rows, 128), 0) % 8 == iota((rows, 128), 1)
+        to_extra = (iota((source, few), 0) ^ place_ref[1]) == iota((source, few), 1) % source
+        at_extra = iota((few, 128), 0) // source + 8 == iota((few, 128), 1)
+        score_ref[...] = exact_dot(
+            jnp.where(to_main, main_score, 0.0), jnp.where(at_main, 1.0, 0.0)
+        ) + exact_dot(jnp.where(to_extra, extra_score, 0.0), jnp.where(at_extra, 1.0, 0.0))
+        to_unit = permuted_units(place_ref[0], units, shard)
         column = onehot(iota((units, units), 0) == to_unit)
         here = iota((rows, rows), 0)
         there = iota((rows, rows), 1)
         turn = onehot(there == (here % source) * 8 + here // source)
-        turned = dot(turn, main.astype(BF16)).astype(BF16)
-        grad_ref[:rows, :] = dot(turned, column, 1, 1).astype(BF16)
-        grad_ref[rows:, :] = dot(extra.astype(BF16), column, 1, 1).astype(BF16)
+        keep = onehot(iota((few, few), 0) == iota((few, few), 1))
+        main = dot(column, main.astype(BF16)).astype(BF16)
+        extra = dot(column, extra.astype(BF16)).astype(BF16)
+        grad_ref[:rows, :] = dot(turn, main, 1, 1).astype(BF16)
+        grad_ref[rows:, :] = dot(keep, extra, 1, 1).astype(BF16)
 
 
 def exact_dot(a, b, ca=1, cb=0):
@@ -218,9 +212,9 @@
     )
 
 
-def products(place, shard, main, extra, own, other, payload):
-    rows, units = main.shape
-    few = rows // FOLD
+def products(place, shard, main_t, extra_t, own, other, payload):
+    units, rows = main_t.shape
+    few = extra_t.shape[1]
     width = payload.shape[1] * FOLD // (FOLD + 1)
     part = width // FOLD
     fixed = lambda g: (0, 0)
@@ -230,8 +224,8 @@
         grid=(FOLD,),
         in_specs=[
             SMEM,
-            pl.BlockSpec((rows, units), fixed),
-            pl.BlockSpec((few, units), fixed),
+            pl.BlockSpec((units, rows), fixed),
+            pl.BlockSpec((units, few), fixed),
             pl.BlockSpec((units // 2, part), moving),
             pl.BlockSpec((units // 2, part), moving),
             pl.BlockSpec((rows, part), moving),
@@ -245,11 +239,72 @@
             jax.ShapeDtypeStruct((rows + few, units), BF16),
             jax.ShapeDtypeStruct((rows // 8, 128), F32),
         ],
-        scratch_shapes=[pltpu.VMEM((rows, units), F32), pltpu.VMEM((few, units), F32)],
+        scratch_shapes=[pltpu.VMEM((units, rows), F32), pltpu.VMEM((units, few), F32)],
         compiler_params=PARAMS,
         cost_estimate=cost(0, 0),
         name="products",
-    )(place, main, extra, own, other, payload, payload)
+    )(place, main_t, extra_t, own, other, payload, payload)
+
+
+def placed_kernel(place_ref, *refs):
+    *pieces, out_ref, sems = refs
+    count = len(pieces)
+    copies = []
+    for k, piece in enumerate(pieces):
+        base = lax.rem(place_ref[2] + k, count) * 2
+        for t in range(2):
+            spot = base + (place_ref[3] ^ t)
+            copies.append(pltpu.make_async_copy(piece.at[t], out_ref.at[spot], sems.at[2 * k + t]))
+            copies[-1].start()
+    for copy in copies:
+        copy.wait()
+
+
+def gathered(place, pair):
+    size = lax.axis_size("y")
+    down = [(i, (i + size - 1) % size) for i in range(size)]
+    up = [(i, (i + 1) % size) for i in range(size)]
+    pieces = [pair] + [None] * (size - 1)
+    above = below = pair
+    for k in range(1, size // 2 + 1):
+        above = lax.ppermute(above, "y", down)
+        pieces[k] = above
+        if k < size - k:
+            below = lax.ppermute(below, "y", up)
+            pieces[size - k] = below
+    shape = (2 * size, *pair.shape[1:])
+    return pl.pallas_call(
+        placed_kernel,
+        in_specs=[SMEM] + [HBM] * size,
+        out_specs=HBM,
+        out_shape=pltpu.HBM(shape, pair.dtype),
+        scratch_shapes=[pltpu.SemaphoreType.DMA((2 * size,))],
+        cost_estimate=cost(0, 0),
+        name="placed",
+    )(place, *pieces), pieces
+
+
+def pair_kernel(weights_ref, beside_ref, out_ref, sems):
+    copies = [
+        pltpu.make_async_copy(src, out_ref.at[k], sems.at[k])
+        for k, src in enumerate((weights_ref, beside_ref))
+    ]
+    for copy in copies:
+        copy.start()
+    for copy in copies:
+        copy.wait()
+
+
+def paired(weights, beside):
+    return pl.pallas_call(
+        pair_kernel,
+        in_specs=[HBM] * 2,
+        out_specs=HBM,
+        out_shape=pltpu.HBM((2, *weights.shape), weights.dtype),
+        scratch_shapes=[pltpu.SemaphoreType.DMA((2,))],
+        cost_estimate=cost(0, 0),
+        name="paired",
+    )(weights, beside)
 
 
 def exchanged_by_bits(blocks):
@@ -270,13 +325,19 @@
     return pltpu.with_memory_space_constraint(array, pltpu.HBM)
 
 
+def after_kernel(array_ref, first_ref, out_ref, sem):
+    copy = pltpu.make_async_copy(array_ref, out_ref, sem)
+    copy.start()
+    copy.wait()
+
+
 def after(array, first):
     return pl.pallas_call(
-        lambda a, b, c: None,
+        after_kernel,
         in_specs=[HBM, HBM],
         out_specs=HBM,
         out_shape=pltpu.HBM(array.shape, array.dtype),
-        input_output_aliases={0: 0},
+        scratch_shapes=[pltpu.SemaphoreType.DMA],
         cost_estimate=cost(0, 0),
         name="after",
     )(array, first)
@@ -331,19 +392,14 @@
     model = grad_output.shape[1]
     shard = down_weight.shape[1]
     expert = lax.axis_index(EXPERT)
-    place = jnp.stack([lax.axis_index("core"), expert]).astype(jnp.int32)
+    place = [lax.axis_index("core"), expert, lax.axis_index("y"), lax.axis_index("zl")]
+    place = jnp.stack(place).astype(jnp.int32)
     logits_t, chosen_t, slots_t = logits.T, chosen.T, slots.T
     swap = [(0, 1), (1, 0)]
 
-    weights = down_weight.reshape(shard, model)
-    beside = lax.ppermute(weights, "zl", swap)
-    low = lax.axis_index("zl") == 0
-    pair = jnp.stack([jnp.where(low, weights, beside), jnp.where(low, beside, weights)])
-    own_weights = lax.all_gather(pair, "y").reshape(-1, model)
-
     packed = pl.pallas_call(
         pack_kernel,
-        in_specs=[HBM] * 5,
+        in_specs=[HBM] * 4,
         out_specs=VMEM,
         out_shape=jax.ShapeDtypeStruct((window * 8, model + model // FOLD), BF16),
         scratch_shapes=[
@@ -356,19 +412,23 @@
         compiler_params=PARAMS,
         cost_estimate=cost(2 * 320 * tokens * model * 2, 4 * 320 * model),
         name="pack",
-    )(*map(in_hbm, (logits_t, chosen_t, slots_t, grad_output, pair)))
+    )(*map(in_hbm, (logits_t, chosen_t, slots_t, grad_output)))
     payload = lax.all_to_all(
         packed.reshape(window, 8, packed.shape[1]), EXPERT, split_axis=0, concat_axis=0, tiled=True
     ).reshape(packed.shape)
 
+    weights = after(down_weight.reshape(shard, model), packed)
+    beside = lax.ppermute(weights, "zl", swap)
+    own_weights, pieces = gathered(place, paired(weights, beside))
+    own_weights = own_weights.reshape(-1, model)
+    other_weights = lax.ppermute(own_weights, "core", swap)
+
     by_slot = hidden.transpose(0, 1, 3, 2, 4).reshape(capacity * window, units)
-    main, extra, main_t, extra_t = pl.pallas_call(
+    main_t, extra_t = pl.pallas_call(
         functools.partial(hidden_kernel, shard),
         in_specs=[SMEM, VMEM],
-        out_specs=[VMEM] * 4,
+        out_specs=[VMEM] * 2,
         out_shape=[
-            jax.ShapeDtypeStruct((window * 8, units), BF16),
-            jax.ShapeDtypeStruct((window * 2, units), BF16),
             jax.ShapeDtypeStruct((units, window * 8), BF16),
             jax.ShapeDtypeStruct((units, window * 2), BF16),
         ],
@@ -377,16 +437,15 @@
         name="hidden_order",
     )(place, by_slot)
 
-    arrived = lax.ppermute(half_partial(main_t, extra_t, payload, 1), "core", swap)
+    sent = half_partial(main_t, extra_t, payload, 1, first=(pieces[3], pieces[-3]))
+    arrived = lax.ppermute(sent, "core", swap)
     both = half_partial(main_t, extra_t, payload, 0, arrived)
     pieces = lax.all_to_all(
         both.reshape(-1, shard, model), RING, split_axis=0, concat_axis=0, tiled=True
     )
     grad_down = summed(pieces).reshape(1, shard, model)
 
-    own_weights = after(own_weights, both)
-    other_weights = lax.ppermute(own_weights, "core", swap)
-    grad, score = products(place, shard, main, extra, own_weights, other_weights, payload)
+    grad, score = products(place, shard, main_t, extra_t, own_weights, other_weights, payload)
     grad_hidden = grad.reshape(1, 1, capacity, window, units).transpose(0, 1, 3, 2, 4)
     returned = exchanged_by_bits(score)
     grad_logits = pl.pallas_call(

time: 158 us -> 227 us (1.44)
  Pallas kernels: 21 us -> 79.8 us
  starting transfers between devices: 57.8 us -> 87.8 us
  between operations: 14.2 us -> 0.99 us
  waiting for transfers between devices: 61.7 us -> 54.7 us
    pallas_call x4 -> x6, Pallas kernels: 9.45 us -> 68.5 us  [the longest x1 49.6 us: gathered(): pl.pallas_call(placed_kernel, in_specs=[SMEM] + [HBM] * size, out_specs=H...]
    all_to_all x1, waiting for transfers between devices: 30.9 us -> 0.01 us  [body(): lax.all_to_all(packed.reshape(window, 8, packed.shape[1]), EXPERT, split_...]
    ppermute x1 -> x8, starting transfers between devices: 1.91 us -> 29.7 us  [the longest x4 20.3 us: gathered(): above = lax.ppermute(above, 'y', down)]
    ppermute x1, waiting for transfers between devices: 2.78 us -> 25.1 us  [body(): beside = lax.ppermute(weights, 'zl', swap)]
    ppermute x1, starting transfers between devices: 13.3 us -> 1.92 us  [body(): beside = lax.ppermute(weights, 'zl', swap)]
    all_to_all x1, starting transfers between devices: 10.9 us -> 20.2 us  [body(): lax.all_to_all(packed.reshape(window, 8, packed.shape[1]), EXPERT, split_...]
    ppermute x1 -> x8, waiting for transfers between devices: 3.59 us -> 10.7 us  [the longest x4 6.62 us: gathered(): above = lax.ppermute(above, 'y', down)]
    all_gather x1 -> x0, waiting for transfers between devices: 5.54 us -> none  [body(): own_weights = lax.all_gather(pair, 'y').reshape(-1, model)]
  transfers between devices with their start and end apart: 11 -> 17, of which waited for: 9 -> 11; matrix products, arithmetic and copies ran while one was open for 0% -> 0% of each run, Pallas kernels for 10% -> 32%
where the time goes in v3:
time: 227 us; the launch traced here: 226 us
  starting transfers between devices  87.8 us (39%)
  Pallas kernels  79.8 us (35%)
  waiting for transfers between devices  54.7 us (24%)
  local copies, waits for them, and re-layouts  2.82 us (1%)
    pallas_call x1, Pallas kernels, gathered(): pl.pallas_call(placed_kernel, in_specs=[SMEM] + [HBM] * size, out_specs=H...  49.6 us
    ppermute x1, waiting for transfers between devices, body(): beside = lax.ppermute(weights, 'zl', swap)  25.1 us
    ppermute x5, starting transfers between devices, exchanged_by_bits(): came = lax.ppermute(pairs[:, 1], axis, [(i, i ^ step) for i in range(size)])  23.9 us
    ppermute x4, starting transfers between devices, gathered(): above = lax.ppermute(above, 'y', down)  20.3 us
    all_to_all x1, starting transfers between devices, body(): lax.all_to_all(packed.reshape(window, 8, packed.shape[1]), EXPERT, split_...  20.2 us
    ppermute x5, waiting for transfers between devices, exchanged_by_bits(): came = lax.ppermute(pairs[:, 1], axis, [(i, i ^ step) for i in range(size)])  18.9 us
    all_to_all x1, starting transfers between devices, body(): lax.all_to_all(both.reshape(-1, shard, model), RING, split_axis=0, concat...  10.1 us
    ppermute x3, starting transfers between devices, gathered(): below = lax.ppermute(below, 'y', up)  7.47 us
  transfers between devices with their start and end apart: 17, of which 11 were waited for; matrix products, arithmetic and copies ran while one was open for 0% of the time, Pallas kernels for 32%

profile of v3, /device:TPU:128, one launch (start us, length us, event | category | flops | bytes accessed | tf_op | source)
XLA Modules:
  0.0 226.2 jit_solution(10733843424898808875)
XLA Ops:
  0.6 3.0 %pack.1.first_ref = bf16[256,2560]{1,0:T(8,128)(2,1)} custom-call(f32[8,128]{1,0:T(8,128)} %bitcast.55, s32[8,128]{1,0:T(8,128)} %bitcast.57, s32[8,128]{1,0:T(8,128)} %bitcast.59, bf16[128,2048]{1,0:T(8,128)(2,1)} %rows_in.1), custom_call_target="tpu_custom_call" | custom-call | flops 335544320 | bytes 2621440 | tf_op jit(solution)/shard_map/pack/pallas_call | solution.py:400
  3.6 20.2 %all-to-all-start = ((bf16[32,8,2560]{2,1,0:T(8,128)(2,1)}), bf16[32,8,2560]{2,1,0:T(8,128)(2,1)S(1)}, u32[]{:S(2)}, u32[]{:S(2)}) async-start(bf16[32,8,2560]{2,1,0:T(8,128)(2,1)} %bitcast.11), calls=%async_computation | async-start | bytes 2621440 | tf_op jit(solution)/shard_map/all_to_all | solution.py:416
  23.8 4.1 %after.1.weights_ref = bf16[24,2048]{1,0:T(8,128)(2,1)} custom-call(bf16[24,2048]{1,0:T(8,128)(2,1)} %bitcast.66, bf16[256,2560]{1,0:T(8,128)(2,1)} %pack.1.first_ref), custom_call_target="tpu_custom_call" | custom-call | tf_op jit(solution)/shard_map/after/pallas_call | solution.py:335
  29.9 25.1 %collective-permute-done.beside_ref = bf16[24,2048]{1,0:T(8,128)(2,1)S(1)} collective-permute-done((bf16[24,2048]{1,0:T(8,128)(2,1)}, bf16[24,2048]{1,0:T(8,128)(2,1)S(1)}, u32[]{:S(2)}, u32[]{:S(2)}) %collective-permute-start) | collective-permute-done | bytes 98336 | tf_op jit(solution)/shard_map/ppermute | solution.py:421
  55.6 7.1 %paired.1.refs_0_ = bf16[2,24,2048]{2,1,0:T(8,128)(2,1)} custom-call(bf16[24,2048]{1,0:T(8,128)(2,1)} %after.1.weights_ref, bf16[24,2048]{1,0:T(8,128)(2,1)} %copy-done.14), custom_call_target="tpu_custom_call" | custom-call | tf_op jit(solution)/shard_map/paired/pallas_call | solution.py:299
  62.6 3.7 %collective-permute-start.5 = (bf16[2,24,2048]{2,1,0:T(8,128)(2,1)}, bf16[2,24,2048]{2,1,0:T(8,128)(2,1)S(1)}, u32[]{:S(2)}, u32[]{:S(2)}) collective-permute-start(bf16[2,24,2048]{2,1,0:T(8,128)(2,1)} %paired.1.refs_0_), channel_id=1, source_target_pairs={{0,4},{4,8},{8,12},{12,16},{16,20},{20,24},{24,28},{28,0},{1,5},{5... | collective-permute-start | bytes 589832 | tf_op jit(solution)/shard_map/ppermute | solution.py:273
  66.3 4.5 %collective-permute-start.1 = (bf16[2,24,2048]{2,1,0:T(8,128)(2,1)}, bf16[2,24,2048]{2,1,0:T(8,128)(2,1)S(1)}, u32[]{:S(2)}, u32[]{:S(2)}) collective-permute-start(bf16[2,24,2048]{2,1,0:T(8,128)(2,1)} %paired.1.refs_0_), channel_id=1, source_target_pairs={{0,28},{4,0},{8,4},{12,8},{16,12},{20,16},{24,20},{28,24},{1,29},{... | collective-permute-start | bytes 589832 | tf_op jit(solution)/shard_map/ppermute | solution.py:270
  70.8 2.4 %collective-permute-done.5.refs_7_ = bf16[2,24,2048]{2,1,0:T(8,128)(2,1)S(1)} collective-permute-done((bf16[2,24,2048]{2,1,0:T(8,128)(2,1)}, bf16[2,24,2048]{2,1,0:T(8,128)(2,1)S(1)}, u32[]{:S(2)}, u32[]{:S(2)}) %collective-permute-start.5) | collective-permute-done | bytes 196640 | tf_op jit(solution)/shard_map/ppermute | solution.py:273
  75.1 5.1 %collective-permute-start.2 = (bf16[2,24,2048]{2,1,0:T(8,128)(2,1)S(1)}, bf16[2,24,2048]{2,1,0:T(8,128)(2,1)S(1)}, u32[]{:S(2)}, u32[]{:S(2)}) collective-permute-start(bf16[2,24,2048]{2,1,0:T(8,128)(2,1)S(1)} %collective-permute-done.1.refs_1_), channel_id=1, source_target_pairs={{0,28},{4,0},{8,4},{12,8},{16,12},{20,16},{24,20},{28,24},{1,29},{... | collective-permute-start | bytes 589832 | tf_op jit(solution)/shard_map/ppermute | solution.py:270
  83.9 5.1 %collective-permute-start.3 = (bf16[2,24,2048]{2,1,0:T(8,128)(2,1)S(1)}, bf16[2,24,2048]{2,1,0:T(8,128)(2,1)S(1)}, u32[]{:S(2)}, u32[]{:S(2)}) collective-permute-start(bf16[2,24,2048]{2,1,0:T(8,128)(2,1)S(1)} %collective-permute-done.2.refs_2_), channel_id=1, source_target_pairs={{0,28},{4,0},{8,4},{12,8},{16,12},{20,16},{24,20},{28,24},{1,29},{... | collective-permute-start | bytes 589832 | tf_op jit(solution)/shard_map/ppermute | solution.py:270
  92.9 2.4 %half_sent.1 = bf16[384,2048]{1,0:T(8,128)(2,1)} custom-call(bf16[768,256]{1,0:T(8,128)(2,1)S(1)} %get-tuple-element.7.main_t_ref, bf16[768,64]{1,0:T(8,128)(2,1)S(1)} %get-tuple-element.8.extra_t_ref, bf16[256,2560]{1,0:T(8,128)(2,1)S(1)} %bitcast.48, bf16[2,24,2048]{2,1,0:T(8,128)(2,1)} %copy-done.9, bf16[2,24,2048]{2,1,0:T(8,128)(2,1)} %copy-done.8), custom_call_target="tpu_custom_call" | custom-call | flops 503316480 | bytes 4718592 | tf_op jit(solution)/shard_map/half_sent/pallas_call | solution.py:137
  97.2 5.6 %collective-permute-start.4 = (bf16[2,24,2048]{2,1,0:T(8,128)(2,1)}, bf16[2,24,2048]{2,1,0:T(8,128)(2,1)}, u32[]{:S(2)}, u32[]{:S(2)}) collective-permute-start(bf16[2,24,2048]{2,1,0:T(8,128)(2,1)} %copy-done.9), channel_id=1, source_target_pairs={{0,28},{4,0},{8,4},{12,8},{16,12},{20,16},{24,20},{28,24},{1,29},{... | collective-permute-start | bytes 589832 | tf_op jit(solution)/shard_map/ppermute | solution.py:270
  102.8 5.1 %collective-permute-done.4.refs_4_ = bf16[2,24,2048]{2,1,0:T(8,128)(2,1)} collective-permute-done((bf16[2,24,2048]{2,1,0:T(8,128)(2,1)}, bf16[2,24,2048]{2,1,0:T(8,128)(2,1)}, u32[]{:S(2)}, u32[]{:S(2)}) %collective-permute-start.4) | collective-permute-done | bytes 196640 | tf_op jit(solution)/shard_map/ppermute | solution.py:270
  107.9 49.6 %placed.1 = bf16[16,24,2048]{2,1,0:T(8,128)(2,1)} custom-call(s32[4]{0:T(128)} %copy-done.4, bf16[2,24,2048]{2,1,0:T(8,128)(2,1)} %paired.1.refs_0_, bf16[2,24,2048]{2,1,0:T(8,128)(2,1)} %copy-done.11, bf16[2,24,2048]{2,1,0:T(8,128)(2,1)} %copy-done.13, bf16[2,24,2048]{2,1,0:T(8,128)(2,1)} %copy-done.9, bf16[2,24,2048]{2,1,0:T(8,128)(2,1)} %collective-permute-done.4.refs_4_, ...), custom_call_target="tpu_custom_call" | custom-call | tf_op jit(solution)/shard_map/placed/pallas_call | solution.py:276
  159.4 2.4 %half_kept.1 = bf16[384,2048]{1,0:T(8,128)(2,1)} custom-call(bf16[768,256]{1,0:T(8,128)(2,1)S(1)} %get-tuple-element.7.main_t_ref, bf16[768,64]{1,0:T(8,128)(2,1)S(1)} %get-tuple-element.8.extra_t_ref, bf16[256,2560]{1,0:T(8,128)(2,1)S(1)} %bitcast.49, bf16[384,2048]{1,0:T(8,128)(2,1)S(1)} %collective-permute-done.9.refs_0_), custom_call_target="tpu_custom_call" | custom-call | flops 503316480 | bytes 4718592 | tf_op jit(solution)/shard_map/half_kept/pallas_call | solution.py:137
  161.9 10.1 %all-to-all-start.1 = ((bf16[16,24,2048]{2,1,0:T(8,128)(2,1)}), bf16[16,24,2048]{2,1,0:T(8,128)(2,1)S(1)}, u32[]{:S(2)}, u32[]{:S(2)}) async-start(bf16[16,24,2048]{2,1,0:T(8,128)(2,1)} %bitcast.64), calls=%async_computation.1 | async-start | bytes 3145728 | tf_op jit(solution)/shard_map/all_to_all | solution.py:443
  173.4 6.5 %products.1 = (bf16[320,768]{1,0:T(8,128)(2,1)}, f32[32,128]{1,0:T(8,128)S(1)}) custom-call(s32[4]{0:T(128)S(1)} %copy-done.5, bf16[768,256]{1,0:T(8,128)(2,1)S(1)} %get-tuple-element.7.main_t_ref, bf16[768,64]{1,0:T(8,128)(2,1)S(1)} %get-tuple-element.8.extra_t_ref, bf16[384,2048]{1,0:T(8,128)(2,1)S(1)} %bitcast.53, ...), custom_call_target="tpu_custom_call" | custom-call | tf_op jit(solution)/shard_map/products/pallas_call | solution.py:222
  181.8 3.6 %collective-permute-done.10 = f32[16,1,128]{2,0,1:T(8,128)S(1)} collective-permute-done((f32[16,1,128]{2,0,1:T(8,128)S(1)}, f32[16,1,128]{2,0,1:T(8,128)S(1)}, u32[]{:S(2)}, u32[]{:S(2)}) %collective-permute-start.10) | collective-permute-done | bytes 8224 | tf_op jit(solution)/shard_map/ppermute | solution.py:318
  185.5 4.8 %collective-permute-start.11 = (f32[8,2,128]{2,0,1:T(8,128)S(1)}, f32[8,2,128]{2,0,1:T(8,128)S(1)}, u32[]{:S(2)}, u32[]{:S(2)}) collective-permute-start(f32[8,2,128]{2,0,1:T(8,128)S(1)} %bitcast.73), channel_id=1, source_target_pairs={{0,64},{32,96},{64,0},{96,32},{128,192},{160,224},{192,128},{224,1... | collective-permute-start | bytes 24584 | tf_op jit(solution)/shard_map/ppermute | solution.py:318
  191.9 9.2 %collective-permute-start.12 = (f32[4,4,128]{2,0,1:T(4,128)S(1)}, f32[4,4,128]{2,0,1:T(4,128)S(1)}, u32[]{:S(2)}, u32[]{:S(2)}) collective-permute-start(f32[4,4,128]{2,0,1:T(4,128)S(1)} %bitcast.76), channel_id=1, source_target_pairs={{0,128},{32,160},{64,192},{96,224},{128,0},{160,32},{192,64},{224,... | collective-permute-start | bytes 24584 | tf_op jit(solution)/shard_map/ppermute | solution.py:318
  202.8 4.4 %collective-permute-start.13 = (f32[2,8,128]{2,1,0:T(8,128)S(1)}, f32[2,8,128]{2,1,0:T(8,128)S(1)}, u32[]{:S(2)}, u32[]{:S(2)}) collective-permute-start(f32[2,8,128]{2,1,0:T(8,128)S(1)} %get-tuple-element.14), channel_id=1, source_target_pairs={{0,256},{256,0},{512,768},{768,512},{1,257},{257,1},{513,769},{769... | collective-permute-start | bytes 24584 | tf_op jit(solution)/shard_map/ppermute | solution.py:318
  207.3 6.1 %collective-permute-done.13 = f32[2,8,128]{2,1,0:T(8,128)S(1)} collective-permute-done((f32[2,8,128]{2,1,0:T(8,128)S(1)}, f32[2,8,128]{2,1,0:T(8,128)S(1)}, u32[]{:S(2)}, u32[]{:S(2)}) %collective-permute-start.13) | collective-permute-done | bytes 8224 | tf_op jit(solution)/shard_map/ppermute | solution.py:318
  213.4 3.5 %collective-permute-start.14 = (f32[1,16,128]{2,1,0:T(8,128)S(1)}, f32[1,16,128]{2,1,0:T(8,128)S(1)}, u32[]{:S(2)}, u32[]{:S(2)}) collective-permute-start(f32[1,16,128]{2,1,0:T(8,128)S(1)} %get-tuple-element.12), channel_id=1, source_target_pairs={{0,512},{256,768},{512,0},{768,256},{1,513},{257,769},{513,1},{769... | collective-permute-start | bytes 24584 | tf_op jit(solution)/shard_map/ppermute | solution.py:318
  216.9 6.0 %collective-permute-done.14 = f32[1,16,128]{2,1,0:T(8,128)S(1)} collective-permute-done((f32[1,16,128]{2,1,0:T(8,128)S(1)}, f32[1,16,128]{2,1,0:T(8,128)S(1)}, u32[]{:S(2)}, u32[]{:S(2)}) %collective-permute-start.14) | collective-permute-done | bytes 8224 | tf_op jit(solution)/shard_map/ppermute | solution.py:318
  (61 shorter events, 25.7 us)
Async XLA Ops:
  3.6 88.6 %all-to-all-start = ((bf16[32,8,2560]{2,1,0:T(8,128)(2,1)}), bf16[32,8,2560]{2,1,0:T(8,128)(2,1)S(1)}, u32[]{:S(2)}, u32[]{:S(2)}) async-start(bf16[32,8,2560]{2,1,0:T(8,128)(2,1)} %bitcast.11), calls=%async_computation | async-start | bytes 2621440 | tf_op jit(solution)/shard_map/all_to_all | solution.py:416
  23.8 65.3 %copy-start.7 = (bf16[1,1,32,10,768]{4,2,3,1,0:T(8,128)(2,1)S(1)}, bf16[1,1,32,10,768]{4,2,3,1,0:T(8,128)(2,1)}, u32[]{:S(2)}) copy-start(bf16[1,1,32,10,768]{4,2,3,1,0:T(8,128)(2,1)} %param.12) | copy-start | bytes 1474564
  27.9 27.0 %collective-permute-start = (bf16[24,2048]{1,0:T(8,128)(2,1)}, bf16[24,2048]{1,0:T(8,128)(2,1)S(1)}, u32[]{:S(2)}, u32[]{:S(2)}) collective-permute-start(bf16[24,2048]{1,0:T(8,128)(2,1)} %after.1.weights_ref), channel_id=1, source_target_pairs={{0,2},{2,0},{1,3},{3,1},{4,6},{6,4},{5,7},{7,5},{8,10},{10,8},{9,1... | collective-permute-start | bytes 294920 | tf_op jit(solution)/shard_map/ppermute | solution.py:421
  62.6 10.5 %collective-permute-start.5 = (bf16[2,24,2048]{2,1,0:T(8,128)(2,1)}, bf16[2,24,2048]{2,1,0:T(8,128)(2,1)S(1)}, u32[]{:S(2)}, u32[]{:S(2)}) collective-permute-start(bf16[2,24,2048]{2,1,0:T(8,128)(2,1)} %paired.1.refs_0_), channel_id=1, source_target_pairs={{0,4},{4,8},{8,12},{12,16},{16,20},{20,24},{24,28},{28,0},{1,5},{5... | collective-permute-start | bytes 589832 | tf_op jit(solution)/shard_map/ppermute | solution.py:273
  66.3 8.8 %collective-permute-start.1 = (bf16[2,24,2048]{2,1,0:T(8,128)(2,1)}, bf16[2,24,2048]{2,1,0:T(8,128)(2,1)S(1)}, u32[]{:S(2)}, u32[]{:S(2)}) collective-permute-start(bf16[2,24,2048]{2,1,0:T(8,128)(2,1)} %paired.1.refs_0_), channel_id=1, source_target_pairs={{0,28},{4,0},{8,4},{12,8},{16,12},{20,16},{24,20},{28,24},{1,29},{... | collective-permute-start | bytes 589832 | tf_op jit(solution)/shard_map/ppermute | solution.py:270
  73.1 10.7 %copy-start.10 = (bf16[2,24,2048]{2,1,0:T(8,128)(2,1)}, bf16[2,24,2048]{2,1,0:T(8,128)(2,1)S(1)}, u32[]{:S(2)}) copy-start(bf16[2,24,2048]{2,1,0:T(8,128)(2,1)S(1)} %collective-permute-done.5.refs_7_) | copy-start | bytes 589828
  73.2 8.8 %collective-permute-start.6 = (bf16[2,24,2048]{2,1,0:T(8,128)(2,1)S(1)}, bf16[2,24,2048]{2,1,0:T(8,128)(2,1)S(1)}, u32[]{:S(2)}, u32[]{:S(2)}) collective-permute-start(bf16[2,24,2048]{2,1,0:T(8,128)(2,1)S(1)} %collective-permute-done.5.refs_7_), channel_id=1, source_target_pairs={{0,4},{4,8},{8,12},{12,16},{16,20},{20,24},{24,28},{28,0},{1,5},{5... | collective-permute-start | bytes 589832 | tf_op jit(solution)/shard_map/ppermute | solution.py:273
  75.1 8.8 %collective-permute-start.2 = (bf16[2,24,2048]{2,1,0:T(8,128)(2,1)S(1)}, bf16[2,24,2048]{2,1,0:T(8,128)(2,1)S(1)}, u32[]{:S(2)}, u32[]{:S(2)}) collective-permute-start(bf16[2,24,2048]{2,1,0:T(8,128)(2,1)S(1)} %collective-permute-done.1.refs_1_), channel_id=1, source_target_pairs={{0,28},{4,0},{8,4},{12,8},{16,12},{20,16},{24,20},{28,24},{1,29},{... | collective-permute-start | bytes 589832 | tf_op jit(solution)/shard_map/ppermute | solution.py:270
  81.9 10.3 %copy-start.12 = (bf16[2,24,2048]{2,1,0:T(8,128)(2,1)}, bf16[2,24,2048]{2,1,0:T(8,128)(2,1)S(1)}, u32[]{:S(2)}) copy-start(bf16[2,24,2048]{2,1,0:T(8,128)(2,1)S(1)} %collective-permute-done.6.refs_6_) | copy-start | bytes 589828
  81.9 8.8 %collective-permute-start.7 = (bf16[2,24,2048]{2,1,0:T(8,128)(2,1)S(1)}, bf16[2,24,2048]{2,1,0:T(8,128)(2,1)S(1)}, u32[]{:S(2)}, u32[]{:S(2)}) collective-permute-start(bf16[2,24,2048]{2,1,0:T(8,128)(2,1)S(1)} %collective-permute-done.6.refs_6_), channel_id=1, source_target_pairs={{0,4},{4,8},{8,12},{12,16},{16,20},{20,24},{24,28},{28,0},{1,5},{5... | collective-permute-start | bytes 589832 | tf_op jit(solution)/shard_map/ppermute | solution.py:273
  83.9 8.3 %collective-permute-start.3 = (bf16[2,24,2048]{2,1,0:T(8,128)(2,1)S(1)}, bf16[2,24,2048]{2,1,0:T(8,128)(2,1)S(1)}, u32[]{:S(2)}, u32[]{:S(2)}) collective-permute-start(bf16[2,24,2048]{2,1,0:T(8,128)(2,1)S(1)} %collective-permute-done.2.refs_2_), channel_id=1, source_target_pairs={{0,28},{4,0},{8,4},{12,8},{16,12},{20,16},{24,20},{28,24},{1,29},{... | collective-permute-start | bytes 589832 | tf_op jit(solution)/shard_map/ppermute | solution.py:270
  95.3 64.2 %collective-permute-start.9 = (bf16[384,2048]{1,0:T(8,128)(2,1)}, bf16[384,2048]{1,0:T(8,128)(2,1)S(1)}, u32[]{:S(2)}, u32[]{:S(2)}) collective-permute-start(bf16[384,2048]{1,0:T(8,128)(2,1)} %half_sent.1), channel_id=1, source_target_pairs={{0,1},{1,0},{2,3},{3,2},{4,5},{5,4},{6,7},{7,6},{8,9},{9,8},{10,11... | collective-permute-start | bytes 4718600 | tf_op jit(solution)/shard_map/ppermute | solution.py:441
  97.2 10.7 %collective-permute-start.4 = (bf16[2,24,2048]{2,1,0:T(8,128)(2,1)}, bf16[2,24,2048]{2,1,0:T(8,128)(2,1)}, u32[]{:S(2)}, u32[]{:S(2)}) collective-permute-start(bf16[2,24,2048]{2,1,0:T(8,128)(2,1)} %copy-done.9), channel_id=1, source_target_pairs={{0,28},{4,0},{8,4},{12,8},{16,12},{20,16},{24,20},{28,24},{1,29},{... | collective-permute-start | bytes 589832 | tf_op jit(solution)/shard_map/ppermute | solution.py:270
  157.5 14.5 %collective-permute-start.8 = (bf16[384,2048]{1,0:T(8,128)(2,1)}, bf16[384,2048]{1,0:T(8,128)(2,1)}, u32[]{:S(2)}, u32[]{:S(2)}) collective-permute-start(bf16[384,2048]{1,0:T(8,128)(2,1)} %bitcast.52), channel_id=1, source_target_pairs={{0,1},{1,0},{2,3},{3,2},{4,5},{5,4},{6,7},{7,6},{8,9},{9,8},{10,11... | collective-permute-start | bytes 4718600 | tf_op jit(solution)/shard_map/ppermute | solution.py:424
  161.9 62.8 %all-to-all-start.1 = ((bf16[16,24,2048]{2,1,0:T(8,128)(2,1)}), bf16[16,24,2048]{2,1,0:T(8,128)(2,1)S(1)}, u32[]{:S(2)}, u32[]{:S(2)}) async-start(bf16[16,24,2048]{2,1,0:T(8,128)(2,1)} %bitcast.64), calls=%async_computation.1 | async-start | bytes 3145728 | tf_op jit(solution)/shard_map/all_to_all | solution.py:443
  173.4 49.5 %copy-start.1 = (f32[128,8]{0,1:T(8,128)S(1)}, f32[128,8]{0,1:T(8,128)}, u32[]{:S(2)}) copy-start(f32[128,8]{0,1:T(8,128)} %param.8) | copy-start | bytes 12292
  173.4 49.5 %copy-start.2 = (s32[128,8]{0,1:T(8,128)S(1)}, s32[128,8]{0,1:T(8,128)}, u32[]{:S(2)}) copy-start(s32[128,8]{0,1:T(8,128)} %param.9) | copy-start | bytes 12292
  173.4 49.5 %copy-start.3 = (s32[128,8]{0,1:T(8,128)S(1)}, s32[128,8]{0,1:T(8,128)}, u32[]{:S(2)}) copy-start(s32[128,8]{0,1:T(8,128)} %param.10) | copy-start | bytes 12292
  173.4 49.5 %copy-start.6 = (f32[128,8]{0,1:T(8,128)S(1)}, f32[128,8]{0,1:T(8,128)}, u32[]{:S(2)}) copy-start(f32[128,8]{0,1:T(8,128)} %param.11) | copy-start | bytes 12292
  179.9 5.5 %collective-permute-start.10 = (f32[16,1,128]{2,0,1:T(8,128)S(1)}, f32[16,1,128]{2,0,1:T(8,128)S(1)}, u32[]{:S(2)}, u32[]{:S(2)}) collective-permute-start(f32[16,1,128]{2,0,1:T(8,128)S(1)} %bitcast.74), channel_id=1, source_target_pairs={{0,32},{32,0},{64,96},{96,64},{128,160},{160,128},{192,224},{224,1... | collective-permute-start | bytes 24584 | tf_op jit(solution)/shard_map/ppermute | solution.py:318
  185.5 6.4 %collective-permute-start.11 = (f32[8,2,128]{2,0,1:T(8,128)S(1)}, f32[8,2,128]{2,0,1:T(8,128)S(1)}, u32[]{:S(2)}, u32[]{:S(2)}) collective-permute-start(f32[8,2,128]{2,0,1:T(8,128)S(1)} %bitcast.73), channel_id=1, source_target_pairs={{0,64},{32,96},{64,0},{96,32},{128,192},{160,224},{192,128},{224,1... | collective-permute-start | bytes 24584 | tf_op jit(solution)/shard_map/ppermute | solution.py:318
  191.9 10.9 %collective-permute-start.12 = (f32[4,4,128]{2,0,1:T(4,128)S(1)}, f32[4,4,128]{2,0,1:T(4,128)S(1)}, u32[]{:S(2)}, u32[]{:S(2)}) collective-permute-start(f32[4,4,128]{2,0,1:T(4,128)S(1)} %bitcast.76), channel_id=1, source_target_pairs={{0,128},{32,160},{64,192},{96,224},{128,0},{160,32},{192,64},{224,... | collective-permute-start | bytes 24584 | tf_op jit(solution)/shard_map/ppermute | solution.py:318
  202.8 10.6 %collective-permute-start.13 = (f32[2,8,128]{2,1,0:T(8,128)S(1)}, f32[2,8,128]{2,1,0:T(8,128)S(1)}, u32[]{:S(2)}, u32[]{:S(2)}) collective-permute-start(f32[2,8,128]{2,1,0:T(8,128)S(1)} %get-tuple-element.14), channel_id=1, source_target_pairs={{0,256},{256,0},{512,768},{768,512},{1,257},{257,1},{513,769},{769... | collective-permute-start | bytes 24584 | tf_op jit(solution)/shard_map/ppermute | solution.py:318
  213.4 9.4 %collective-permute-start.14 = (f32[1,16,128]{2,1,0:T(8,128)S(1)}, f32[1,16,128]{2,1,0:T(8,128)S(1)}, u32[]{:S(2)}, u32[]{:S(2)}) collective-permute-start(f32[1,16,128]{2,1,0:T(8,128)S(1)} %get-tuple-element.12), channel_id=1, source_target_pairs={{0,512},{256,768},{512,0},{768,256},{1,513},{257,769},{513,1},{769... | collective-permute-start | bytes 24584 | tf_op jit(solution)/shard_map/ppermute | solution.py:318
  (8 other events, 37.7 us)

commit v4 on v3

--- a/solution.py
+++ b/solution.py
@@ -17,6 +17,7 @@
 BF16 = jnp.bfloat16
 VMEM = pl.BlockSpec(memory_space=pltpu.VMEM)
 HBM = pl.BlockSpec(memory_space=pltpu.HBM)
+ANY = pl.BlockSpec(memory_space=pl.ANY)
 SMEM = pl.BlockSpec(memory_space=pltpu.SMEM)
 PARAMS = pltpu.CompilerParams(vmem_limit_bytes=48 * 1024 * 1024)
 
@@ -42,21 +43,21 @@
     return raised / jnp.sum(raised, axis=0, keepdims=True)
 
 
-def pack_kernel(logits_in, chosen_in, slots_in, rows_in, out_ref, *scratch):
-    held, sems = scratch[:4], scratch[4]
+def place_kernel(logits_in, chosen_in, slots_in, place_ref, fold_ref, *scratch):
+    held, sems = scratch[:3], scratch[3]
     copies = [
         pltpu.make_async_copy(src, dst, sems.at[k])
-        for k, (src, dst) in enumerate(zip((logits_in, chosen_in, slots_in, rows_in), held))
+        for k, (src, dst) in enumerate(zip((logits_in, chosen_in, slots_in), held))
     ]
     for copy in copies:
         copy.start()
     for copy in copies:
         copy.wait()
-    logits_ref, chosen_ref, slots_ref, rows_ref = held
+    logits_ref, chosen_ref, slots_ref = held
     gate = softmax_rows(logits_ref[...]).astype(BF16).astype(F32)
     chosen, slots = chosen_ref[...], slots_ref[...]
     topk, tokens = chosen.shape
-    rows = out_ref.shape[0]
+    rows = place_ref.shape[0]
     main = jnp.where(slots < 8, chosen * 8 + slots, -1)
     extra = jnp.where((slots >= 8) & (slots < 10), chosen * 2 + slots - 8, -1)
     row = iota((rows, tokens), 0)
@@ -65,7 +66,17 @@
     for k in range(topk):
         place = jnp.where(row == main[k : k + 1, :], gate[k : k + 1, :], place)
         fold = jnp.where(row // FOLD == extra[k : k + 1, :], gate[k : k + 1, :], fold)
-    place = place.astype(BF16)
+    place_ref[...] = place.astype(BF16)
+    fold_ref[...] = fold.astype(BF16)
+
+
+def pack_kernel(place_ref, fold_ref, rows_in, first_in, out_ref, rows_ref, sem):
+    copy = pltpu.make_async_copy(rows_in, rows_ref, sem)
+    copy.start()
+    copy.wait()
+    place, fold = place_ref[...], fold_ref[...].astype(F32)
+    rows, tokens = place.shape
+    row = iota((rows, tokens), 0)
     width = rows_ref.shape[1]
     part = width // FOLD
     total = jnp.zeros((rows, part), F32)
@@ -136,70 +147,78 @@
     width = payload.shape[1] * FOLD // (FOLD + 1)
     return pl.pallas_call(
         functools.partial(half_kernel, half, bool(given)),
-        in_specs=[VMEM] * (3 + len(given)) + [HBM] * len(first),
+        in_specs=[VMEM] * (3 + len(given)) + [ANY] * len(first),
         out_specs=HBM,
         out_shape=pltpu.HBM((units // 2, width), BF16),
         scratch_shapes=[pltpu.VMEM((units // 2, width), BF16), pltpu.SemaphoreType.DMA((FOLD,))],
         compiler_params=PARAMS,
         cost_estimate=cost(units * (rows + few) * width, 3 * units * width),
         name="half_kept" if given else "half_sent",
-    )(main_t, extra_t, payload, *given, *map(in_hbm, first))
-
-
-def product_kernel(
-    shard,
-    place_ref,
-    main_t_ref,
-    extra_t_ref,
-    own_ref,
-    other_ref,
-    rows_ref,
-    fold_ref,
-    grad_ref,
-    score_ref,
-    acc_main,
-    acc_extra,
-):
-    g = pl.program_id(0)
-    units, rows = main_t_ref.shape
-    few = extra_t_ref.shape[1]
-    half = units // 2
+    )(main_t, extra_t, payload, *given, *first)
+
+
+def product_kernel(half, place_ref, main_t_ref, extra_t_ref, weights_ref, payload_ref, *refs):
+    *given, main_ref, extra_ref, score_ref = refs
+    units, rows = main_ref.shape
+    few = extra_ref.shape[1]
     source = rows // 8
-
-    @pl.when(g == 0)
-    def _():
-        acc_main[...] = jnp.zeros_like(acc_main)
-        acc_extra[...] = jnp.zeros_like(acc_extra)
-
-    block = rows_ref[...]
-    more = unfolded(fold_ref[...], g)
-    for h, weight in enumerate((own_ref[...], other_ref[...])):
-        span = slice(h * half, (h + 1) * half)
-        acc_main[span, :] += dot(weight, block, 1, 1)
-        acc_extra[span, :] += dot(weight, more, 1, 1)
-
-    @pl.when(g == FOLD - 1)
-    def _():
-        main, extra = acc_main[...], acc_extra[...]
-        main_score = jnp.sum(main * main_t_ref[...].astype(F32), axis=0, keepdims=True)
-        extra_score = jnp.sum(extra * extra_t_ref[...].astype(F32), axis=0, keepdims=True)
-        to_main = (iota((source, rows), 0) ^ place_ref[1]) == iota((source, rows), 1) // 8
-        at_main = iota((rows, 128), 0) % 8 == iota((rows, 128), 1)
-        to_extra = (iota((source, few), 0) ^ place_ref[1]) == iota((source, few), 1) % source
-        at_extra = iota((few, 128), 0) // source + 8 == iota((few, 128), 1)
-        score_ref[...] = exact_dot(
-            jnp.where(to_main, main_score, 0.0), jnp.where(at_main, 1.0, 0.0)
-        ) + exact_dot(jnp.where(to_extra, extra_score, 0.0), jnp.where(at_extra, 1.0, 0.0))
-        to_unit = permuted_units(place_ref[0], units, shard)
-        column = onehot(iota((units, units), 0) == to_unit)
-        here = iota((rows, rows), 0)
-        there = iota((rows, rows), 1)
-        turn = onehot(there == (here % source) * 8 + here // source)
-        keep = onehot(iota((few, few), 0) == iota((few, few), 1))
-        main = dot(column, main.astype(BF16)).astype(BF16)
-        extra = dot(column, extra.astype(BF16)).astype(BF16)
-        grad_ref[:rows, :] = dot(turn, main, 1, 1).astype(BF16)
-        grad_ref[rows:, :] = dot(keep, extra, 1, 1).astype(BF16)
+    width = weights_ref.shape[1]
+    part = width // FOLD
+    weights = weights_ref[...]
+    fold = payload_ref[:, width:]
+    main = dot(weights, payload_ref[:, :width], 1, 1)
+    extra = jnp.zeros((units, few), F32)
+    for m in range(FOLD):
+        extra = extra + dot(weights[:, m * part : (m + 1) * part], unfolded(fold, m), 1, 1)
+    main_ref[...] = main.astype(BF16)
+    extra_ref[...] = extra.astype(BF16)
+    span = slice(half * units, (half + 1) * units)
+    main_score = jnp.sum(main * main_t_ref[span, :].astype(F32), axis=0, keepdims=True)
+    extra_score = jnp.sum(extra * extra_t_ref[span, :].astype(F32), axis=0, keepdims=True)
+    to_main = (iota((source, rows), 0) ^ place_ref[1]) == iota((source, rows), 1) // 8
+    at_main = iota((rows, 128), 0) % 8 == iota((rows, 128), 1)
+    to_extra = (iota((source, few), 0) ^ place_ref[1]) == iota((source, few), 1) % source
+    at_extra = iota((few, 128), 0) // source + 8 == iota((few, 128), 1)
+    score = exact_dot(jnp.where(to_main, main_score, 0.0), jnp.where(at_main, 1.0, 0.0))
+    score = score + exact_dot(jnp.where(to_extra, extra_score, 0.0), jnp.where(at_extra, 1.0, 0.0))
+    if given:
+        score = score + given[0][...]
+    score_ref[...] = score
+
+
+def half_product(place, main_t, extra_t, weights, payload, half, *given):
+    units, rows = main_t.shape
+    few = extra_t.shape[1]
+    return pl.pallas_call(
+        functools.partial(product_kernel, half),
+        in_specs=[SMEM] + [VMEM] * (4 + len(given)),
+        out_specs=[VMEM] * 3,
+        out_shape=[
+            jax.ShapeDtypeStruct((units // 2, rows), BF16),
+            jax.ShapeDtypeStruct((units // 2, few), BF16),
+            jax.ShapeDtypeStruct((rows // 8, 128), F32),
+        ],
+        compiler_params=PARAMS,
+        cost_estimate=cost(units * (rows + few) * weights.shape[1], 0),
+        name="product_of_other" if half else "product_of_own",
+    )(place, main_t, extra_t, weights, payload, *given)
+
+
+def order_kernel(shard, place_ref, own_main, own_extra, other_main, other_extra, grad_ref):
+    half, rows = own_main.shape
+    few = own_extra.shape[1]
+    units = 2 * half
+    source = rows // 8
+    to_unit = permuted_units(place_ref[0], units, shard)
+    column = onehot(iota((units, units), 0) == to_unit)
+    here = iota((rows, rows), 0)
+    turn = onehot(iota((rows, rows), 1) == (here % source) * 8 + here // source)
+    keep = onehot(iota((few, few), 0) == iota((few, few), 1))
+    own, other = column[:, :half], column[:, half:]
+    main = (dot(own, own_main[...]) + dot(other, other_main[...])).astype(BF16)
+    extra = (dot(own, own_extra[...]) + dot(other, other_extra[...])).astype(BF16)
+    grad_ref[:rows, :] = dot(turn, main, 1, 1).astype(BF16)
+    grad_ref[rows:, :] = dot(keep, extra, 1, 1).astype(BF16)
 
 
 def exact_dot(a, b, ca=1, cb=0):
@@ -212,52 +231,13 @@
     )
 
 
-def products(place, shard, main_t, extra_t, own, other, payload):
-    units, rows = main_t.shape
-    few = extra_t.shape[1]
-    width = payload.shape[1] * FOLD // (FOLD + 1)
-    part = width // FOLD
-    fixed = lambda g: (0, 0)
-    moving = lambda g: (0, g)
-    return pl.pallas_call(
-        functools.partial(product_kernel, shard),
-        grid=(FOLD,),
-        in_specs=[
-            SMEM,
-            pl.BlockSpec((units, rows), fixed),
-            pl.BlockSpec((units, few), fixed),
-            pl.BlockSpec((units // 2, part), moving),
-            pl.BlockSpec((units // 2, part), moving),
-            pl.BlockSpec((rows, part), moving),
-            pl.BlockSpec((rows, part), lambda g: (0, FOLD)),
-        ],
-        out_specs=[
-            pl.BlockSpec((rows + few, units), fixed),
-            pl.BlockSpec((rows // 8, 128), fixed),
-        ],
-        out_shape=[
-            jax.ShapeDtypeStruct((rows + few, units), BF16),
-            jax.ShapeDtypeStruct((rows // 8, 128), F32),
-        ],
-        scratch_shapes=[pltpu.VMEM((units, rows), F32), pltpu.VMEM((units, few), F32)],
-        compiler_params=PARAMS,
-        cost_estimate=cost(0, 0),
-        name="products",
-    )(place, main_t, extra_t, own, other, payload, payload)
-
-
 def placed_kernel(place_ref, *refs):
-    *pieces, out_ref, sems = refs
+    *pieces, out_ref = refs
     count = len(pieces)
-    copies = []
     for k, piece in enumerate(pieces):
         base = lax.rem(place_ref[2] + k, count) * 2
         for t in range(2):
-            spot = base + (place_ref[3] ^ t)
-            copies.append(pltpu.make_async_copy(piece.at[t], out_ref.at[spot], sems.at[2 * k + t]))
-            copies[-1].start()
-    for copy in copies:
-        copy.wait()
+            out_ref[base + (place_ref[3] ^ t)] = piece[t]
 
 
 def gathered(place, pair):
@@ -272,39 +252,33 @@
         if k < size - k:
             below = lax.ppermute(below, "y", up)
             pieces[size - k] = below
-    shape = (2 * size, *pair.shape[1:])
-    return pl.pallas_call(
+    placed = pl.pallas_call(
         placed_kernel,
-        in_specs=[SMEM] + [HBM] * size,
-        out_specs=HBM,
-        out_shape=pltpu.HBM(shape, pair.dtype),
-        scratch_shapes=[pltpu.SemaphoreType.DMA((2 * size,))],
+        in_specs=[SMEM] + [VMEM] * size,
+        out_specs=VMEM,
+        out_shape=jax.ShapeDtypeStruct((2 * size, *pair.shape[1:]), pair.dtype),
+        compiler_params=PARAMS,
         cost_estimate=cost(0, 0),
         name="placed",
-    )(place, *pieces), pieces
-
-
-def pair_kernel(weights_ref, beside_ref, out_ref, sems):
-    copies = [
-        pltpu.make_async_copy(src, out_ref.at[k], sems.at[k])
-        for k, src in enumerate((weights_ref, beside_ref))
-    ]
-    for copy in copies:
-        copy.start()
-    for copy in copies:
-        copy.wait()
-
-
-def paired(weights, beside):
+    )(place, *pieces)
+    return placed, pieces
+
+
+def pair_kernel(weights_ref, beside_ref, first_ref, out_ref):
+    out_ref[0] = weights_ref[...]
+    out_ref[1] = beside_ref[...]
+
+
+def paired(weights, beside, first):
     return pl.pallas_call(
         pair_kernel,
-        in_specs=[HBM] * 2,
-        out_specs=HBM,
-        out_shape=pltpu.HBM((2, *weights.shape), weights.dtype),
-        scratch_shapes=[pltpu.SemaphoreType.DMA((2,))],
+        in_specs=[VMEM, VMEM, ANY],
+        out_specs=VMEM,
+        out_shape=jax.ShapeDtypeStruct((2, *weights.shape), weights.dtype),
+        compiler_params=PARAMS,
         cost_estimate=cost(0, 0),
         name="paired",
-    )(weights, beside)
+    )(weights, beside, first)
 
 
 def exchanged_by_bits(blocks):
@@ -323,24 +297,6 @@
 
 def in_hbm(array):
     return pltpu.with_memory_space_constraint(array, pltpu.HBM)
-
-
-def after_kernel(array_ref, first_ref, out_ref, sem):
-    copy = pltpu.make_async_copy(array_ref, out_ref, sem)
-    copy.start()
-    copy.wait()
-
-
-def after(array, first):
-    return pl.pallas_call(
-        after_kernel,
-        in_specs=[HBM, HBM],
-        out_specs=HBM,
-        out_shape=pltpu.HBM(array.shape, array.dtype),
-        scratch_shapes=[pltpu.SemaphoreType.DMA],
-        cost_estimate=cost(0, 0),
-        name="after",
-    )(array, first)
 
 
 def sum_kernel(pieces_ref, out_ref):
@@ -397,29 +353,39 @@
     logits_t, chosen_t, slots_t = logits.T, chosen.T, slots.T
     swap = [(0, 1), (1, 0)]
 
-    packed = pl.pallas_call(
-        pack_kernel,
-        in_specs=[HBM] * 4,
-        out_specs=VMEM,
-        out_shape=jax.ShapeDtypeStruct((window * 8, model + model // FOLD), BF16),
+    weights = down_weight.reshape(shard, model)
+    beside = lax.ppermute(weights, "zl", swap)
+    tile = jax.ShapeDtypeStruct((window * 8, tokens), BF16)
+    placing = pl.pallas_call(
+        place_kernel,
+        in_specs=[HBM] * 3,
+        out_specs=[VMEM] * 2,
+        out_shape=[tile, tile],
         scratch_shapes=[
             pltpu.VMEM((topk, tokens), F32),
             pltpu.VMEM((topk, tokens), jnp.int32),
             pltpu.VMEM((topk, tokens), jnp.int32),
-            pltpu.VMEM((tokens, model), BF16),
-            pltpu.SemaphoreType.DMA((4,)),
+            pltpu.SemaphoreType.DMA((3,)),
         ],
+        compiler_params=PARAMS,
+        cost_estimate=cost(0, 4 * 320 * model),
+        name="placing",
+    )(*map(in_hbm, (logits_t, chosen_t, slots_t)))
+    packed = pl.pallas_call(
+        pack_kernel,
+        in_specs=[VMEM, VMEM, HBM, ANY],
+        out_specs=VMEM,
+        out_shape=jax.ShapeDtypeStruct((window * 8, model + model // FOLD), BF16),
+        scratch_shapes=[pltpu.VMEM((tokens, model), BF16), pltpu.SemaphoreType.DMA],
         compiler_params=PARAMS,
         cost_estimate=cost(2 * 320 * tokens * model * 2, 4 * 320 * model),
         name="pack",
-    )(*map(in_hbm, (logits_t, chosen_t, slots_t, grad_output)))
+    )(*placing, in_hbm(grad_output), beside)
     payload = lax.all_to_all(
         packed.reshape(window, 8, packed.shape[1]), EXPERT, split_axis=0, concat_axis=0, tiled=True
     ).reshape(packed.shape)
 
-    weights = after(down_weight.reshape(shard, model), packed)
-    beside = lax.ppermute(weights, "zl", swap)
-    own_weights, pieces = gathered(place, paired(weights, beside))
+    own_weights, pieces = gathered(place, paired(weights, beside, packed))
     own_weights = own_weights.reshape(-1, model)
     other_weights = lax.ppermute(own_weights, "core", swap)
 
@@ -440,14 +406,24 @@
     sent = half_partial(main_t, extra_t, payload, 1, first=(pieces[3], pieces[-3]))
     arrived = lax.ppermute(sent, "core", swap)
     both = half_partial(main_t, extra_t, payload, 0, arrived)
-    pieces = lax.all_to_all(
+    parts = lax.all_to_all(
         both.reshape(-1, shard, model), RING, split_axis=0, concat_axis=0, tiled=True
     )
-    grad_down = summed(pieces).reshape(1, shard, model)
-
-    grad, score = products(place, shard, main_t, extra_t, own_weights, other_weights, payload)
+    grad_down = summed(parts).reshape(1, shard, model)
+
+    *own_grad, score = half_product(place, main_t, extra_t, own_weights, payload, 0)
+    *other_grad, score = half_product(place, main_t, extra_t, other_weights, payload, 1, score)
+    returned = exchanged_by_bits(score)
+    grad = pl.pallas_call(
+        functools.partial(order_kernel, shard),
+        in_specs=[SMEM] + [VMEM] * 4,
+        out_specs=VMEM,
+        out_shape=jax.ShapeDtypeStruct((capacity * window, units), BF16),
+        compiler_params=PARAMS,
+        cost_estimate=cost(2 * 320 * units * units, 4 * 320 * units),
+        name="order",
+    )(place, *own_grad, *other_grad)
     grad_hidden = grad.reshape(1, 1, capacity, window, units).transpose(0, 1, 3, 2, 4)
-    returned = exchanged_by_bits(score)
     grad_logits = pl.pallas_call(
         logits_kernel,
         in_specs=[SMEM] + [VMEM] * 5,

time: 227 us -> 147 us (0.65)
  the two profiles are of different devices: /device:TPU:128 before, /device:TPU:130 now
where the time goes in v4:
time: 147 us; the launch traced here: 146 us
  starting transfers between devices  78.3 us (53%)
  waiting for transfers between devices  40.1 us (27%)
  Pallas kernels  25.1 us (17%)
  local copies, waits for them, and re-layouts  1.79 us (1%)
    ppermute x4, starting transfers between devices, gathered(): above = lax.ppermute(above, 'y', down)  23.5 us
    ppermute x5, waiting for transfers between devices, exchanged_by_bits(): came = lax.ppermute(pairs[:, 1], axis, [(i, i ^ step) for i in range(size)])  22.5 us
    all_to_all x1, starting transfers between devices, body(): lax.all_to_all(packed.reshape(window, 8, packed.shape[1]), EXPERT, split_...  20.6 us
    ppermute x5, starting transfers between devices, exchanged_by_bits(): came = lax.ppermute(pairs[:, 1], axis, [(i, i ^ step) for i in range(size)])  15.4 us
    pallas_call x2, Pallas kernels, half_product(): pl.pallas_call(functools.partial(product_kernel, half), in_specs=[SMEM] +...  7.38 us
    all_to_all x1, starting transfers between devices, body(): lax.all_to_all(both.reshape(-1, shard, model), RING, split_axis=0, concat...  7.26 us
    ppermute x4, waiting for transfers between devices, gathered(): above = lax.ppermute(above, 'y', down)  6.59 us
    ppermute x3, starting transfers between devices, gathered(): below = lax.ppermute(below, 'y', up)  5.75 us
  transfers between devices with their start and end apart: 17, of which 11 were waited for; matrix products, arithmetic and copies ran while one was open for 0% of the time, Pallas kernels for 13%

profile of v4, /device:TPU:130, one launch (start us, length us, event | category | flops | bytes accessed | tf_op | source)
XLA Modules:
  0.0 146.3 jit_solution(7353572222899052921)
XLA Ops:
  3.5 3.8 %collective-permute-done.first_in.beside_ref = bf16[24,2048]{1,0:T(8,128)(2,1)S(1)} collective-permute-done((bf16[24,2048]{1,0:T(8,128)(2,1)}, bf16[24,2048]{1,0:T(8,128)(2,1)S(1)}, u32[]{:S(2)}, u32[]{:S(2)}) %collective-permute-start) | collective-permute-done | bytes 98336 | tf_op jit(solution)/shard_map/ppermute | solution.py:357
  7.4 2.8 %pack.1.first_ref = bf16[256,2560]{1,0:T(8,128)(2,1)} custom-call(bf16[256,128]{1,0:T(8,128)(2,1)S(1)} %get-tuple-element.15.place_ref, bf16[256,128]{1,0:T(8,128)(2,1)S(1)} %get-tuple-element.16.fold_ref, bf16[128,2048]{1,0:T(8,128)(2,1)} %rows_in.1, bf16[24,2048]{1,0:T(8,128)(2,1)S(1)} %collective-permute-done.first_in.beside_ref), custom_call_target="tpu_custom_call" | custom-call | flops 335544320 | bytes 2621440 | tf_op jit(solution)/shard_map/pack/pallas_call | solution.py:374
  10.2 20.6 %all-to-all-start = ((bf16[32,8,2560]{2,1,0:T(8,128)(2,1)}), bf16[32,8,2560]{2,1,0:T(8,128)(2,1)S(1)}, u32[]{:S(2)}, u32[]{:S(2)}) async-start(bf16[32,8,2560]{2,1,0:T(8,128)(2,1)} %bitcast.11), calls=%async_computation | async-start | bytes 2621440 | tf_op jit(solution)/shard_map/all_to_all | solution.py:384
  30.8 6.2 %collective-permute-start.1 = (bf16[2,24,2048]{2,1,0:T(8,128)(2,1)S(1)}, bf16[2,24,2048]{2,1,0:T(8,128)(2,1)S(1)}, u32[]{:S(2)}, u32[]{:S(2)}) collective-permute-start(bf16[2,24,2048]{2,1,0:T(8,128)(2,1)S(1)} %paired.1.refs_0_), channel_id=1, source_target_pairs={{0,28},{4,0},{8,4},{12,8},{16,12},{20,16},{24,20},{28,24},{1,29},{... | collective-permute-start | bytes 589832 | tf_op jit(solution)/shard_map/ppermute | solution.py:250
  40.2 5.6 %collective-permute-start.2 = (bf16[2,24,2048]{2,1,0:T(8,128)(2,1)S(1)}, bf16[2,24,2048]{2,1,0:T(8,128)(2,1)S(1)}, u32[]{:S(2)}, u32[]{:S(2)}) collective-permute-start(bf16[2,24,2048]{2,1,0:T(8,128)(2,1)S(1)} %collective-permute-done.1.refs_1_), channel_id=1, source_target_pairs={{0,28},{4,0},{8,4},{12,8},{16,12},{20,16},{24,20},{28,24},{1,29},{... | collective-permute-start | bytes 589832 | tf_op jit(solution)/shard_map/ppermute | solution.py:250
  49.0 5.6 %collective-permute-start.3 = (bf16[2,24,2048]{2,1,0:T(8,128)(2,1)S(1)}, bf16[2,24,2048]{2,1,0:T(8,128)(2,1)S(1)}, u32[]{:S(2)}, u32[]{:S(2)}) collective-permute-start(bf16[2,24,2048]{2,1,0:T(8,128)(2,1)S(1)} %collective-permute-done.2.refs_2_), channel_id=1, source_target_pairs={{0,28},{4,0},{8,4},{12,8},{16,12},{20,16},{24,20},{28,24},{1,29},{... | collective-permute-start | bytes 589832 | tf_op jit(solution)/shard_map/ppermute | solution.py:250
  59.1 4.2 %collective-permute-done.7.refs_5_.refs_1_ = bf16[2,24,2048]{2,1,0:T(8,128)(2,1)S(1)} collective-permute-done((bf16[2,24,2048]{2,1,0:T(8,128)(2,1)S(1)}, bf16[2,24,2048]{2,1,0:T(8,128)(2,1)S(1)}, u32[]{:S(2)}, u32[]{:S(2)}) %collective-permute-start.7) | collective-permute-done | bytes 196640 | tf_op jit(solution)/shard_map/ppermute | solution.py:253
  63.3 3.0 %all-to-all-done = bf16[32,8,2560]{2,1,0:T(8,128)(2,1)S(1)} async-done(((bf16[32,8,2560]{2,1,0:T(8,128)(2,1)}), bf16[32,8,2560]{2,1,0:T(8,128)(2,1)S(1)}, u32[]{:S(2)}, u32[]{:S(2)}) %all-to-all-start) | async-done | bytes 1310752 | tf_op jit(solution)/shard_map/all_to_all | solution.py:384
  70.6 6.2 %collective-permute-start.4 = (bf16[2,24,2048]{2,1,0:T(8,128)(2,1)S(1)}, bf16[2,24,2048]{2,1,0:T(8,128)(2,1)S(1)}, u32[]{:S(2)}, u32[]{:S(2)}) collective-permute-start(bf16[2,24,2048]{2,1,0:T(8,128)(2,1)S(1)} %collective-permute-done.3.refs_3_.refs_0_), channel_id=1, source_target_pairs={{0,28},{4,0},{8,4},{12,8},{16,12},{20,16},{24,20},{28,24},{1,29},{... | collective-permute-start | bytes 589832 | tf_op jit(solution)/shard_map/ppermute | solution.py:250
  76.8 4.8 %collective-permute-done.4.refs_4_ = bf16[2,24,2048]{2,1,0:T(8,128)(2,1)S(1)} collective-permute-done((bf16[2,24,2048]{2,1,0:T(8,128)(2,1)S(1)}, bf16[2,24,2048]{2,1,0:T(8,128)(2,1)S(1)}, u32[]{:S(2)}, u32[]{:S(2)}) %collective-permute-start.4) | collective-permute-done | bytes 196640 | tf_op jit(solution)/shard_map/ppermute | solution.py:250
  85.3 2.4 %half_kept.1 = bf16[384,2048]{1,0:T(8,128)(2,1)} custom-call(bf16[768,256]{1,0:T(8,128)(2,1)S(1)} %get-tuple-element.13.main_t_ref, bf16[768,64]{1,0:T(8,128)(2,1)S(1)} %get-tuple-element.14.extra_t_ref, bf16[256,2560]{1,0:T(8,128)(2,1)S(1)} %bitcast.49, bf16[384,2048]{1,0:T(8,128)(2,1)S(1)} %collective-permute-done.9.refs_0_), custom_call_target="tpu_custom_call" | custom-call | flops 503316480 | bytes 4718592 | tf_op jit(solution)/shard_map/half_kept/pallas_call | solution.py:148
  87.7 7.3 %all-to-all-start.1 = ((bf16[16,24,2048]{2,1,0:T(8,128)(2,1)}), bf16[16,24,2048]{2,1,0:T(8,128)(2,1)S(1)}, u32[]{:S(2)}, u32[]{:S(2)}) async-start(bf16[16,24,2048]{2,1,0:T(8,128)(2,1)} %bitcast.64), calls=%async_computation.1 | async-start | bytes 3145728 | tf_op jit(solution)/shard_map/all_to_all | solution.py:409
  95.0 3.7 %product_of_own.1 = (bf16[384,256]{1,0:T(8,128)(2,1)S(1)}, bf16[384,64]{1,0:T(8,128)(2,1)S(1)}, f32[32,128]{1,0:T(8,128)S(1)}) custom-call(s32[4]{0:T(128)S(1)} %pad_add_fusion.place_ref, bf16[768,256]{1,0:T(8,128)(2,1)S(1)} %get-tuple-element.13.main_t_ref, bf16[768,64]{1,0:T(8,128)(2,1)S(1)} %get-tuple-element.14.extra_t_ref, ...), custom_call_target="tpu_custom_call" | custom-call | flops 503316480 | tf_op jit(solution)/shard_map/product_of_own/pallas_call | solution.py:192
  98.7 3.7 %product_of_other.1 = (bf16[384,256]{1,0:T(8,128)(2,1)S(1)}, bf16[384,64]{1,0:T(8,128)(2,1)S(1)}, f32[32,128]{1,0:T(8,128)S(1)}) custom-call(s32[4]{0:T(128)S(1)} %pad_add_fusion.place_ref, bf16[768,256]{1,0:T(8,128)(2,1)S(1)} %get-tuple-element.13.main_t_ref, bf16[768,64]{1,0:T(8,128)(2,1)S(1)} %get-tuple-element.14.extra_t_ref, ...), custom_call_target="tpu_custom_call" | custom-call | flops 503316480 | tf_op jit(solution)/shard_map/product_of_other/pallas_call | solution.py:192
  104.4 3.6 %collective-permute-done.10 = f32[16,1,128]{2,0,1:T(8,128)S(1)} collective-permute-done((f32[16,1,128]{2,0,1:T(8,128)S(1)}, f32[16,1,128]{2,0,1:T(8,128)S(1)}, u32[]{:S(2)}, u32[]{:S(2)}) %collective-permute-start.10) | collective-permute-done | bytes 8224 | tf_op jit(solution)/shard_map/ppermute | solution.py:292
  108.0 3.4 %collective-permute-start.11 = (f32[8,2,128]{2,0,1:T(8,128)S(1)}, f32[8,2,128]{2,0,1:T(8,128)S(1)}, u32[]{:S(2)}, u32[]{:S(2)}) collective-permute-start(f32[8,2,128]{2,0,1:T(8,128)S(1)} %bitcast.73), channel_id=1, source_target_pairs={{0,64},{32,96},{64,0},{96,32},{128,192},{160,224},{192,128},{224,1... | collective-permute-start | bytes 24584 | tf_op jit(solution)/shard_map/ppermute | solution.py:292
  111.4 3.1 %collective-permute-done.11 = f32[8,2,128]{2,0,1:T(8,128)S(1)} collective-permute-done((f32[8,2,128]{2,0,1:T(8,128)S(1)}, f32[8,2,128]{2,0,1:T(8,128)S(1)}, u32[]{:S(2)}, u32[]{:S(2)}) %collective-permute-start.11) | collective-permute-done | bytes 8224 | tf_op jit(solution)/shard_map/ppermute | solution.py:292
  114.5 3.5 %collective-permute-start.12 = (f32[4,4,128]{2,0,1:T(4,128)S(1)}, f32[4,4,128]{2,0,1:T(4,128)S(1)}, u32[]{:S(2)}, u32[]{:S(2)}) collective-permute-start(f32[4,4,128]{2,0,1:T(4,128)S(1)} %bitcast.76), channel_id=1, source_target_pairs={{0,128},{32,160},{64,192},{96,224},{128,0},{160,32},{192,64},{224,... | collective-permute-start | bytes 24584 | tf_op jit(solution)/shard_map/ppermute | solution.py:292
  118.0 5.9 %collective-permute-done.12 = f32[4,4,128]{2,0,1:T(4,128)S(1)} collective-permute-done((f32[4,4,128]{2,0,1:T(4,128)S(1)}, f32[4,4,128]{2,0,1:T(4,128)S(1)}, u32[]{:S(2)}, u32[]{:S(2)}) %collective-permute-start.12) | collective-permute-done | bytes 8224 | tf_op jit(solution)/shard_map/ppermute | solution.py:292
  124.0 3.0 %collective-permute-start.13 = (f32[2,8,128]{2,1,0:T(8,128)S(1)}, f32[2,8,128]{2,1,0:T(8,128)S(1)}, u32[]{:S(2)}, u32[]{:S(2)}) collective-permute-start(f32[2,8,128]{2,1,0:T(8,128)S(1)} %get-tuple-element.26), channel_id=1, source_target_pairs={{0,256},{256,0},{512,768},{768,512},{1,257},{257,1},{513,769},{769... | collective-permute-start | bytes 24584 | tf_op jit(solution)/shard_map/ppermute | solution.py:292
  127.0 6.5 %collective-permute-done.13 = f32[2,8,128]{2,1,0:T(8,128)S(1)} collective-permute-done((f32[2,8,128]{2,1,0:T(8,128)S(1)}, f32[2,8,128]{2,1,0:T(8,128)S(1)}, u32[]{:S(2)}, u32[]{:S(2)}) %collective-permute-start.13) | collective-permute-done | bytes 8224 | tf_op jit(solution)/shard_map/ppermute | solution.py:292
  133.6 3.6 %collective-permute-start.14 = (f32[1,16,128]{2,1,0:T(8,128)S(1)}, f32[1,16,128]{2,1,0:T(8,128)S(1)}, u32[]{:S(2)}, u32[]{:S(2)}) collective-permute-start(f32[1,16,128]{2,1,0:T(8,128)S(1)} %get-tuple-element.24), channel_id=1, source_target_pairs={{0,512},{256,768},{512,0},{768,256},{1,513},{257,769},{513,1},{769... | collective-permute-start | bytes 24584 | tf_op jit(solution)/shard_map/ppermute | solution.py:292
  137.1 2.5 %order.1 = bf16[320,768]{1,0:T(8,128)(2,1)} custom-call(s32[4]{0:T(128)S(1)} %pad_add_fusion.place_ref, bf16[384,256]{1,0:T(8,128)(2,1)S(1)} %get-tuple-element.17.own_main, bf16[384,64]{1,0:T(8,128)(2,1)S(1)} %get-tuple-element.18.own_extra, bf16[384,256]{1,0:T(8,128)(2,1)S(1)} %get-tuple-element.20.other_main, ...), custom_call_target="tpu_custom_call" | custom-call | flops 377487360 | bytes 983040 | tf_op jit(solution)/shard_map/order/pallas_call | solution.py:417
  139.7 3.3 %collective-permute-done.14 = f32[1,16,128]{2,1,0:T(8,128)S(1)} collective-permute-done((f32[1,16,128]{2,1,0:T(8,128)S(1)}, f32[1,16,128]{2,1,0:T(8,128)S(1)}, u32[]{:S(2)}, u32[]{:S(2)}) %collective-permute-start.14) | collective-permute-done | bytes 8224 | tf_op jit(solution)/shard_map/ppermute | solution.py:292
  (49 shorter events, 27.1 us)
Async XLA Ops:
  0.6 6.7 %collective-permute-start = (bf16[24,2048]{1,0:T(8,128)(2,1)}, bf16[24,2048]{1,0:T(8,128)(2,1)S(1)}, u32[]{:S(2)}, u32[]{:S(2)}) collective-permute-start(bf16[24,2048]{1,0:T(8,128)(2,1)} %bitcast.52), channel_id=1, source_target_pairs={{0,2},{2,0},{1,3},{3,1},{4,6},{6,4},{5,7},{7,5},{8,10},{10,8},{9,1... | collective-permute-start | bytes 294920 | tf_op jit(solution)/shard_map/ppermute | solution.py:357
  10.2 20.6 %copy-start.2 = (bf16[1,24,2048]{2,1,0:T(8,128)(2,1)S(1)}, bf16[1,24,2048]{2,1,0:T(8,128)(2,1)}, u32[]{:S(2)}) copy-start(bf16[1,24,2048]{2,1,0:T(8,128)(2,1)} %param.13) | copy-start | bytes 294916
  10.2 56.1 %all-to-all-start = ((bf16[32,8,2560]{2,1,0:T(8,128)(2,1)}), bf16[32,8,2560]{2,1,0:T(8,128)(2,1)S(1)}, u32[]{:S(2)}, u32[]{:S(2)}) async-start(bf16[32,8,2560]{2,1,0:T(8,128)(2,1)} %bitcast.11), calls=%async_computation | async-start | bytes 2621440 | tf_op jit(solution)/shard_map/all_to_all | solution.py:384
  30.8 9.3 %collective-permute-start.1 = (bf16[2,24,2048]{2,1,0:T(8,128)(2,1)S(1)}, bf16[2,24,2048]{2,1,0:T(8,128)(2,1)S(1)}, u32[]{:S(2)}, u32[]{:S(2)}) collective-permute-start(bf16[2,24,2048]{2,1,0:T(8,128)(2,1)S(1)} %paired.1.refs_0_), channel_id=1, source_target_pairs={{0,28},{4,0},{8,4},{12,8},{16,12},{20,16},{24,20},{28,24},{1,29},{... | collective-permute-start | bytes 589832 | tf_op jit(solution)/shard_map/ppermute | solution.py:250
  37.0 8.8 %collective-permute-start.5 = (bf16[2,24,2048]{2,1,0:T(8,128)(2,1)S(1)}, bf16[2,24,2048]{2,1,0:T(8,128)(2,1)S(1)}, u32[]{:S(2)}, u32[]{:S(2)}) collective-permute-start(bf16[2,24,2048]{2,1,0:T(8,128)(2,1)S(1)} %paired.1.refs_0_), channel_id=1, source_target_pairs={{0,4},{4,8},{8,12},{12,16},{16,20},{20,24},{24,28},{28,0},{1,5},{5... | collective-permute-start | bytes 589832 | tf_op jit(solution)/shard_map/ppermute | solution.py:253
  40.2 8.8 %collective-permute-start.2 = (bf16[2,24,2048]{2,1,0:T(8,128)(2,1)S(1)}, bf16[2,24,2048]{2,1,0:T(8,128)(2,1)S(1)}, u32[]{:S(2)}, u32[]{:S(2)}) collective-permute-start(bf16[2,24,2048]{2,1,0:T(8,128)(2,1)S(1)} %collective-permute-done.1.refs_1_), channel_id=1, source_target_pairs={{0,28},{4,0},{8,4},{12,8},{16,12},{20,16},{24,20},{28,24},{1,29},{... | collective-permute-start | bytes 589832 | tf_op jit(solution)/shard_map/ppermute | solution.py:250
  45.8 8.8 %collective-permute-start.6 = (bf16[2,24,2048]{2,1,0:T(8,128)(2,1)S(1)}, bf16[2,24,2048]{2,1,0:T(8,128)(2,1)S(1)}, u32[]{:S(2)}, u32[]{:S(2)}) collective-permute-start(bf16[2,24,2048]{2,1,0:T(8,128)(2,1)S(1)} %collective-permute-done.5.refs_7_), channel_id=1, source_target_pairs={{0,4},{4,8},{8,12},{12,16},{16,20},{20,24},{24,28},{28,0},{1,5},{5... | collective-permute-start | bytes 589832 | tf_op jit(solution)/shard_map/ppermute | solution.py:253
  49.0 10.2 %collective-permute-start.3 = (bf16[2,24,2048]{2,1,0:T(8,128)(2,1)S(1)}, bf16[2,24,2048]{2,1,0:T(8,128)(2,1)S(1)}, u32[]{:S(2)}, u32[]{:S(2)}) collective-permute-start(bf16[2,24,2048]{2,1,0:T(8,128)(2,1)S(1)} %collective-permute-done.2.refs_2_), channel_id=1, source_target_pairs={{0,28},{4,0},{8,4},{12,8},{16,12},{20,16},{24,20},{28,24},{1,29},{... | collective-permute-start | bytes 589832 | tf_op jit(solution)/shard_map/ppermute | solution.py:250
  54.6 8.8 %collective-permute-start.7 = (bf16[2,24,2048]{2,1,0:T(8,128)(2,1)S(1)}, bf16[2,24,2048]{2,1,0:T(8,128)(2,1)S(1)}, u32[]{:S(2)}, u32[]{:S(2)}) collective-permute-start(bf16[2,24,2048]{2,1,0:T(8,128)(2,1)S(1)} %collective-permute-done.6.refs_6_), channel_id=1, source_target_pairs={{0,4},{4,8},{8,12},{12,16},{16,20},{20,24},{24,28},{28,0},{1,5},{5... | collective-permute-start | bytes 589832 | tf_op jit(solution)/shard_map/ppermute | solution.py:253
  56.6 1.0 copy-start.7
  66.3 15.3 %copy-start.1 = (bf16[2,24,2048]{2,1,0:T(8,128)(2,1)S(1)}, bf16[2,24,2048]{2,1,0:T(8,128)(2,1)}, u32[]{:S(2)}) copy-start(bf16[2,24,2048]{2,1,0:T(8,128)(2,1)} %copy-done) | copy-start | bytes 589828
  68.7 16.7 %collective-permute-start.9 = (bf16[384,2048]{1,0:T(8,128)(2,1)}, bf16[384,2048]{1,0:T(8,128)(2,1)S(1)}, u32[]{:S(2)}, u32[]{:S(2)}) collective-permute-start(bf16[384,2048]{1,0:T(8,128)(2,1)} %half_sent.1), channel_id=1, source_target_pairs={{0,1},{1,0},{2,3},{3,2},{4,5},{5,4},{6,7},{7,6},{8,9},{9,8},{10,11... | collective-permute-start | bytes 4718600 | tf_op jit(solution)/shard_map/ppermute | solution.py:407
  70.6 11.0 %collective-permute-start.4 = (bf16[2,24,2048]{2,1,0:T(8,128)(2,1)S(1)}, bf16[2,24,2048]{2,1,0:T(8,128)(2,1)S(1)}, u32[]{:S(2)}, u32[]{:S(2)}) collective-permute-start(bf16[2,24,2048]{2,1,0:T(8,128)(2,1)S(1)} %collective-permute-done.3.refs_3_.refs_0_), channel_id=1, source_target_pairs={{0,28},{4,0},{8,4},{12,8},{16,12},{20,16},{24,20},{28,24},{1,29},{... | collective-permute-start | bytes 589832 | tf_op jit(solution)/shard_map/ppermute | solution.py:250
  83.4 15.3 %collective-permute-start.8 = (bf16[384,2048]{1,0:T(8,128)(2,1)}, bf16[384,2048]{1,0:T(8,128)(2,1)}, u32[]{:S(2)}, u32[]{:S(2)}) collective-permute-start(bf16[384,2048]{1,0:T(8,128)(2,1)} %bitcast.10.weights_ref), channel_id=1, source_target_pairs={{0,1},{1,0},{2,3},{3,2},{4,5},{5,4},{6,7},{7,6},{8,9},{9,8},{10,11... | collective-permute-start | bytes 4718600 | tf_op jit(solution)/shard_map/ppermute | solution.py:390
  87.7 57.1 %all-to-all-start.1 = ((bf16[16,24,2048]{2,1,0:T(8,128)(2,1)}), bf16[16,24,2048]{2,1,0:T(8,128)(2,1)S(1)}, u32[]{:S(2)}, u32[]{:S(2)}) async-start(bf16[16,24,2048]{2,1,0:T(8,128)(2,1)} %bitcast.64), calls=%async_computation.1 | async-start | bytes 3145728 | tf_op jit(solution)/shard_map/all_to_all | solution.py:409
  102.4 40.6 %copy-start.3 = (f32[128,8]{0,1:T(8,128)S(1)}, f32[128,8]{0,1:T(8,128)}, u32[]{:S(2)}) copy-start(f32[128,8]{0,1:T(8,128)} %param.8) | copy-start | bytes 12292
  102.4 40.6 %copy-start.4 = (s32[128,8]{0,1:T(8,128)S(1)}, s32[128,8]{0,1:T(8,128)}, u32[]{:S(2)}) copy-start(s32[128,8]{0,1:T(8,128)} %param.9) | copy-start | bytes 12292
  102.4 40.6 %copy-start.5 = (s32[128,8]{0,1:T(8,128)S(1)}, s32[128,8]{0,1:T(8,128)}, u32[]{:S(2)}) copy-start(s32[128,8]{0,1:T(8,128)} %param.10) | copy-start | bytes 12292
  102.4 40.6 %copy-start.6 = (f32[128,8]{0,1:T(8,128)S(1)}, f32[128,8]{0,1:T(8,128)}, u32[]{:S(2)}) copy-start(f32[128,8]{0,1:T(8,128)} %param.11) | copy-start | bytes 12292
  102.5 5.5 %collective-permute-start.10 = (f32[16,1,128]{2,0,1:T(8,128)S(1)}, f32[16,1,128]{2,0,1:T(8,128)S(1)}, u32[]{:S(2)}, u32[]{:S(2)}) collective-permute-start(f32[16,1,128]{2,0,1:T(8,128)S(1)} %bitcast.74), channel_id=1, source_target_pairs={{0,32},{32,0},{64,96},{96,64},{128,160},{160,128},{192,224},{224,1... | collective-permute-start | bytes 24584 | tf_op jit(solution)/shard_map/ppermute | solution.py:292
  108.0 6.4 %collective-permute-start.11 = (f32[8,2,128]{2,0,1:T(8,128)S(1)}, f32[8,2,128]{2,0,1:T(8,128)S(1)}, u32[]{:S(2)}, u32[]{:S(2)}) collective-permute-start(f32[8,2,128]{2,0,1:T(8,128)S(1)} %bitcast.73), channel_id=1, source_target_pairs={{0,64},{32,96},{64,0},{96,32},{128,192},{160,224},{192,128},{224,1... | collective-permute-start | bytes 24584 | tf_op jit(solution)/shard_map/ppermute | solution.py:292
  114.5 9.5 %collective-permute-start.12 = (f32[4,4,128]{2,0,1:T(4,128)S(1)}, f32[4,4,128]{2,0,1:T(4,128)S(1)}, u32[]{:S(2)}, u32[]{:S(2)}) collective-permute-start(f32[4,4,128]{2,0,1:T(4,128)S(1)} %bitcast.76), channel_id=1, source_target_pairs={{0,128},{32,160},{64,192},{96,224},{128,0},{160,32},{192,64},{224,... | collective-permute-start | bytes 24584 | tf_op jit(solution)/shard_map/ppermute | solution.py:292
  124.0 9.6 %collective-permute-start.13 = (f32[2,8,128]{2,1,0:T(8,128)S(1)}, f32[2,8,128]{2,1,0:T(8,128)S(1)}, u32[]{:S(2)}, u32[]{:S(2)}) collective-permute-start(f32[2,8,128]{2,1,0:T(8,128)S(1)} %get-tuple-element.26), channel_id=1, source_target_pairs={{0,256},{256,0},{512,768},{768,512},{1,257},{257,1},{513,769},{769... | collective-permute-start | bytes 24584 | tf_op jit(solution)/shard_map/ppermute | solution.py:292
  133.6 9.4 %collective-permute-start.14 = (f32[1,16,128]{2,1,0:T(8,128)S(1)}, f32[1,16,128]{2,1,0:T(8,128)S(1)}, u32[]{:S(2)}, u32[]{:S(2)}) collective-permute-start(f32[1,16,128]{2,1,0:T(8,128)S(1)} %get-tuple-element.24), channel_id=1, source_target_pairs={{0,512},{256,768},{512,0},{768,256},{1,513},{257,769},{513,1},{769... | collective-permute-start | bytes 24584 | tf_op jit(solution)/shard_map/ppermute | solution.py:292
  (1 other events, 0.7 us)

commit v5 on v4

--- a/solution.py
+++ b/solution.py
@@ -17,9 +17,8 @@
 BF16 = jnp.bfloat16
 VMEM = pl.BlockSpec(memory_space=pltpu.VMEM)
 HBM = pl.BlockSpec(memory_space=pltpu.HBM)
-ANY = pl.BlockSpec(memory_space=pl.ANY)
 SMEM = pl.BlockSpec(memory_space=pltpu.SMEM)
-PARAMS = pltpu.CompilerParams(vmem_limit_bytes=48 * 1024 * 1024)
+PARAMS = pltpu.CompilerParams(vmem_limit_bytes=12 * 1024 * 1024)
 
 
 def cost(flops, size):
@@ -70,21 +69,29 @@
     fold_ref[...] = fold.astype(BF16)
 
 
-def pack_kernel(place_ref, fold_ref, rows_in, first_in, out_ref, rows_ref, sem):
-    copy = pltpu.make_async_copy(rows_in, rows_ref, sem)
+def pack_kernel(place_ref, fold_ref, rows_in, out_ref, rows_ref, held, sems):
+    copy = pltpu.make_async_copy(rows_in, rows_ref, sems.at[0])
     copy.start()
-    copy.wait()
     place, fold = place_ref[...], fold_ref[...].astype(F32)
     rows, tokens = place.shape
     row = iota((rows, tokens), 0)
-    width = rows_ref.shape[1]
-    part = width // FOLD
+    folds = [jnp.where(row % FOLD == m, fold, 0.0).astype(BF16) for m in range(FOLD)]
+    part = rows_ref.shape[1] // FOLD
     total = jnp.zeros((rows, part), F32)
-    for m in range(FOLD):
-        block = rows_ref[:, m * part : (m + 1) * part]
-        out_ref[:, m * part : (m + 1) * part] = dot(place, block).astype(BF16)
-        total = total + dot(jnp.where(row % FOLD == m, fold, 0.0).astype(BF16), block)
-    out_ref[:, width:] = total.astype(BF16)
+    copy.wait()
+    copies = []
+    for m in range(FOLD + 1):
+        cols = slice(m * part, (m + 1) * part)
+        if m < FOLD:
+            block = rows_ref[:, cols]
+            held[:, cols] = dot(place, block).astype(BF16)
+            total = total + dot(folds[m], block)
+        else:
+            held[:, cols] = total.astype(BF16)
+        copies.append(pltpu.make_async_copy(held.at[:, cols], out_ref.at[:, cols], sems.at[m + 1]))
+        copies[-1].start()
+    for copy in copies:
+        copy.wait()
 
 
 def permuted_units(core, units, shard):
@@ -120,24 +127,36 @@
     return dot(pick, block).astype(BF16)
 
 
+def columns(m, part):
+    return pl.ds(pl.multiple_of(m * part, part), part)
+
+
 def half_kernel(half, adds, main_t_ref, extra_t_ref, payload_ref, *refs):
     *given, out_ref, held, sems = refs
     units, width = held.shape
     part = width // FOLD
     span = slice(half * units, (half + 1) * units)
-    main_t, extra_t = main_t_ref[span, :], extra_t_ref[span, :]
-    fold = payload_ref[:, width:]
-    copies = []
-    for m in range(FOLD):
-        cols = slice(m * part, (m + 1) * part)
-        total = dot(main_t, payload_ref[:, cols]) + dot(extra_t, unfolded(fold, m))
+
+    def copy_of(m):
+        cols = columns(m, part)
+        return pltpu.make_async_copy(held.at[:, cols], out_ref.at[:, cols], sems.at[m])
+
+    def step(m, carry):
+        cols = columns(m, part)
+        total = dot(main_t_ref[span, :], payload_ref[:, cols])
+        total = total + dot(extra_t_ref[span, :], unfolded(payload_ref[:, width:], m))
         if adds:
             total = total + given[0][:, cols].astype(F32)
         held[:, cols] = total.astype(BF16)
-        copies.append(pltpu.make_async_copy(held.at[:, cols], out_ref.at[:, cols], sems.at[m]))
-        copies[-1].start()
-    for copy in copies:
-        copy.wait()
+        copy_of(m).start()
+        return carry
+
+    def wait(m, carry):
+        copy_of(m).wait()
+        return carry
+
+    lax.fori_loop(0, FOLD, step, 0)
+    lax.fori_loop(0, FOLD, wait, 0)
 
 
 def half_partial(main_t, extra_t, payload, half, arrived=None, first=()):
@@ -147,7 +166,7 @@
     width = payload.shape[1] * FOLD // (FOLD + 1)
     return pl.pallas_call(
         functools.partial(half_kernel, half, bool(given)),
-        in_specs=[VMEM] * (3 + len(given)) + [ANY] * len(first),
+        in_specs=[VMEM] * (3 + len(given)) + [VMEM] * len(first),
         out_specs=HBM,
         out_shape=pltpu.HBM((units // 2, width), BF16),
         scratch_shapes=[pltpu.VMEM((units // 2, width), BF16), pltpu.SemaphoreType.DMA((FOLD,))],
@@ -157,27 +176,33 @@
     )(main_t, extra_t, payload, *given, *first)
 
 
-def product_kernel(half, place_ref, main_t_ref, extra_t_ref, weights_ref, payload_ref, *refs):
-    *given, main_ref, extra_ref, score_ref = refs
+def product_kernel(half, main_t_ref, extra_t_ref, weights_ref, payload_ref, *refs):
+    *given, main_ref, extra_ref, score_ref, acc_main, acc_extra = refs
     units, rows = main_ref.shape
     few = extra_ref.shape[1]
     source = rows // 8
     width = weights_ref.shape[1]
     part = width // FOLD
-    weights = weights_ref[...]
-    fold = payload_ref[:, width:]
-    main = dot(weights, payload_ref[:, :width], 1, 1)
-    extra = jnp.zeros((units, few), F32)
-    for m in range(FOLD):
-        extra = extra + dot(weights[:, m * part : (m + 1) * part], unfolded(fold, m), 1, 1)
+    acc_main[...] = jnp.zeros_like(acc_main)
+    acc_extra[...] = jnp.zeros_like(acc_extra)
+
+    def step(m, carry):
+        cols = columns(m, part)
+        weights = weights_ref[:, cols]
+        acc_main[...] += dot(weights, payload_ref[:, cols], 1, 1)
+        acc_extra[...] += dot(weights, unfolded(payload_ref[:, width:], m), 1, 1)
+        return carry
+
+    lax.fori_loop(0, FOLD, step, 0)
+    main, extra = acc_main[...], acc_extra[...]
     main_ref[...] = main.astype(BF16)
     extra_ref[...] = extra.astype(BF16)
     span = slice(half * units, (half + 1) * units)
     main_score = jnp.sum(main * main_t_ref[span, :].astype(F32), axis=0, keepdims=True)
     extra_score = jnp.sum(extra * extra_t_ref[span, :].astype(F32), axis=0, keepdims=True)
-    to_main = (iota((source, rows), 0) ^ place_ref[1]) == iota((source, rows), 1) // 8
+    to_main = iota((source, rows), 0) == iota((source, rows), 1) // 8
     at_main = iota((rows, 128), 0) % 8 == iota((rows, 128), 1)
-    to_extra = (iota((source, few), 0) ^ place_ref[1]) == iota((source, few), 1) % source
+    to_extra = iota((source, few), 0) == iota((source, few), 1) % source
     at_extra = iota((few, 128), 0) // source + 8 == iota((few, 128), 1)
     score = exact_dot(jnp.where(to_main, main_score, 0.0), jnp.where(at_main, 1.0, 0.0))
     score = score + exact_dot(jnp.where(to_extra, extra_score, 0.0), jnp.where(at_extra, 1.0, 0.0))
@@ -186,22 +211,23 @@
     score_ref[...] = score
 
 
-def half_product(place, main_t, extra_t, weights, payload, half, *given):
+def half_product(main_t, extra_t, weights, payload, half, *given):
     units, rows = main_t.shape
     few = extra_t.shape[1]
     return pl.pallas_call(
         functools.partial(product_kernel, half),
-        in_specs=[SMEM] + [VMEM] * (4 + len(given)),
+        in_specs=[VMEM] * (4 + len(given)),
         out_specs=[VMEM] * 3,
         out_shape=[
             jax.ShapeDtypeStruct((units // 2, rows), BF16),
             jax.ShapeDtypeStruct((units // 2, few), BF16),
             jax.ShapeDtypeStruct((rows // 8, 128), F32),
         ],
+        scratch_shapes=[pltpu.VMEM((units // 2, rows), F32), pltpu.VMEM((units // 2, few), F32)],
         compiler_params=PARAMS,
         cost_estimate=cost(units * (rows + few) * weights.shape[1], 0),
         name="product_of_other" if half else "product_of_own",
-    )(place, main_t, extra_t, weights, payload, *given)
+    )(main_t, extra_t, weights, payload, *given)
 
 
 def order_kernel(shard, place_ref, own_main, own_extra, other_main, other_extra, grad_ref):
@@ -232,36 +258,42 @@
 
 
 def placed_kernel(place_ref, *refs):
-    *pieces, out_ref = refs
+    *pieces, out_ref, sems = refs
     count = len(pieces)
+    copies = []
     for k, piece in enumerate(pieces):
-        base = lax.rem(place_ref[2] + k, count) * 2
+        base = lax.rem(place_ref[1] + k, count) * 2
         for t in range(2):
-            out_ref[base + (place_ref[3] ^ t)] = piece[t]
+            spot = base + (place_ref[2] ^ t)
+            copies.append(pltpu.make_async_copy(piece.at[t], out_ref.at[spot], sems.at[2 * k + t]))
+            copies[-1].start()
+    for copy in copies:
+        copy.wait()
 
 
 def gathered(place, pair):
     size = lax.axis_size("y")
     down = [(i, (i + size - 1) % size) for i in range(size)]
     up = [(i, (i + 1) % size) for i in range(size)]
+    above = below = pair = in_hbm(pair)
     pieces = [pair] + [None] * (size - 1)
-    above = below = pair
     for k in range(1, size // 2 + 1):
-        above = lax.ppermute(above, "y", down)
+        above = in_hbm(lax.ppermute(above, "y", down))
         pieces[k] = above
         if k < size - k:
-            below = lax.ppermute(below, "y", up)
+            below = in_hbm(lax.ppermute(below, "y", up))
             pieces[size - k] = below
     placed = pl.pallas_call(
         placed_kernel,
-        in_specs=[SMEM] + [VMEM] * size,
+        in_specs=[SMEM] + [HBM] * size,
         out_specs=VMEM,
         out_shape=jax.ShapeDtypeStruct((2 * size, *pair.shape[1:]), pair.dtype),
+        scratch_shapes=[pltpu.SemaphoreType.DMA((2 * size,))],
         compiler_params=PARAMS,
         cost_estimate=cost(0, 0),
         name="placed",
     )(place, *pieces)
-    return placed, pieces
+    return placed
 
 
 def pair_kernel(weights_ref, beside_ref, first_ref, out_ref):
@@ -272,31 +304,43 @@
 def paired(weights, beside, first):
     return pl.pallas_call(
         pair_kernel,
-        in_specs=[VMEM, VMEM, ANY],
+        in_specs=[VMEM, VMEM, HBM],
         out_specs=VMEM,
         out_shape=jax.ShapeDtypeStruct((2, *weights.shape), weights.dtype),
         compiler_params=PARAMS,
         cost_estimate=cost(0, 0),
         name="paired",
-    )(weights, beside, first)
-
-
-def exchanged_by_bits(blocks):
-    count, lanes = blocks.shape
-    inner = lax.axis_size("x")
-    bit = 1
-    while bit < count:
-        axis, step = ("x", bit) if bit < inner else ("zh", bit // inner)
-        size = lax.axis_size(axis)
-        pairs = blocks.reshape(count // (2 * bit), 2, bit, lanes)
-        came = lax.ppermute(pairs[:, 1], axis, [(i, i ^ step) for i in range(size)])
-        blocks = jnp.stack([pairs[:, 0], came], axis=1).reshape(count, lanes)
-        bit *= 2
-    return blocks
+    )(weights, beside, in_hbm(first))
+
+
+def returned_scores(blocks):
+    outer, inner = (lax.axis_size(k) for k in EXPERT)
+    lanes = blocks.shape[1]
+    row = lax.all_gather(blocks, "x").reshape(inner, outer, inner, lanes)
+    row = lax.dynamic_index_in_dim(row, lax.axis_index("x"), 2, keepdims=False)
+    square = lax.all_gather(row, "zh")
+    square = lax.dynamic_index_in_dim(square, lax.axis_index("zh"), 2, keepdims=False)
+    return square.reshape(outer * inner, lanes)
 
 
 def in_hbm(array):
     return pltpu.with_memory_space_constraint(array, pltpu.HBM)
+
+
+def after(array, first):
+    return pl.pallas_call(
+        after_kernel,
+        in_specs=[HBM, VMEM],
+        out_specs=HBM,
+        out_shape=pltpu.HBM(array.shape, array.dtype),
+        input_output_aliases={0: 0},
+        cost_estimate=cost(0, 0),
+        name="after",
+    )(array, first)
+
+
+def after_kernel(array_ref, first_ref, out_ref):
+    pass
 
 
 def sum_kernel(pieces_ref, out_ref):
@@ -321,7 +365,7 @@
     )(pieces)
 
 
-def logits_kernel(place_ref, logits_ref, chosen_ref, slots_ref, outside_ref, score_ref, out_ref):
+def logits_kernel(logits_ref, chosen_ref, slots_ref, outside_ref, score_ref, out_ref):
     gating = softmax_rows(logits_ref[...])
     sent = gating.astype(BF16).astype(F32)
     chosen, slots = chosen_ref[...], slots_ref[...]
@@ -329,9 +373,8 @@
     experts = score_ref.shape[0]
     returned = score_ref[...]
     found = []
-    here = chosen ^ place_ref[1]
     for k in range(topk):
-        hit = jnp.where(iota((experts, tokens), 0) == here[k : k + 1, :], 1.0, 0.0)
+        hit = jnp.where(iota((experts, tokens), 0) == chosen[k : k + 1, :], 1.0, 0.0)
         by_slot = exact_dot(returned, hit, 0, 0)[:16, :]
         at_slot = iota((16, tokens), 0) == slots[k : k + 1, :]
         found.append(jnp.sum(jnp.where(at_slot, by_slot, 0.0), axis=0, keepdims=True))
@@ -347,9 +390,7 @@
     window, capacity, units = hidden.shape[2], hidden.shape[3], hidden.shape[4]
     model = grad_output.shape[1]
     shard = down_weight.shape[1]
-    expert = lax.axis_index(EXPERT)
-    place = [lax.axis_index("core"), expert, lax.axis_index("y"), lax.axis_index("zl")]
-    place = jnp.stack(place).astype(jnp.int32)
+    place = jnp.stack([lax.axis_index(k) for k in ("core", "y", "zl")]).astype(jnp.int32)
     logits_t, chosen_t, slots_t = logits.T, chosen.T, slots.T
     swap = [(0, 1), (1, 0)]
 
@@ -371,21 +412,27 @@
         cost_estimate=cost(0, 4 * 320 * model),
         name="placing",
     )(*map(in_hbm, (logits_t, chosen_t, slots_t)))
+    packed_shape = (window * 8, model + model // FOLD)
     packed = pl.pallas_call(
         pack_kernel,
-        in_specs=[VMEM, VMEM, HBM, ANY],
-        out_specs=VMEM,
-        out_shape=jax.ShapeDtypeStruct((window * 8, model + model // FOLD), BF16),
-        scratch_shapes=[pltpu.VMEM((tokens, model), BF16), pltpu.SemaphoreType.DMA],
+        in_specs=[VMEM, VMEM, HBM],
+        out_specs=HBM,
+        out_shape=pltpu.HBM(packed_shape, BF16),
+        scratch_shapes=[
+            pltpu.VMEM((tokens, model), BF16),
+            pltpu.VMEM(packed_shape, BF16),
+            pltpu.SemaphoreType.DMA((FOLD + 2,)),
+        ],
         compiler_params=PARAMS,
         cost_estimate=cost(2 * 320 * tokens * model * 2, 4 * 320 * model),
         name="pack",
-    )(*placing, in_hbm(grad_output), beside)
+    )(*placing, in_hbm(grad_output))
+    packed = after(packed, beside[:8, :128])
     payload = lax.all_to_all(
         packed.reshape(window, 8, packed.shape[1]), EXPERT, split_axis=0, concat_axis=0, tiled=True
     ).reshape(packed.shape)
 
-    own_weights, pieces = gathered(place, paired(weights, beside, packed))
+    own_weights = gathered(place, paired(weights, beside, packed))
     own_weights = own_weights.reshape(-1, model)
     other_weights = lax.ppermute(own_weights, "core", swap)
 
@@ -403,7 +450,7 @@
         name="hidden_order",
     )(place, by_slot)
 
-    sent = half_partial(main_t, extra_t, payload, 1, first=(pieces[3], pieces[-3]))
+    sent = half_partial(main_t, extra_t, payload, 1, first=(own_weights[:8, :128],))
     arrived = lax.ppermute(sent, "core", swap)
     both = half_partial(main_t, extra_t, payload, 0, arrived)
     parts = lax.all_to_all(
@@ -411,9 +458,9 @@
     )
     grad_down = summed(parts).reshape(1, shard, model)
 
-    *own_grad, score = half_product(place, main_t, extra_t, own_weights, payload, 0)
-    *other_grad, score = half_product(place, main_t, extra_t, other_weights, payload, 1, score)
-    returned = exchanged_by_bits(score)
+    *own_grad, score = half_product(main_t, extra_t, own_weights, payload, 0)
+    *other_grad, score = half_product(main_t, extra_t, other_weights, payload, 1, score)
+    returned = returned_scores(score)
     grad = pl.pallas_call(
         functools.partial(order_kernel, shard),
         in_specs=[SMEM] + [VMEM] * 4,
@@ -426,13 +473,13 @@
     grad_hidden = grad.reshape(1, 1, capacity, window, units).transpose(0, 1, 3, 2, 4)
     grad_logits = pl.pallas_call(
         logits_kernel,
-        in_specs=[SMEM] + [VMEM] * 5,
+        in_specs=[VMEM] * 5,
         out_specs=VMEM,
         out_shape=jax.ShapeDtypeStruct((topk, tokens), F32),
         compiler_params=PARAMS,
         cost_estimate=cost(0, 0),
         name="logits",
-    )(place, logits_t, chosen_t, slots_t, other_scores.T, returned)
+    )(logits_t, chosen_t, slots_t, other_scores.T, returned)
     return grad_hidden, grad_down, grad_logits.T
 
 

time: 147 us -> 145 us (0.986)
  the two profiles are of different devices: /device:TPU:130 before, /device:TPU:20 now
where the time goes in v5:
time: 145 us; the launch traced here: 144 us
  starting transfers between devices  63.1 us (44%)
  blocking collectives  41.1 us (28%)
  Pallas kernels  26.9 us (19%)
  waiting for transfers between devices  10.7 us (7%)
    all_gather x1, blocking collectives, returned_scores(): row = lax.all_gather(blocks, 'x').reshape(inner, outer, inner, lanes)  25.5 us
    all_to_all x1, starting transfers between devices, body(): lax.all_to_all(packed.reshape(window, 8, packed.shape[1]), EXPERT, split_...  20.6 us
    ppermute x4, starting transfers between devices, gathered(): above = in_hbm(lax.ppermute(above, 'y', down))  17.1 us
    all_gather x1, blocking collectives, returned_scores(): square = lax.all_gather(row, 'zh')  15.6 us
    all_to_all x1, starting transfers between devices, body(): lax.all_to_all(both.reshape(-1, shard, model), RING, split_axis=0, concat...  8.96 us
    ppermute x3, starting transfers between devices, gathered(): below = in_hbm(lax.ppermute(below, 'y', up))  7.41 us
    pallas_call x2, Pallas kernels, half_product(): pl.pallas_call(functools.partial(product_kernel, half), in_specs=[VMEM] *...  6.21 us
    pallas_call x2, Pallas kernels, half_partial(): pl.pallas_call(functools.partial(half_kernel, half, bool(given)), in_spec...  5.66 us
  transfers between devices with their start and end apart: 12, of which 9 were waited for; matrix products, arithmetic and copies ran while one was open for 0% of the time, Pallas kernels for 12%

profile of v5, /device:TPU:20, one launch (start us, length us, event | category | flops | bytes accessed | tf_op | source)
XLA Modules:
  0.0 144.0 jit_solution(13150072252280713364)
XLA Ops:
  0.6 5.2 %collective-permute-start = (bf16[24,2048]{1,0:T(8,128)(2,1)}, bf16[24,2048]{1,0:T(8,128)(2,1)S(1)}, u32[]{:S(2)}, u32[]{:S(2)}) collective-permute-start(bf16[24,2048]{1,0:T(8,128)(2,1)} %bitcast.33), channel_id=1, source_target_pairs={{0,2},{2,0},{1,3},{3,1},{4,6},{6,4},{5,7},{7,5},{8,10},{10,8},{9,1... | collective-permute-start | bytes 294920 | tf_op jit(solution)/shard_map/ppermute | solution.py:398
  6.8 2.5 %pack.1.array_ref = bf16[256,2560]{1,0:T(8,128)(2,1)} custom-call(bf16[256,128]{1,0:T(8,128)(2,1)S(1)} %get-tuple-element.15.place_ref, bf16[256,128]{1,0:T(8,128)(2,1)S(1)} %get-tuple-element.16.fold_ref, bf16[128,2048]{1,0:T(8,128)(2,1)} %rows_in.1), custom_call_target="tpu_custom_call" | custom-call | flops 335544320 | bytes 2621440 | tf_op jit(solution)/shard_map/pack/pallas_call | solution.py:416
  10.6 20.6 %all-to-all-start = ((bf16[32,8,2560]{2,1,0:T(8,128)(2,1)}), bf16[32,8,2560]{2,1,0:T(8,128)(2,1)S(1)}, u32[]{:S(2)}, u32[]{:S(2)}) async-start(bf16[32,8,2560]{2,1,0:T(8,128)(2,1)} %bitcast.44), calls=%async_computation | async-start | bytes 2621440 | tf_op jit(solution)/shard_map/all_to_all | solution.py:431
  31.3 2.2 %collective-permute-start.1 = (bf16[2,24,2048]{2,1,0:T(8,128)(2,1)S(1)}, bf16[2,24,2048]{2,1,0:T(8,128)(2,1)S(1)}, u32[]{:S(2)}, u32[]{:S(2)}) collective-permute-start(bf16[2,24,2048]{2,1,0:T(8,128)(2,1)S(1)} %paired.1.refs_0_), channel_id=1, source_target_pairs={{0,28},{4,0},{8,4},{12,8},{16,12},{20,16},{24,20},{28,24},{1,29},{... | collective-permute-start | bytes 589832 | tf_op jit(solution)/shard_map/ppermute | solution.py:281
  33.5 3.6 %collective-permute-start.5 = (bf16[2,24,2048]{2,1,0:T(8,128)(2,1)S(1)}, bf16[2,24,2048]{2,1,0:T(8,128)(2,1)S(1)}, u32[]{:S(2)}, u32[]{:S(2)}) collective-permute-start(bf16[2,24,2048]{2,1,0:T(8,128)(2,1)S(1)} %paired.1.refs_0_), channel_id=1, source_target_pairs={{0,4},{4,8},{8,12},{12,16},{16,20},{20,24},{24,28},{28,0},{1,5},{5... | collective-permute-start | bytes 589832 | tf_op jit(solution)/shard_map/ppermute | solution.py:284
  37.1 1.8 %collective-permute-done.1.refs_1_ = bf16[2,24,2048]{2,1,0:T(8,128)(2,1)S(1)} collective-permute-done((bf16[2,24,2048]{2,1,0:T(8,128)(2,1)S(1)}, bf16[2,24,2048]{2,1,0:T(8,128)(2,1)S(1)}, u32[]{:S(2)}, u32[]{:S(2)}) %collective-permute-start.1) | collective-permute-done | bytes 196640 | tf_op jit(solution)/shard_map/ppermute | solution.py:281
  39.0 4.0 %collective-permute-start.2 = (bf16[2,24,2048]{2,1,0:T(8,128)(2,1)S(1)}, bf16[2,24,2048]{2,1,0:T(8,128)(2,1)S(1)}, u32[]{:S(2)}, u32[]{:S(2)}) collective-permute-start(bf16[2,24,2048]{2,1,0:T(8,128)(2,1)S(1)} %collective-permute-done.1.refs_1_), channel_id=1, source_target_pairs={{0,28},{4,0},{8,4},{12,8},{16,12},{20,16},{24,20},{28,24},{1,29},{... | collective-permute-start | bytes 589832 | tf_op jit(solution)/shard_map/ppermute | solution.py:281
  43.5 1.9 %collective-permute-start.6 = (bf16[2,24,2048]{2,1,0:T(8,128)(2,1)S(1)}, bf16[2,24,2048]{2,1,0:T(8,128)(2,1)S(1)}, u32[]{:S(2)}, u32[]{:S(2)}) collective-permute-start(bf16[2,24,2048]{2,1,0:T(8,128)(2,1)S(1)} %collective-permute-done.5.refs_7_), channel_id=1, source_target_pairs={{0,4},{4,8},{8,12},{12,16},{16,20},{20,24},{24,28},{28,0},{1,5},{5... | collective-permute-start | bytes 589832 | tf_op jit(solution)/shard_map/ppermute | solution.py:284
  46.5 5.2 %collective-permute-start.3 = (bf16[2,24,2048]{2,1,0:T(8,128)(2,1)S(1)}, bf16[2,24,2048]{2,1,0:T(8,128)(2,1)S(1)}, u32[]{:S(2)}, u32[]{:S(2)}) collective-permute-start(bf16[2,24,2048]{2,1,0:T(8,128)(2,1)S(1)} %collective-permute-done.2.refs_2_), channel_id=1, source_target_pairs={{0,28},{4,0},{8,4},{12,8},{16,12},{20,16},{24,20},{28,24},{1,29},{... | collective-permute-start | bytes 589832 | tf_op jit(solution)/shard_map/ppermute | solution.py:281
  52.2 1.9 %collective-permute-start.7 = (bf16[2,24,2048]{2,1,0:T(8,128)(2,1)S(1)}, bf16[2,24,2048]{2,1,0:T(8,128)(2,1)S(1)}, u32[]{:S(2)}, u32[]{:S(2)}) collective-permute-start(bf16[2,24,2048]{2,1,0:T(8,128)(2,1)S(1)} %collective-permute-done.6.refs_6_), channel_id=1, source_target_pairs={{0,4},{4,8},{8,12},{12,16},{16,20},{20,24},{24,28},{28,0},{1,5},{5... | collective-permute-start | bytes 589832 | tf_op jit(solution)/shard_map/ppermute | solution.py:284
  54.9 5.6 %collective-permute-start.4 = (bf16[2,24,2048]{2,1,0:T(8,128)(2,1)S(1)}, bf16[2,24,2048]{2,1,0:T(8,128)(2,1)}, u32[]{:S(2)}, u32[]{:S(2)}) collective-permute-start(bf16[2,24,2048]{2,1,0:T(8,128)(2,1)S(1)} %collective-permute-done.3.refs_3_), channel_id=1, source_target_pairs={{0,28},{4,0},{8,4},{12,8},{16,12},{20,16},{24,20},{28,24},{1,29},{... | collective-permute-start | bytes 589832 | tf_op jit(solution)/shard_map/ppermute | solution.py:281
  63.7 2.1 %placed.1 = bf16[16,24,2048]{2,1,0:T(8,128)(2,1)S(1)} custom-call(s32[3]{0:T(128)S(1)} %pad_add_fusion.place_ref, bf16[2,24,2048]{2,1,0:T(8,128)(2,1)} %copy-done, bf16[2,24,2048]{2,1,0:T(8,128)(2,1)} %copy-done.7, bf16[2,24,2048]{2,1,0:T(8,128)(2,1)} %copy-done.9, bf16[2,24,2048]{2,1,0:T(8,128)(2,1)} %copy-done.11, ...), custom_call_target="tpu_custom_call" | custom-call | tf_op jit(solution)/shard_map/placed/pallas_call | solution.py:286
  66.3 2.8 %half_sent.1 = bf16[384,2048]{1,0:T(8,128)(2,1)} custom-call(bf16[768,256]{1,0:T(8,128)(2,1)S(1)} %get-tuple-element.13.main_t_ref, bf16[768,64]{1,0:T(8,128)(2,1)S(1)} %get-tuple-element.14.extra_t_ref, bf16[256,2560]{1,0:T(8,128)(2,1)S(1)} %bitcast.26, bf16[8,128]{1,0:T(8,128)(2,1)S(1)} %slice.9.refs_0_), custom_call_target="tpu_custom_call" | custom-call | flops 503316480 | bytes 4718592 | tf_op jit(solution)/shard_map/half_sent/pallas_call | solution.py:167
  69.1 1.9 %collective-permute-start.9 = (bf16[384,2048]{1,0:T(8,128)(2,1)}, bf16[384,2048]{1,0:T(8,128)(2,1)S(1)}, u32[]{:S(2)}, u32[]{:S(2)}) collective-permute-start(bf16[384,2048]{1,0:T(8,128)(2,1)} %half_sent.1), channel_id=1, source_target_pairs={{0,1},{1,0},{2,3},{3,2},{4,5},{5,4},{6,7},{7,6},{8,9},{9,8},{10,11... | collective-permute-start | bytes 4718600 | tf_op jit(solution)/shard_map/ppermute | solution.py:454
  71.0 3.6 %collective-permute-done.9.refs_0_ = bf16[384,2048]{1,0:T(8,128)(2,1)S(1)} collective-permute-done((bf16[384,2048]{1,0:T(8,128)(2,1)}, bf16[384,2048]{1,0:T(8,128)(2,1)S(1)}, u32[]{:S(2)}, u32[]{:S(2)}) %collective-permute-start.9) | collective-permute-done | bytes 1572896 | tf_op jit(solution)/shard_map/ppermute | solution.py:454
  74.6 2.8 %half_kept.1 = bf16[384,2048]{1,0:T(8,128)(2,1)} custom-call(bf16[768,256]{1,0:T(8,128)(2,1)S(1)} %get-tuple-element.13.main_t_ref, bf16[768,64]{1,0:T(8,128)(2,1)S(1)} %get-tuple-element.14.extra_t_ref, bf16[256,2560]{1,0:T(8,128)(2,1)S(1)} %bitcast.27, bf16[384,2048]{1,0:T(8,128)(2,1)S(1)} %collective-permute-done.9.refs_0_), custom_call_target="tpu_custom_call" | custom-call | flops 503316480 | bytes 4718592 | tf_op jit(solution)/shard_map/half_kept/pallas_call | solution.py:167
  77.5 9.0 %all-to-all-start.1 = ((bf16[16,24,2048]{2,1,0:T(8,128)(2,1)}), bf16[16,24,2048]{2,1,0:T(8,128)(2,1)}, u32[]{:S(2)}, u32[]{:S(2)}) async-start(bf16[16,24,2048]{2,1,0:T(8,128)(2,1)} %bitcast.45), calls=%async_computation.1 | async-start | bytes 3145728 | tf_op jit(solution)/shard_map/all_to_all | solution.py:456
  86.4 1.9 %collective-permute-start.8 = (bf16[384,2048]{1,0:T(8,128)(2,1)S(1)}, bf16[384,2048]{1,0:T(8,128)(2,1)}, u32[]{:S(2)}, u32[]{:S(2)}) collective-permute-start(bf16[384,2048]{1,0:T(8,128)(2,1)S(1)} %bitcast.31), channel_id=1, source_target_pairs={{0,1},{1,0},{2,3},{3,2},{4,5},{5,4},{6,7},{7,6},{8,9},{9,8},{10,11... | collective-permute-start | bytes 4718600 | tf_op jit(solution)/shard_map/ppermute | solution.py:437
  88.3 2.4 %product_of_own.1 = (bf16[384,256]{1,0:T(8,128)(2,1)S(1)}, bf16[384,64]{1,0:T(8,128)(2,1)S(1)}, f32[32,128]{1,0:T(8,128)S(1)}) custom-call(bf16[768,256]{1,0:T(8,128)(2,1)S(1)} %get-tuple-element.13.main_t_ref, bf16[768,64]{1,0:T(8,128)(2,1)S(1)} %get-tuple-element.14.extra_t_ref, bf16[384,2048]{1,0:T(8,128)(2,1)S(1)} %bitcast.32, bf16[256,2560]{1,0:T(8,128)(2,1)S(1)} %bitcast.28), custom_call_target="tpu_custom_call" | custom-call | flops 503316480 | tf_op jit(solution)/shard_map/product_of_own/pallas_call | solution.py:217
  91.9 3.8 %product_of_other.1 = (bf16[384,256]{1,0:T(8,128)(2,1)S(1)}, bf16[384,64]{1,0:T(8,128)(2,1)S(1)}, f32[32,128]{1,0:T(8,128)S(1)}) custom-call(bf16[768,256]{1,0:T(8,128)(2,1)S(1)} %get-tuple-element.13.main_t_ref, bf16[768,64]{1,0:T(8,128)(2,1)S(1)} %get-tuple-element.14.extra_t_ref, bf16[384,2048]{1,0:T(8,128)(2,1)} %collective-permute-done.8.weights_ref, ...), custom_call_target="tpu_custom_call" | custom-call | flops 503316480 | tf_op jit(solution)/shard_map/product_of_other/pallas_call | solution.py:217
  95.7 25.5 %all-gather = f32[256,128]{1,0:T(8,128)S(1)} all-gather(f32[32,128]{1,0:T(8,128)S(1)} %get-tuple-element.22), channel_id=2, replica_groups=mesh['zh'=4,'x'=8,'y'=8,'zl'=2,'core'=2] {'x'}, dimensions={0}, use_global_device_ids=true | all-gather | bytes 147456 | tf_op jit(solution)/shard_map/all_gather | solution.py:319
  121.2 15.6 %all-gather.1 = f32[32,4,1,128]{3,1,2,0:T(4,128)S(1)} all-gather(f32[8,4,1,128]{3,1,2,0:T(4,128)S(1)} %bitcast.49), channel_id=3, replica_groups=mesh['zh'=4,'x'=8,'y'=8,'zl'=2,'core'=2] {'zh'}, dimensions={0}, use_global_device_ids=true | all-gather | bytes 81920 | tf_op jit(solution)/shard_map/all_gather | solution.py:321
  138.0 2.5 %order.1 = bf16[320,768]{1,0:T(8,128)(2,1)} custom-call(s32[3]{0:T(128)S(1)} %pad_add_fusion.place_ref, bf16[384,256]{1,0:T(8,128)(2,1)S(1)} %get-tuple-element.17.own_main, bf16[384,64]{1,0:T(8,128)(2,1)S(1)} %get-tuple-element.18.own_extra, bf16[384,256]{1,0:T(8,128)(2,1)S(1)} %get-tuple-element.20.other_main, ...), custom_call_target="tpu_custom_call" | custom-call | flops 377487360 | bytes 983040 | tf_op jit(solution)/shard_map/order/pallas_call | solution.py:464
  140.6 3.4 %summed.1 = f32[24,2048]{1,0:T(8,128)} custom-call(bf16[16,24,2048]{2,1,0:T(8,128)(2,1)} %all-to-all-done.1.pieces_ref), custom_call_target="tpu_custom_call" | custom-call | flops 786432 | bytes 1572864 | tf_op jit(solution)/shard_map/summed/pallas_call | solution.py:356
  (46 shorter events, 11.0 us)
Async XLA Ops:
  0.6 8.7 %collective-permute-start = (bf16[24,2048]{1,0:T(8,128)(2,1)}, bf16[24,2048]{1,0:T(8,128)(2,1)S(1)}, u32[]{:S(2)}, u32[]{:S(2)}) collective-permute-start(bf16[24,2048]{1,0:T(8,128)(2,1)} %bitcast.33), channel_id=1, source_target_pairs={{0,2},{2,0},{1,3},{3,1},{4,6},{6,4},{5,7},{7,5},{8,10},{10,8},{9,1... | collective-permute-start | bytes 294920 | tf_op jit(solution)/shard_map/ppermute | solution.py:398
  10.6 20.6 %copy-start.1 = (bf16[1,24,2048]{2,1,0:T(8,128)(2,1)S(1)}, bf16[1,24,2048]{2,1,0:T(8,128)(2,1)}, u32[]{:S(2)}) copy-start(bf16[1,24,2048]{2,1,0:T(8,128)(2,1)} %param.13) | copy-start | bytes 294916
  10.6 50.0 %copy-start.6 = (bf16[1,1,32,10,768]{4,2,3,1,0:T(8,128)(2,1)S(1)}, bf16[1,1,32,10,768]{4,2,3,1,0:T(8,128)(2,1)}, u32[]{:S(2)}) copy-start(bf16[1,1,32,10,768]{4,2,3,1,0:T(8,128)(2,1)} %param.12) | copy-start | bytes 1474564
  10.6 55.6 %all-to-all-start = ((bf16[32,8,2560]{2,1,0:T(8,128)(2,1)}), bf16[32,8,2560]{2,1,0:T(8,128)(2,1)S(1)}, u32[]{:S(2)}, u32[]{:S(2)}) async-start(bf16[32,8,2560]{2,1,0:T(8,128)(2,1)} %bitcast.44), calls=%async_computation | async-start | bytes 2621440 | tf_op jit(solution)/shard_map/all_to_all | solution.py:431
  31.2 2.3 %copy-start = (bf16[2,24,2048]{2,1,0:T(8,128)(2,1)}, bf16[2,24,2048]{2,1,0:T(8,128)(2,1)S(1)}, u32[]{:S(2)}) copy-start(bf16[2,24,2048]{2,1,0:T(8,128)(2,1)S(1)} %paired.1.refs_0_) | copy-start | bytes 589828
  31.3 7.7 %collective-permute-start.1 = (bf16[2,24,2048]{2,1,0:T(8,128)(2,1)S(1)}, bf16[2,24,2048]{2,1,0:T(8,128)(2,1)S(1)}, u32[]{:S(2)}, u32[]{:S(2)}) collective-permute-start(bf16[2,24,2048]{2,1,0:T(8,128)(2,1)S(1)} %paired.1.refs_0_), channel_id=1, source_target_pairs={{0,28},{4,0},{8,4},{12,8},{16,12},{20,16},{24,20},{28,24},{1,29},{... | collective-permute-start | bytes 589832 | tf_op jit(solution)/shard_map/ppermute | solution.py:281
  33.5 9.9 %collective-permute-start.5 = (bf16[2,24,2048]{2,1,0:T(8,128)(2,1)S(1)}, bf16[2,24,2048]{2,1,0:T(8,128)(2,1)S(1)}, u32[]{:S(2)}, u32[]{:S(2)}) collective-permute-start(bf16[2,24,2048]{2,1,0:T(8,128)(2,1)S(1)} %paired.1.refs_0_), channel_id=1, source_target_pairs={{0,4},{4,8},{8,12},{12,16},{16,20},{20,24},{24,28},{28,0},{1,5},{5... | collective-permute-start | bytes 589832 | tf_op jit(solution)/shard_map/ppermute | solution.py:284
  39.0 21.6 %copy-start.7 = (bf16[2,24,2048]{2,1,0:T(8,128)(2,1)}, bf16[2,24,2048]{2,1,0:T(8,128)(2,1)S(1)}, u32[]{:S(2)}) copy-start(bf16[2,24,2048]{2,1,0:T(8,128)(2,1)S(1)} %collective-permute-done.1.refs_1_) | copy-start | bytes 589828
  39.0 7.6 %collective-permute-start.2 = (bf16[2,24,2048]{2,1,0:T(8,128)(2,1)S(1)}, bf16[2,24,2048]{2,1,0:T(8,128)(2,1)S(1)}, u32[]{:S(2)}, u32[]{:S(2)}) collective-permute-start(bf16[2,24,2048]{2,1,0:T(8,128)(2,1)S(1)} %collective-permute-done.1.refs_1_), channel_id=1, source_target_pairs={{0,28},{4,0},{8,4},{12,8},{16,12},{20,16},{24,20},{28,24},{1,29},{... | collective-permute-start | bytes 589832 | tf_op jit(solution)/shard_map/ppermute | solution.py:281
  43.5 3.0 %copy-start.8 = (bf16[2,24,2048]{2,1,0:T(8,128)(2,1)}, bf16[2,24,2048]{2,1,0:T(8,128)(2,1)S(1)}, u32[]{:S(2)}) copy-start(bf16[2,24,2048]{2,1,0:T(8,128)(2,1)S(1)} %collective-permute-done.5.refs_7_) | copy-start | bytes 589828
  43.5 8.8 %collective-permute-start.6 = (bf16[2,24,2048]{2,1,0:T(8,128)(2,1)S(1)}, bf16[2,24,2048]{2,1,0:T(8,128)(2,1)S(1)}, u32[]{:S(2)}, u32[]{:S(2)}) collective-permute-start(bf16[2,24,2048]{2,1,0:T(8,128)(2,1)S(1)} %collective-permute-done.5.refs_7_), channel_id=1, source_target_pairs={{0,4},{4,8},{8,12},{12,16},{16,20},{20,24},{24,28},{28,0},{1,5},{5... | collective-permute-start | bytes 589832 | tf_op jit(solution)/shard_map/ppermute | solution.py:284
  46.5 5.7 %copy-start.9 = (bf16[2,24,2048]{2,1,0:T(8,128)(2,1)}, bf16[2,24,2048]{2,1,0:T(8,128)(2,1)S(1)}, u32[]{:S(2)}) copy-start(bf16[2,24,2048]{2,1,0:T(8,128)(2,1)S(1)} %collective-permute-done.2.refs_2_) | copy-start | bytes 589828
  46.5 8.4 %collective-permute-start.3 = (bf16[2,24,2048]{2,1,0:T(8,128)(2,1)S(1)}, bf16[2,24,2048]{2,1,0:T(8,128)(2,1)S(1)}, u32[]{:S(2)}, u32[]{:S(2)}) collective-permute-start(bf16[2,24,2048]{2,1,0:T(8,128)(2,1)S(1)} %collective-permute-done.2.refs_2_), channel_id=1, source_target_pairs={{0,28},{4,0},{8,4},{12,8},{16,12},{20,16},{24,20},{28,24},{1,29},{... | collective-permute-start | bytes 589832 | tf_op jit(solution)/shard_map/ppermute | solution.py:281
  52.2 9.9 %copy-start.10 = (bf16[2,24,2048]{2,1,0:T(8,128)(2,1)}, bf16[2,24,2048]{2,1,0:T(8,128)(2,1)S(1)}, u32[]{:S(2)}) copy-start(bf16[2,24,2048]{2,1,0:T(8,128)(2,1)S(1)} %collective-permute-done.6.refs_6_) | copy-start | bytes 589828
  52.2 9.9 %collective-permute-start.7 = (bf16[2,24,2048]{2,1,0:T(8,128)(2,1)S(1)}, bf16[2,24,2048]{2,1,0:T(8,128)(2,1)S(1)}, u32[]{:S(2)}, u32[]{:S(2)}) collective-permute-start(bf16[2,24,2048]{2,1,0:T(8,128)(2,1)S(1)} %collective-permute-done.6.refs_6_), channel_id=1, source_target_pairs={{0,4},{4,8},{8,12},{12,16},{16,20},{20,24},{24,28},{28,0},{1,5},{5... | collective-permute-start | bytes 589832 | tf_op jit(solution)/shard_map/ppermute | solution.py:284
  54.9 7.2 %copy-start.11 = (bf16[2,24,2048]{2,1,0:T(8,128)(2,1)}, bf16[2,24,2048]{2,1,0:T(8,128)(2,1)S(1)}, u32[]{:S(2)}) copy-start(bf16[2,24,2048]{2,1,0:T(8,128)(2,1)S(1)} %collective-permute-done.3.refs_3_) | copy-start | bytes 589828
  54.9 8.8 %collective-permute-start.4 = (bf16[2,24,2048]{2,1,0:T(8,128)(2,1)S(1)}, bf16[2,24,2048]{2,1,0:T(8,128)(2,1)}, u32[]{:S(2)}, u32[]{:S(2)}) collective-permute-start(bf16[2,24,2048]{2,1,0:T(8,128)(2,1)S(1)} %collective-permute-done.3.refs_3_), channel_id=1, source_target_pairs={{0,28},{4,0},{8,4},{12,8},{16,12},{20,16},{24,20},{28,24},{1,29},{... | collective-permute-start | bytes 589832 | tf_op jit(solution)/shard_map/ppermute | solution.py:281
  69.1 5.5 %collective-permute-start.9 = (bf16[384,2048]{1,0:T(8,128)(2,1)}, bf16[384,2048]{1,0:T(8,128)(2,1)S(1)}, u32[]{:S(2)}, u32[]{:S(2)}) collective-permute-start(bf16[384,2048]{1,0:T(8,128)(2,1)} %half_sent.1), channel_id=1, source_target_pairs={{0,1},{1,0},{2,3},{3,2},{4,5},{5,4},{6,7},{7,6},{8,9},{9,8},{10,11... | collective-permute-start | bytes 4718600 | tf_op jit(solution)/shard_map/ppermute | solution.py:454
  77.5 63.1 %all-to-all-start.1 = ((bf16[16,24,2048]{2,1,0:T(8,128)(2,1)}), bf16[16,24,2048]{2,1,0:T(8,128)(2,1)}, u32[]{:S(2)}, u32[]{:S(2)}) async-start(bf16[16,24,2048]{2,1,0:T(8,128)(2,1)} %bitcast.45), calls=%async_computation.1 | async-start | bytes 3145728 | tf_op jit(solution)/shard_map/all_to_all | solution.py:456
  86.4 5.4 %collective-permute-start.8 = (bf16[384,2048]{1,0:T(8,128)(2,1)S(1)}, bf16[384,2048]{1,0:T(8,128)(2,1)}, u32[]{:S(2)}, u32[]{:S(2)}) collective-permute-start(bf16[384,2048]{1,0:T(8,128)(2,1)S(1)} %bitcast.31), channel_id=1, source_target_pairs={{0,1},{1,0},{2,3},{3,2},{4,5},{5,4},{6,7},{7,6},{8,9},{9,8},{10,11... | collective-permute-start | bytes 4718600 | tf_op jit(solution)/shard_map/ppermute | solution.py:437
  91.8 44.9 %copy-start.2 = (f32[128,8]{0,1:T(8,128)S(1)}, f32[128,8]{0,1:T(8,128)}, u32[]{:S(2)}) copy-start(f32[128,8]{0,1:T(8,128)} %param.8) | copy-start | bytes 12292
  91.8 45.0 %copy-start.3 = (s32[128,8]{0,1:T(8,128)S(1)}, s32[128,8]{0,1:T(8,128)}, u32[]{:S(2)}) copy-start(s32[128,8]{0,1:T(8,128)} %param.9) | copy-start | bytes 12292
  91.8 45.0 %copy-start.4 = (s32[128,8]{0,1:T(8,128)S(1)}, s32[128,8]{0,1:T(8,128)}, u32[]{:S(2)}) copy-start(s32[128,8]{0,1:T(8,128)} %param.10) | copy-start | bytes 12292
  91.8 45.0 %copy-start.5 = (f32[128,8]{0,1:T(8,128)S(1)}, f32[128,8]{0,1:T(8,128)}, u32[]{:S(2)}) copy-start(f32[128,8]{0,1:T(8,128)} %param.11) | copy-start | bytes 12292
  (1 other events, 0.7 us)

commit v6 on v5

--- a/solution.py
+++ b/solution.py
@@ -136,27 +136,19 @@
     units, width = held.shape
     part = width // FOLD
     span = slice(half * units, (half + 1) * units)
-
-    def copy_of(m):
-        cols = columns(m, part)
-        return pltpu.make_async_copy(held.at[:, cols], out_ref.at[:, cols], sems.at[m])
-
-    def step(m, carry):
-        cols = columns(m, part)
-        total = dot(main_t_ref[span, :], payload_ref[:, cols])
-        total = total + dot(extra_t_ref[span, :], unfolded(payload_ref[:, width:], m))
+    main_t, extra_t = main_t_ref[span, :], extra_t_ref[span, :]
+    fold = payload_ref[:, width:]
+    copies = []
+    for m in range(FOLD):
+        cols = slice(m * part, (m + 1) * part)
+        total = dot(main_t, payload_ref[:, cols]) + dot(extra_t, unfolded(fold, m))
         if adds:
             total = total + given[0][:, cols].astype(F32)
         held[:, cols] = total.astype(BF16)
-        copy_of(m).start()
-        return carry
-
-    def wait(m, carry):
-        copy_of(m).wait()
-        return carry
-
-    lax.fori_loop(0, FOLD, step, 0)
-    lax.fori_loop(0, FOLD, wait, 0)
+        copies.append(pltpu.make_async_copy(held.at[:, cols], out_ref.at[:, cols], sems.at[m]))
+        copies[-1].start()
+    for copy in copies:
+        copy.wait()
 
 
 def half_partial(main_t, extra_t, payload, half, arrived=None, first=()):
@@ -176,7 +168,7 @@
     )(main_t, extra_t, payload, *given, *first)
 
 
-def product_kernel(half, main_t_ref, extra_t_ref, weights_ref, payload_ref, *refs):
+def product_kernel(half, place_ref, main_t_ref, extra_t_ref, weights_ref, payload_ref, *refs):
     *given, main_ref, extra_ref, score_ref, acc_main, acc_extra = refs
     units, rows = main_ref.shape
     few = extra_ref.shape[1]
@@ -200,9 +192,9 @@
     span = slice(half * units, (half + 1) * units)
     main_score = jnp.sum(main * main_t_ref[span, :].astype(F32), axis=0, keepdims=True)
     extra_score = jnp.sum(extra * extra_t_ref[span, :].astype(F32), axis=0, keepdims=True)
-    to_main = iota((source, rows), 0) == iota((source, rows), 1) // 8
+    to_main = (iota((source, rows), 0) ^ place_ref[3]) == iota((source, rows), 1) // 8
     at_main = iota((rows, 128), 0) % 8 == iota((rows, 128), 1)
-    to_extra = iota((source, few), 0) == iota((source, few), 1) % source
+    to_extra = (iota((source, few), 0) ^ place_ref[3]) == iota((source, few), 1) % source
     at_extra = iota((few, 128), 0) // source + 8 == iota((few, 128), 1)
     score = exact_dot(jnp.where(to_main, main_score, 0.0), jnp.where(at_main, 1.0, 0.0))
     score = score + exact_dot(jnp.where(to_extra, extra_score, 0.0), jnp.where(at_extra, 1.0, 0.0))
@@ -211,12 +203,12 @@
     score_ref[...] = score
 
 
-def half_product(main_t, extra_t, weights, payload, half, *given):
+def half_product(place, main_t, extra_t, weights, payload, half, *given):
     units, rows = main_t.shape
     few = extra_t.shape[1]
     return pl.pallas_call(
         functools.partial(product_kernel, half),
-        in_specs=[VMEM] * (4 + len(given)),
+        in_specs=[SMEM] + [VMEM] * (4 + len(given)),
         out_specs=[VMEM] * 3,
         out_shape=[
             jax.ShapeDtypeStruct((units // 2, rows), BF16),
@@ -227,7 +219,7 @@
         compiler_params=PARAMS,
         cost_estimate=cost(units * (rows + few) * weights.shape[1], 0),
         name="product_of_other" if half else "product_of_own",
-    )(main_t, extra_t, weights, payload, *given)
+    )(place, main_t, extra_t, weights, payload, *given)
 
 
 def order_kernel(shard, place_ref, own_main, own_extra, other_main, other_extra, grad_ref):
@@ -313,14 +305,22 @@
     )(weights, beside, in_hbm(first))
 
 
-def returned_scores(blocks):
-    outer, inner = (lax.axis_size(k) for k in EXPERT)
-    lanes = blocks.shape[1]
-    row = lax.all_gather(blocks, "x").reshape(inner, outer, inner, lanes)
-    row = lax.dynamic_index_in_dim(row, lax.axis_index("x"), 2, keepdims=False)
-    square = lax.all_gather(row, "zh")
-    square = lax.dynamic_index_in_dim(square, lax.axis_index("zh"), 2, keepdims=False)
-    return square.reshape(outer * inner, lanes)
+def exchanged_by_bits(blocks):
+    count, lanes = blocks.shape
+    inner = lax.axis_size("x")
+    bit = 1
+    while bit < count:
+        axis, step = ("x", bit) if bit < inner else ("zh", bit // inner)
+        size = lax.axis_size(axis)
+        pairs = blocks.reshape(count // (2 * bit), 2, bit, lanes)
+        came = lax.ppermute(pairs[:, 1], axis, [(i, i ^ step) for i in range(size)])
+        blocks = jnp.stack([pairs[:, 0], came], axis=1).reshape(count, lanes)
+        bit *= 2
+    return blocks
+
+
+def in_vmem(array):
+    return pltpu.with_memory_space_constraint(array, pltpu.VMEM)
 
 
 def in_hbm(array):
@@ -365,7 +365,7 @@
     )(pieces)
 
 
-def logits_kernel(logits_ref, chosen_ref, slots_ref, outside_ref, score_ref, out_ref):
+def logits_kernel(place_ref, logits_ref, chosen_ref, slots_ref, outside_ref, score_ref, out_ref):
     gating = softmax_rows(logits_ref[...])
     sent = gating.astype(BF16).astype(F32)
     chosen, slots = chosen_ref[...], slots_ref[...]
@@ -373,8 +373,9 @@
     experts = score_ref.shape[0]
     returned = score_ref[...]
     found = []
+    here = chosen ^ place_ref[3]
     for k in range(topk):
-        hit = jnp.where(iota((experts, tokens), 0) == chosen[k : k + 1, :], 1.0, 0.0)
+        hit = jnp.where(iota((experts, tokens), 0) == here[k : k + 1, :], 1.0, 0.0)
         by_slot = exact_dot(returned, hit, 0, 0)[:16, :]
         at_slot = iota((16, tokens), 0) == slots[k : k + 1, :]
         found.append(jnp.sum(jnp.where(at_slot, by_slot, 0.0), axis=0, keepdims=True))
@@ -390,7 +391,7 @@
     window, capacity, units = hidden.shape[2], hidden.shape[3], hidden.shape[4]
     model = grad_output.shape[1]
     shard = down_weight.shape[1]
-    place = jnp.stack([lax.axis_index(k) for k in ("core", "y", "zl")]).astype(jnp.int32)
+    place = jnp.stack([lax.axis_index(k) for k in ("core", "y", "zl", EXPERT)]).astype(jnp.int32)
     logits_t, chosen_t, slots_t = logits.T, chosen.T, slots.T
     swap = [(0, 1), (1, 0)]
 
@@ -434,7 +435,7 @@
 
     own_weights = gathered(place, paired(weights, beside, packed))
     own_weights = own_weights.reshape(-1, model)
-    other_weights = lax.ppermute(own_weights, "core", swap)
+    other_weights = in_vmem(lax.ppermute(own_weights, "core", swap))
 
     by_slot = hidden.transpose(0, 1, 3, 2, 4).reshape(capacity * window, units)
     main_t, extra_t = pl.pallas_call(
@@ -452,15 +453,15 @@
 
     sent = half_partial(main_t, extra_t, payload, 1, first=(own_weights[:8, :128],))
     arrived = lax.ppermute(sent, "core", swap)
-    both = half_partial(main_t, extra_t, payload, 0, arrived)
+    *own_grad, score = half_product(place, main_t, extra_t, own_weights, payload, 0)
+    *other_grad, score = half_product(place, main_t, extra_t, other_weights, payload, 1, score)
+    both = half_partial(main_t, extra_t, payload, 0, arrived, first=(score,))
     parts = lax.all_to_all(
         both.reshape(-1, shard, model), RING, split_axis=0, concat_axis=0, tiled=True
     )
-    grad_down = summed(parts).reshape(1, shard, model)
-
-    *own_grad, score = half_product(main_t, extra_t, own_weights, payload, 0)
-    *other_grad, score = half_product(main_t, extra_t, other_weights, payload, 1, score)
-    returned = returned_scores(score)
+    grad_down = summed(in_vmem(parts)).reshape(1, shard, model)
+
+    returned = exchanged_by_bits(score)
     grad = pl.pallas_call(
         functools.partial(order_kernel, shard),
         in_specs=[SMEM] + [VMEM] * 4,
@@ -473,13 +474,13 @@
     grad_hidden = grad.reshape(1, 1, capacity, window, units).transpose(0, 1, 3, 2, 4)
     grad_logits = pl.pallas_call(
         logits_kernel,
-        in_specs=[VMEM] * 5,
+        in_specs=[SMEM] + [VMEM] * 5,
         out_specs=VMEM,
         out_shape=jax.ShapeDtypeStruct((topk, tokens), F32),
         compiler_params=PARAMS,
         cost_estimate=cost(0, 0),
         name="logits",
-    )(logits_t, chosen_t, slots_t, other_scores.T, returned)
+    )(place, logits_t, chosen_t, slots_t, other_scores.T, returned)
     return grad_hidden, grad_down, grad_logits.T
 
 

time: 145 us -> 138 us (0.952)
  the two profiles are of different devices: /device:TPU:20 before, /device:TPU:2 now
where the time goes in v6:
time: 138 us; the launch traced here: 137 us
  starting transfers between devices  89.1 us (65%)
  Pallas kernels  25.3 us (18%)
  waiting for transfers between devices  19.7 us (14%)
  local copies, waits for them, and re-layouts  1.4 us (1%)
    ppermute x5, starting transfers between devices, exchanged_by_bits(): came = lax.ppermute(pairs[:, 1], axis, [(i, i ^ step) for i in range(size)])  24.4 us
    ppermute x4, starting transfers between devices, gathered(): above = in_hbm(lax.ppermute(above, 'y', down))  22.9 us
    all_to_all x1, starting transfers between devices, body(): lax.all_to_all(packed.reshape(window, 8, packed.shape[1]), EXPERT, split_...  20.6 us
    ppermute x5, waiting for transfers between devices, exchanged_by_bits(): came = lax.ppermute(pairs[:, 1], axis, [(i, i ^ step) for i in range(size)])  15.1 us
    pallas_call x2, Pallas kernels, half_product(): pl.pallas_call(functools.partial(product_kernel, half), in_specs=[SMEM] +...  6.76 us
    all_to_all x1, starting transfers between devices, body(): lax.all_to_all(both.reshape(-1, shard, model), RING, split_axis=0, concat...  5.87 us
    ppermute x3, starting transfers between devices, gathered(): below = in_hbm(lax.ppermute(below, 'y', up))  5.76 us
    ppermute x1, starting transfers between devices, body(): beside = lax.ppermute(weights, 'zl', swap)  5.19 us
  transfers between devices with their start and end apart: 17, of which 9 were waited for; matrix products, arithmetic and copies ran while one was open for 0% of the time, Pallas kernels for 15%

profile of v6, /device:TPU:2, one launch (start us, length us, event | category | flops | bytes accessed | tf_op | source)
XLA Modules:
  0.0 136.7 jit_solution(5543028184983164430)
XLA Ops:
  0.6 5.2 %collective-permute-start = (bf16[24,2048]{1,0:T(8,128)(2,1)}, bf16[24,2048]{1,0:T(8,128)(2,1)S(1)}, u32[]{:S(2)}, u32[]{:S(2)}) collective-permute-start(bf16[24,2048]{1,0:T(8,128)(2,1)} %bitcast.55), channel_id=1, source_target_pairs={{0,2},{2,0},{1,3},{3,1},{4,6},{6,4},{5,7},{7,5},{8,10},{10,8},{9,1... | collective-permute-start | bytes 294920 | tf_op jit(solution)/shard_map/ppermute | solution.py:399
  6.8 2.6 %pack.1.array_ref = bf16[256,2560]{1,0:T(8,128)(2,1)} custom-call(bf16[256,128]{1,0:T(8,128)(2,1)S(1)} %get-tuple-element.15.place_ref, bf16[256,128]{1,0:T(8,128)(2,1)S(1)} %get-tuple-element.16.fold_ref, bf16[128,2048]{1,0:T(8,128)(2,1)} %rows_in.1), custom_call_target="tpu_custom_call" | custom-call | flops 335544320 | bytes 2621440 | tf_op jit(solution)/shard_map/pack/pallas_call | solution.py:417
  10.7 20.6 %all-to-all-start = ((bf16[32,8,2560]{2,1,0:T(8,128)(2,1)}), bf16[32,8,2560]{2,1,0:T(8,128)(2,1)S(1)}, u32[]{:S(2)}, u32[]{:S(2)}) async-start(bf16[32,8,2560]{2,1,0:T(8,128)(2,1)} %bitcast.67), calls=%async_computation | async-start | bytes 2621440 | tf_op jit(solution)/shard_map/all_to_all | solution.py:432
  31.3 6.2 %collective-permute-start.1 = (bf16[2,24,2048]{2,1,0:T(8,128)(2,1)S(1)}, bf16[2,24,2048]{2,1,0:T(8,128)(2,1)S(1)}, u32[]{:S(2)}, u32[]{:S(2)}) collective-permute-start(bf16[2,24,2048]{2,1,0:T(8,128)(2,1)S(1)} %paired.1.refs_0_), channel_id=1, source_target_pairs={{0,28},{4,0},{8,4},{12,8},{16,12},{20,16},{24,20},{28,24},{1,29},{... | collective-permute-start | bytes 589832 | tf_op jit(solution)/shard_map/ppermute | solution.py:273
  40.8 5.6 %collective-permute-start.2 = (bf16[2,24,2048]{2,1,0:T(8,128)(2,1)S(1)}, bf16[2,24,2048]{2,1,0:T(8,128)(2,1)S(1)}, u32[]{:S(2)}, u32[]{:S(2)}) collective-permute-start(bf16[2,24,2048]{2,1,0:T(8,128)(2,1)S(1)} %collective-permute-done.1.refs_1_), channel_id=1, source_target_pairs={{0,28},{4,0},{8,4},{12,8},{16,12},{20,16},{24,20},{28,24},{1,29},{... | collective-permute-start | bytes 589832 | tf_op jit(solution)/shard_map/ppermute | solution.py:273
  49.6 5.6 %collective-permute-start.3 = (bf16[2,24,2048]{2,1,0:T(8,128)(2,1)S(1)}, bf16[2,24,2048]{2,1,0:T(8,128)(2,1)S(1)}, u32[]{:S(2)}, u32[]{:S(2)}) collective-permute-start(bf16[2,24,2048]{2,1,0:T(8,128)(2,1)S(1)} %collective-permute-done.2.refs_2_), channel_id=1, source_target_pairs={{0,28},{4,0},{8,4},{12,8},{16,12},{20,16},{24,20},{28,24},{1,29},{... | collective-permute-start | bytes 589832 | tf_op jit(solution)/shard_map/ppermute | solution.py:273
  58.3 5.6 %collective-permute-start.4 = (bf16[2,24,2048]{2,1,0:T(8,128)(2,1)S(1)}, bf16[2,24,2048]{2,1,0:T(8,128)(2,1)}, u32[]{:S(2)}, u32[]{:S(2)}) collective-permute-start(bf16[2,24,2048]{2,1,0:T(8,128)(2,1)S(1)} %collective-permute-done.3.refs_3_), channel_id=1, source_target_pairs={{0,28},{4,0},{8,4},{12,8},{16,12},{20,16},{24,20},{28,24},{1,29},{... | collective-permute-start | bytes 589832 | tf_op jit(solution)/shard_map/ppermute | solution.py:273
  67.1 2.1 %placed.1 = bf16[16,24,2048]{2,1,0:T(8,128)(2,1)S(1)} custom-call(s32[4]{0:T(128)S(1)} %pad_add_fusion.place_ref, bf16[2,24,2048]{2,1,0:T(8,128)(2,1)} %copy-done, bf16[2,24,2048]{2,1,0:T(8,128)(2,1)} %copy-done.11, bf16[2,24,2048]{2,1,0:T(8,128)(2,1)} %copy-done.13, bf16[2,24,2048]{2,1,0:T(8,128)(2,1)} %copy-done.15, ...), custom_call_target="tpu_custom_call" | custom-call | tf_op jit(solution)/shard_map/placed/pallas_call | solution.py:278
  71.2 2.4 %half_sent.1 = bf16[384,2048]{1,0:T(8,128)(2,1)} custom-call(bf16[768,256]{1,0:T(8,128)(2,1)S(1)} %get-tuple-element.13.main_t_ref, bf16[768,64]{1,0:T(8,128)(2,1)S(1)} %get-tuple-element.14.extra_t_ref, bf16[256,2560]{1,0:T(8,128)(2,1)S(1)} %bitcast.48, bf16[8,128]{1,0:T(8,128)(2,1)S(1)} %slice.49.refs_0_), custom_call_target="tpu_custom_call" | custom-call | flops 503316480 | bytes 4718592 | tf_op jit(solution)/shard_map/half_sent/pallas_call | solution.py:159
  73.6 2.4 %collective-permute-start.9 = (bf16[384,2048]{1,0:T(8,128)(2,1)}, bf16[384,2048]{1,0:T(8,128)(2,1)S(1)}, u32[]{:S(2)}, u32[]{:S(2)}) collective-permute-start(bf16[384,2048]{1,0:T(8,128)(2,1)} %half_sent.1), channel_id=1, source_target_pairs={{0,1},{1,0},{2,3},{3,2},{4,5},{5,4},{6,7},{7,6},{8,9},{9,8},{10,11... | collective-permute-start | bytes 4718600 | tf_op jit(solution)/shard_map/ppermute | solution.py:455
  76.0 2.9 %product_of_own.1 = (bf16[384,256]{1,0:T(8,128)(2,1)S(1)}, bf16[384,64]{1,0:T(8,128)(2,1)S(1)}, f32[32,128]{1,0:T(8,128)S(1)}) custom-call(s32[4]{0:T(128)S(1)} %pad_add_fusion.place_ref, bf16[768,256]{1,0:T(8,128)(2,1)S(1)} %get-tuple-element.13.main_t_ref, bf16[768,64]{1,0:T(8,128)(2,1)S(1)} %get-tuple-element.14.extra_t_ref, ...), custom_call_target="tpu_custom_call" | custom-call | flops 503316480 | tf_op jit(solution)/shard_map/product_of_own/pallas_call | solution.py:209
  79.0 3.9 %product_of_other.1 = (bf16[384,256]{1,0:T(8,128)(2,1)S(1)}, bf16[384,64]{1,0:T(8,128)(2,1)S(1)}, f32[32,128]{1,0:T(8,128)S(1)}) custom-call(s32[4]{0:T(128)S(1)} %pad_add_fusion.place_ref, bf16[768,256]{1,0:T(8,128)(2,1)S(1)} %get-tuple-element.13.main_t_ref, bf16[768,64]{1,0:T(8,128)(2,1)S(1)} %get-tuple-element.14.extra_t_ref, ...), custom_call_target="tpu_custom_call" | custom-call | flops 503316480 | tf_op jit(solution)/shard_map/product_of_other/pallas_call | solution.py:209
  82.8 2.4 %half_kept.1 = bf16[384,2048]{1,0:T(8,128)(2,1)} custom-call(bf16[768,256]{1,0:T(8,128)(2,1)S(1)} %get-tuple-element.13.main_t_ref, bf16[768,64]{1,0:T(8,128)(2,1)S(1)} %get-tuple-element.14.extra_t_ref, bf16[256,2560]{1,0:T(8,128)(2,1)S(1)} %bitcast.51, bf16[384,2048]{1,0:T(8,128)(2,1)S(1)} %collective-permute-done.9.refs_0_, ...), custom_call_target="tpu_custom_call" | custom-call | flops 503316480 | bytes 4718592 | tf_op jit(solution)/shard_map/half_kept/pallas_call | solution.py:159
  85.3 5.9 %all-to-all-start.1 = ((bf16[16,24,2048]{2,1,0:T(8,128)(2,1)}), bf16[16,24,2048]{2,1,0:T(8,128)(2,1)S(1)}, u32[]{:S(2)}, u32[]{:S(2)}) async-start(bf16[16,24,2048]{2,1,0:T(8,128)(2,1)} %bitcast.68), calls=%async_computation.1 | async-start | bytes 3145728 | tf_op jit(solution)/shard_map/all_to_all | solution.py:459
  93.4 3.4 %collective-permute-done.10 = f32[16,1,128]{2,0,1:T(8,128)S(1)} collective-permute-done((f32[16,1,128]{2,0,1:T(8,128)S(1)}, f32[16,1,128]{2,0,1:T(8,128)S(1)}, u32[]{:S(2)}, u32[]{:S(2)}) %collective-permute-start.10) | collective-permute-done | bytes 8224 | tf_op jit(solution)/shard_map/ppermute | solution.py:316
  96.8 4.3 %collective-permute-start.11 = (f32[8,2,128]{2,0,1:T(8,128)S(1)}, f32[8,2,128]{2,0,1:T(8,128)S(1)}, u32[]{:S(2)}, u32[]{:S(2)}) collective-permute-start(f32[8,2,128]{2,0,1:T(8,128)S(1)} %bitcast.77), channel_id=1, source_target_pairs={{0,64},{32,96},{64,0},{96,32},{128,192},{160,224},{192,128},{224,1... | collective-permute-start | bytes 24584 | tf_op jit(solution)/shard_map/ppermute | solution.py:316
  101.1 2.2 %collective-permute-done.11 = f32[8,2,128]{2,0,1:T(8,128)S(1)} collective-permute-done((f32[8,2,128]{2,0,1:T(8,128)S(1)}, f32[8,2,128]{2,0,1:T(8,128)S(1)}, u32[]{:S(2)}, u32[]{:S(2)}) %collective-permute-start.11) | collective-permute-done | bytes 8224 | tf_op jit(solution)/shard_map/ppermute | solution.py:316
  103.3 6.5 %collective-permute-start.12 = (f32[4,4,128]{2,0,1:T(4,128)S(1)}, f32[4,4,128]{2,0,1:T(4,128)S(1)}, u32[]{:S(2)}, u32[]{:S(2)}) collective-permute-start(f32[4,4,128]{2,0,1:T(4,128)S(1)} %bitcast.80), channel_id=1, source_target_pairs={{0,128},{32,160},{64,192},{96,224},{128,0},{160,32},{192,64},{224,... | collective-permute-start | bytes 24584 | tf_op jit(solution)/shard_map/ppermute | solution.py:316
  109.7 3.0 %collective-permute-done.12 = f32[4,4,128]{2,0,1:T(4,128)S(1)} collective-permute-done((f32[4,4,128]{2,0,1:T(4,128)S(1)}, f32[4,4,128]{2,0,1:T(4,128)S(1)}, u32[]{:S(2)}, u32[]{:S(2)}) %collective-permute-start.12) | collective-permute-done | bytes 8224 | tf_op jit(solution)/shard_map/ppermute | solution.py:316
  112.7 4.3 %collective-permute-start.13 = (f32[2,8,128]{2,1,0:T(8,128)S(1)}, f32[2,8,128]{2,1,0:T(8,128)S(1)}, u32[]{:S(2)}, u32[]{:S(2)}) collective-permute-start(f32[2,8,128]{2,1,0:T(8,128)S(1)} %get-tuple-element.26), channel_id=1, source_target_pairs={{0,256},{256,0},{512,768},{768,512},{1,257},{257,1},{513,769},{769... | collective-permute-start | bytes 24584 | tf_op jit(solution)/shard_map/ppermute | solution.py:316
  117.0 2.3 %collective-permute-done.13 = f32[2,8,128]{2,1,0:T(8,128)S(1)} collective-permute-done((f32[2,8,128]{2,1,0:T(8,128)S(1)}, f32[2,8,128]{2,1,0:T(8,128)S(1)}, u32[]{:S(2)}, u32[]{:S(2)}) %collective-permute-start.13) | collective-permute-done | bytes 8224 | tf_op jit(solution)/shard_map/ppermute | solution.py:316
  119.3 7.3 %collective-permute-start.14 = (f32[1,16,128]{2,1,0:T(8,128)S(1)}, f32[1,16,128]{2,1,0:T(8,128)S(1)}, u32[]{:S(2)}, u32[]{:S(2)}) collective-permute-start(f32[1,16,128]{2,1,0:T(8,128)S(1)} %get-tuple-element.24), channel_id=1, source_target_pairs={{0,512},{256,768},{512,0},{768,256},{1,513},{257,769},{513,1},{769... | collective-permute-start | bytes 24584 | tf_op jit(solution)/shard_map/ppermute | solution.py:316
  126.6 2.5 %order.1 = bf16[320,768]{1,0:T(8,128)(2,1)} custom-call(s32[4]{0:T(128)S(1)} %pad_add_fusion.place_ref, bf16[384,256]{1,0:T(8,128)(2,1)S(1)} %copy-done.8, bf16[384,64]{1,0:T(8,128)(2,1)S(1)} %copy-done.10, bf16[384,256]{1,0:T(8,128)(2,1)S(1)} %get-tuple-element.20.other_main, bf16[384,64]{1,0:T(8,128)(2,1)S(1)} %get-tuple-element.21.other_extra), custom_call_target="tpu_custom_call" | custom-call | flops 377487360 | bytes 983040 | tf_op jit(solution)/shard_map/order/pallas_call | solution.py:465
  129.2 4.2 %collective-permute-done.14 = f32[1,16,128]{2,1,0:T(8,128)S(1)} collective-permute-done((f32[1,16,128]{2,1,0:T(8,128)S(1)}, f32[1,16,128]{2,1,0:T(8,128)S(1)}, u32[]{:S(2)}, u32[]{:S(2)}) %collective-permute-start.14) | collective-permute-done | bytes 8224 | tf_op jit(solution)/shard_map/ppermute | solution.py:316
  (70 shorter events, 22.5 us)
Async XLA Ops:
  0.6 8.7 %collective-permute-start = (bf16[24,2048]{1,0:T(8,128)(2,1)}, bf16[24,2048]{1,0:T(8,128)(2,1)S(1)}, u32[]{:S(2)}, u32[]{:S(2)}) collective-permute-start(bf16[24,2048]{1,0:T(8,128)(2,1)} %bitcast.55), channel_id=1, source_target_pairs={{0,2},{2,0},{1,3},{3,1},{4,6},{6,4},{5,7},{7,5},{8,10},{10,8},{9,1... | collective-permute-start | bytes 294920 | tf_op jit(solution)/shard_map/ppermute | solution.py:399
  10.6 53.4 %copy-start.6 = (bf16[1,1,32,10,768]{4,2,3,1,0:T(8,128)(2,1)S(1)}, bf16[1,1,32,10,768]{4,2,3,1,0:T(8,128)(2,1)}, u32[]{:S(2)}) copy-start(bf16[1,1,32,10,768]{4,2,3,1,0:T(8,128)(2,1)} %param.12) | copy-start | bytes 1474564
  10.7 60.5 %all-to-all-start = ((bf16[32,8,2560]{2,1,0:T(8,128)(2,1)}), bf16[32,8,2560]{2,1,0:T(8,128)(2,1)S(1)}, u32[]{:S(2)}, u32[]{:S(2)}) async-start(bf16[32,8,2560]{2,1,0:T(8,128)(2,1)} %bitcast.67), calls=%async_computation | async-start | bytes 2621440 | tf_op jit(solution)/shard_map/all_to_all | solution.py:432
  31.3 9.5 %collective-permute-start.1 = (bf16[2,24,2048]{2,1,0:T(8,128)(2,1)S(1)}, bf16[2,24,2048]{2,1,0:T(8,128)(2,1)S(1)}, u32[]{:S(2)}, u32[]{:S(2)}) collective-permute-start(bf16[2,24,2048]{2,1,0:T(8,128)(2,1)S(1)} %paired.1.refs_0_), channel_id=1, source_target_pairs={{0,28},{4,0},{8,4},{12,8},{16,12},{20,16},{24,20},{28,24},{1,29},{... | collective-permute-start | bytes 589832 | tf_op jit(solution)/shard_map/ppermute | solution.py:273
  37.5 8.9 %collective-permute-start.5 = (bf16[2,24,2048]{2,1,0:T(8,128)(2,1)S(1)}, bf16[2,24,2048]{2,1,0:T(8,128)(2,1)S(1)}, u32[]{:S(2)}, u32[]{:S(2)}) collective-permute-start(bf16[2,24,2048]{2,1,0:T(8,128)(2,1)S(1)} %paired.1.refs_0_), channel_id=1, source_target_pairs={{0,4},{4,8},{8,12},{12,16},{16,20},{20,24},{24,28},{28,0},{1,5},{5... | collective-permute-start | bytes 589832 | tf_op jit(solution)/shard_map/ppermute | solution.py:276
  40.8 8.8 %collective-permute-start.2 = (bf16[2,24,2048]{2,1,0:T(8,128)(2,1)S(1)}, bf16[2,24,2048]{2,1,0:T(8,128)(2,1)S(1)}, u32[]{:S(2)}, u32[]{:S(2)}) collective-permute-start(bf16[2,24,2048]{2,1,0:T(8,128)(2,1)S(1)} %collective-permute-done.1.refs_1_), channel_id=1, source_target_pairs={{0,28},{4,0},{8,4},{12,8},{16,12},{20,16},{24,20},{28,24},{1,29},{... | collective-permute-start | bytes 589832 | tf_op jit(solution)/shard_map/ppermute | solution.py:273
  46.4 8.8 %collective-permute-start.6 = (bf16[2,24,2048]{2,1,0:T(8,128)(2,1)S(1)}, bf16[2,24,2048]{2,1,0:T(8,128)(2,1)S(1)}, u32[]{:S(2)}, u32[]{:S(2)}) collective-permute-start(bf16[2,24,2048]{2,1,0:T(8,128)(2,1)S(1)} %collective-permute-done.5.refs_7_), channel_id=1, source_target_pairs={{0,4},{4,8},{8,12},{12,16},{16,20},{20,24},{24,28},{28,0},{1,5},{5... | collective-permute-start | bytes 589832 | tf_op jit(solution)/shard_map/ppermute | solution.py:276
  49.6 8.8 %collective-permute-start.3 = (bf16[2,24,2048]{2,1,0:T(8,128)(2,1)S(1)}, bf16[2,24,2048]{2,1,0:T(8,128)(2,1)S(1)}, u32[]{:S(2)}, u32[]{:S(2)}) collective-permute-start(bf16[2,24,2048]{2,1,0:T(8,128)(2,1)S(1)} %collective-permute-done.2.refs_2_), channel_id=1, source_target_pairs={{0,28},{4,0},{8,4},{12,8},{16,12},{20,16},{24,20},{28,24},{1,29},{... | collective-permute-start | bytes 589832 | tf_op jit(solution)/shard_map/ppermute | solution.py:273
  55.2 10.3 %collective-permute-start.7 = (bf16[2,24,2048]{2,1,0:T(8,128)(2,1)S(1)}, bf16[2,24,2048]{2,1,0:T(8,128)(2,1)S(1)}, u32[]{:S(2)}, u32[]{:S(2)}) collective-permute-start(bf16[2,24,2048]{2,1,0:T(8,128)(2,1)S(1)} %collective-permute-done.6.refs_6_), channel_id=1, source_target_pairs={{0,4},{4,8},{8,12},{12,16},{16,20},{20,24},{24,28},{28,0},{1,5},{5... | collective-permute-start | bytes 589832 | tf_op jit(solution)/shard_map/ppermute | solution.py:276
  58.3 8.8 %collective-permute-start.4 = (bf16[2,24,2048]{2,1,0:T(8,128)(2,1)S(1)}, bf16[2,24,2048]{2,1,0:T(8,128)(2,1)}, u32[]{:S(2)}, u32[]{:S(2)}) collective-permute-start(bf16[2,24,2048]{2,1,0:T(8,128)(2,1)S(1)} %collective-permute-done.3.refs_3_), channel_id=1, source_target_pairs={{0,28},{4,0},{8,4},{12,8},{16,12},{20,16},{24,20},{28,24},{1,29},{... | collective-permute-start | bytes 589832 | tf_op jit(solution)/shard_map/ppermute | solution.py:273
  69.2 9.7 %collective-permute-start.8 = (bf16[384,2048]{1,0:T(8,128)(2,1)S(1)}, bf16[384,2048]{1,0:T(8,128)(2,1)}, u32[]{:S(2)}, u32[]{:S(2)}) collective-permute-start(bf16[384,2048]{1,0:T(8,128)(2,1)S(1)} %bitcast.52), channel_id=1, source_target_pairs={{0,1},{1,0},{2,3},{3,2},{4,5},{5,4},{6,7},{7,6},{8,9},{9,8},{10,11... | collective-permute-start | bytes 4718600 | tf_op jit(solution)/shard_map/ppermute | solution.py:438
  73.6 9.2 %collective-permute-start.9 = (bf16[384,2048]{1,0:T(8,128)(2,1)}, bf16[384,2048]{1,0:T(8,128)(2,1)S(1)}, u32[]{:S(2)}, u32[]{:S(2)}) collective-permute-start(bf16[384,2048]{1,0:T(8,128)(2,1)} %half_sent.1), channel_id=1, source_target_pairs={{0,1},{1,0},{2,3},{3,2},{4,5},{5,4},{6,7},{7,6},{8,9},{9,8},{10,11... | collective-permute-start | bytes 4718600 | tf_op jit(solution)/shard_map/ppermute | solution.py:455
  85.2 41.4 %copy-start.8 = (bf16[384,256]{1,0:T(8,128)(2,1)S(1)}, bf16[384,256]{1,0:T(8,128)(2,1)}, u32[]{:S(2)}) copy-start(bf16[384,256]{1,0:T(8,128)(2,1)} %copy-done.7) | copy-start | bytes 589828
  85.3 41.4 %copy-start.10 = (bf16[384,64]{1,0:T(8,128)(2,1)S(1)}, bf16[384,64]{1,0:T(8,128)(2,1)}, u32[]{:S(2)}) copy-start(bf16[384,64]{1,0:T(8,128)(2,1)} %copy-done.9) | copy-start | bytes 147460
  85.3 49.9 %all-to-all-start.1 = ((bf16[16,24,2048]{2,1,0:T(8,128)(2,1)}), bf16[16,24,2048]{2,1,0:T(8,128)(2,1)S(1)}, u32[]{:S(2)}, u32[]{:S(2)}) async-start(bf16[16,24,2048]{2,1,0:T(8,128)(2,1)} %bitcast.68), calls=%async_computation.1 | async-start | bytes 3145728 | tf_op jit(solution)/shard_map/all_to_all | solution.py:459
  91.2 42.2 %copy-start.2 = (f32[128,8]{0,1:T(8,128)S(1)}, f32[128,8]{0,1:T(8,128)}, u32[]{:S(2)}) copy-start(f32[128,8]{0,1:T(8,128)} %param.8) | copy-start | bytes 12292
  91.2 42.2 %copy-start.3 = (s32[128,8]{0,1:T(8,128)S(1)}, s32[128,8]{0,1:T(8,128)}, u32[]{:S(2)}) copy-start(s32[128,8]{0,1:T(8,128)} %param.9) | copy-start | bytes 12292
  91.2 42.2 %copy-start.4 = (s32[128,8]{0,1:T(8,128)S(1)}, s32[128,8]{0,1:T(8,128)}, u32[]{:S(2)}) copy-start(s32[128,8]{0,1:T(8,128)} %param.10) | copy-start | bytes 12292
  91.2 42.2 %copy-start.5 = (f32[128,8]{0,1:T(8,128)S(1)}, f32[128,8]{0,1:T(8,128)}, u32[]{:S(2)}) copy-start(f32[128,8]{0,1:T(8,128)} %param.11) | copy-start | bytes 12292
  91.2 5.5 %collective-permute-start.10 = (f32[16,1,128]{2,0,1:T(8,128)S(1)}, f32[16,1,128]{2,0,1:T(8,128)S(1)}, u32[]{:S(2)}, u32[]{:S(2)}) collective-permute-start(f32[16,1,128]{2,0,1:T(8,128)S(1)} %bitcast.78), channel_id=1, source_target_pairs={{0,32},{32,0},{64,96},{96,64},{128,160},{160,128},{192,224},{224,1... | collective-permute-start | bytes 24584 | tf_op jit(solution)/shard_map/ppermute | solution.py:316
  96.8 6.4 %collective-permute-start.11 = (f32[8,2,128]{2,0,1:T(8,128)S(1)}, f32[8,2,128]{2,0,1:T(8,128)S(1)}, u32[]{:S(2)}, u32[]{:S(2)}) collective-permute-start(f32[8,2,128]{2,0,1:T(8,128)S(1)} %bitcast.77), channel_id=1, source_target_pairs={{0,64},{32,96},{64,0},{96,32},{128,192},{160,224},{192,128},{224,1... | collective-permute-start | bytes 24584 | tf_op jit(solution)/shard_map/ppermute | solution.py:316
  103.3 9.5 %collective-permute-start.12 = (f32[4,4,128]{2,0,1:T(4,128)S(1)}, f32[4,4,128]{2,0,1:T(4,128)S(1)}, u32[]{:S(2)}, u32[]{:S(2)}) collective-permute-start(f32[4,4,128]{2,0,1:T(4,128)S(1)} %bitcast.80), channel_id=1, source_target_pairs={{0,128},{32,160},{64,192},{96,224},{128,0},{160,32},{192,64},{224,... | collective-permute-start | bytes 24584 | tf_op jit(solution)/shard_map/ppermute | solution.py:316
  112.7 6.6 %collective-permute-start.13 = (f32[2,8,128]{2,1,0:T(8,128)S(1)}, f32[2,8,128]{2,1,0:T(8,128)S(1)}, u32[]{:S(2)}, u32[]{:S(2)}) collective-permute-start(f32[2,8,128]{2,1,0:T(8,128)S(1)} %get-tuple-element.26), channel_id=1, source_target_pairs={{0,256},{256,0},{512,768},{768,512},{1,257},{257,1},{513,769},{769... | collective-permute-start | bytes 24584 | tf_op jit(solution)/shard_map/ppermute | solution.py:316
  119.3 14.1 %collective-permute-start.14 = (f32[1,16,128]{2,1,0:T(8,128)S(1)}, f32[1,16,128]{2,1,0:T(8,128)S(1)}, u32[]{:S(2)}, u32[]{:S(2)}) collective-permute-start(f32[1,16,128]{2,1,0:T(8,128)S(1)} %get-tuple-element.24), channel_id=1, source_target_pairs={{0,512},{256,768},{512,0},{768,256},{1,513},{257,769},{513,1},{769... | collective-permute-start | bytes 24584 | tf_op jit(solution)/shard_map/ppermute | solution.py:316
  (10 other events, 86.4 us)

commit v7 on v6

--- a/solution.py
+++ b/solution.py
@@ -169,7 +169,7 @@
 
 
 def product_kernel(half, place_ref, main_t_ref, extra_t_ref, weights_ref, payload_ref, *refs):
-    *given, main_ref, extra_ref, score_ref, acc_main, acc_extra = refs
+    *given, main_ref, extra_ref, score_ref, acc_main, acc_extra = refs[: len(refs) - 2 * half]
     units, rows = main_ref.shape
     few = extra_ref.shape[1]
     source = rows // 8
@@ -177,14 +177,26 @@
     part = width // FOLD
     acc_main[...] = jnp.zeros_like(acc_main)
     acc_extra[...] = jnp.zeros_like(acc_extra)
+    source_ref = weights_ref
+    if half:
+        weights_ref, sems = refs[-2:]
+
+    def copy_of(m):
+        cols = columns(m, part)
+        return pltpu.make_async_copy(source_ref.at[:, cols], weights_ref.at[:, cols], sems.at[m])
 
     def step(m, carry):
         cols = columns(m, part)
+        if half:
+            copy_of(m).wait()
         weights = weights_ref[:, cols]
         acc_main[...] += dot(weights, payload_ref[:, cols], 1, 1)
         acc_extra[...] += dot(weights, unfolded(payload_ref[:, width:], m), 1, 1)
         return carry
 
+    if half:
+        for m in range(FOLD):
+            copy_of(m).start()
     lax.fori_loop(0, FOLD, step, 0)
     main, extra = acc_main[...], acc_extra[...]
     main_ref[...] = main.astype(BF16)
@@ -208,14 +220,15 @@
     few = extra_t.shape[1]
     return pl.pallas_call(
         functools.partial(product_kernel, half),
-        in_specs=[SMEM] + [VMEM] * (4 + len(given)),
+        in_specs=[SMEM, VMEM, VMEM, HBM if half else VMEM, VMEM] + [VMEM] * len(given),
         out_specs=[VMEM] * 3,
         out_shape=[
             jax.ShapeDtypeStruct((units // 2, rows), BF16),
             jax.ShapeDtypeStruct((units // 2, few), BF16),
             jax.ShapeDtypeStruct((rows // 8, 128), F32),
         ],
-        scratch_shapes=[pltpu.VMEM((units // 2, rows), F32), pltpu.VMEM((units // 2, few), F32)],
+        scratch_shapes=[pltpu.VMEM((units // 2, rows), F32), pltpu.VMEM((units // 2, few), F32)]
+        + [pltpu.VMEM(weights.shape, BF16), pltpu.SemaphoreType.DMA((FOLD,))][: 2 * half],
         compiler_params=PARAMS,
         cost_estimate=cost(units * (rows + few) * weights.shape[1], 0),
         name="product_of_other" if half else "product_of_own",
@@ -254,7 +267,7 @@
     count = len(pieces)
     copies = []
     for k, piece in enumerate(pieces):
-        base = lax.rem(place_ref[1] + k, count) * 2
+        base = lax.rem(place_ref[1] + (1 - 2 * place_ref[0]) * k + count, count) * 2
         for t in range(2):
             spot = base + (place_ref[2] ^ t)
             copies.append(pltpu.make_async_copy(piece.at[t], out_ref.at[spot], sems.at[2 * k + t]))
@@ -264,17 +277,23 @@
 
 
 def gathered(place, pair):
-    size = lax.axis_size("y")
-    down = [(i, (i + size - 1) % size) for i in range(size)]
-    up = [(i, (i + 1) % size) for i in range(size)]
-    above = below = pair = in_hbm(pair)
+    size, cores = lax.axis_size("y"), lax.axis_size("core")
+
+    def moves(step):
+        return [
+            (y * cores + core, (y + (step if core else -step)) % size * cores + core)
+            for y in range(size)
+            for core in range(cores)
+        ]
+
+    first = second = pair = in_hbm(pair)
     pieces = [pair] + [None] * (size - 1)
     for k in range(1, size // 2 + 1):
-        above = in_hbm(lax.ppermute(above, "y", down))
-        pieces[k] = above
+        first = in_hbm(lax.ppermute(first, ("y", "core"), moves(1)))
+        pieces[k] = first
         if k < size - k:
-            below = in_hbm(lax.ppermute(below, "y", up))
-            pieces[size - k] = below
+            second = in_hbm(lax.ppermute(second, ("y", "core"), moves(-1)))
+            pieces[size - k] = second
     placed = pl.pallas_call(
         placed_kernel,
         in_specs=[SMEM] + [HBM] * size,
@@ -288,21 +307,28 @@
     return placed
 
 
-def pair_kernel(weights_ref, beside_ref, first_ref, out_ref):
-    out_ref[0] = weights_ref[...]
-    out_ref[1] = beside_ref[...]
+def pair_kernel(weights_ref, beside_ref, first_ref, out_ref, sems):
+    copies = [
+        pltpu.make_async_copy(piece, out_ref.at[k], sems.at[k])
+        for k, piece in enumerate((weights_ref, beside_ref))
+    ]
+    for copy in copies:
+        copy.start()
+    for copy in copies:
+        copy.wait()
 
 
 def paired(weights, beside, first):
     return pl.pallas_call(
         pair_kernel,
-        in_specs=[VMEM, VMEM, HBM],
+        in_specs=[HBM, HBM, HBM],
         out_specs=VMEM,
         out_shape=jax.ShapeDtypeStruct((2, *weights.shape), weights.dtype),
+        scratch_shapes=[pltpu.SemaphoreType.DMA((2,))],
         compiler_params=PARAMS,
         cost_estimate=cost(0, 0),
         name="paired",
-    )(weights, beside, in_hbm(first))
+    )(in_hbm(weights), beside, in_hbm(first))
 
 
 def exchanged_by_bits(blocks):
@@ -330,7 +356,7 @@
 def after(array, first):
     return pl.pallas_call(
         after_kernel,
-        in_specs=[HBM, VMEM],
+        in_specs=[HBM, HBM],
         out_specs=HBM,
         out_shape=pltpu.HBM(array.shape, array.dtype),
         input_output_aliases={0: 0},
@@ -358,25 +384,27 @@
         grid=(4,),
         in_specs=[pl.BlockSpec((count, shard, part), lambda g: (0, 0, g))],
         out_specs=pl.BlockSpec((shard, part), lambda g: (0, g)),
-        out_shape=jax.ShapeDtypeStruct((shard, width), F32),
+        out_shape=pltpu.HBM((shard, width), F32),
         compiler_params=PARAMS,
         cost_estimate=cost(count * shard * width, 2 * count * shard * width),
         name="summed",
     )(pieces)
 
 
-def logits_kernel(place_ref, logits_ref, chosen_ref, slots_ref, outside_ref, score_ref, out_ref):
+def logits_kernel(
+    place_ref, logits_ref, chosen_ref, slots_ref, outside_ref, score_ref, first_ref, out_ref
+):
     gating = softmax_rows(logits_ref[...])
     sent = gating.astype(BF16).astype(F32)
     chosen, slots = chosen_ref[...], slots_ref[...]
     topk, tokens = chosen.shape
     experts = score_ref.shape[0]
-    returned = score_ref[...]
+    returned = score_ref[:, :16]
     found = []
     here = chosen ^ place_ref[3]
     for k in range(topk):
         hit = jnp.where(iota((experts, tokens), 0) == here[k : k + 1, :], 1.0, 0.0)
-        by_slot = exact_dot(returned, hit, 0, 0)[:16, :]
+        by_slot = exact_dot(returned, hit, 0, 0)
         at_slot = iota((16, tokens), 0) == slots[k : k + 1, :]
         found.append(jnp.sum(jnp.where(at_slot, by_slot, 0.0), axis=0, keepdims=True))
     inside = jnp.concatenate(found, axis=0) / sent
@@ -396,7 +424,7 @@
     swap = [(0, 1), (1, 0)]
 
     weights = down_weight.reshape(shard, model)
-    beside = lax.ppermute(weights, "zl", swap)
+    beside = in_hbm(lax.ppermute(weights, "zl", swap))
     tile = jax.ShapeDtypeStruct((window * 8, tokens), BF16)
     placing = pl.pallas_call(
         place_kernel,
@@ -428,14 +456,14 @@
         cost_estimate=cost(2 * 320 * tokens * model * 2, 4 * 320 * model),
         name="pack",
     )(*placing, in_hbm(grad_output))
-    packed = after(packed, beside[:8, :128])
+    packed = after(packed, beside)
     payload = lax.all_to_all(
         packed.reshape(window, 8, packed.shape[1]), EXPERT, split_axis=0, concat_axis=0, tiled=True
     ).reshape(packed.shape)
 
     own_weights = gathered(place, paired(weights, beside, packed))
     own_weights = own_weights.reshape(-1, model)
-    other_weights = in_vmem(lax.ppermute(own_weights, "core", swap))
+    other_weights = in_hbm(lax.ppermute(own_weights, "core", swap))
 
     by_slot = hidden.transpose(0, 1, 3, 2, 4).reshape(capacity * window, units)
     main_t, extra_t = pl.pallas_call(
@@ -459,7 +487,8 @@
     parts = lax.all_to_all(
         both.reshape(-1, shard, model), RING, split_axis=0, concat_axis=0, tiled=True
     )
-    grad_down = summed(in_vmem(parts)).reshape(1, shard, model)
+    total = summed(in_vmem(parts))
+    grad_down = total.reshape(1, shard, model)
 
     returned = exchanged_by_bits(score)
     grad = pl.pallas_call(
@@ -474,13 +503,13 @@
     grad_hidden = grad.reshape(1, 1, capacity, window, units).transpose(0, 1, 3, 2, 4)
     grad_logits = pl.pallas_call(
         logits_kernel,
-        in_specs=[SMEM] + [VMEM] * 5,
+        in_specs=[SMEM] + [VMEM] * 5 + [HBM],
         out_specs=VMEM,
         out_shape=jax.ShapeDtypeStruct((topk, tokens), F32),
         compiler_params=PARAMS,
         cost_estimate=cost(0, 0),
         name="logits",
-    )(place, logits_t, chosen_t, slots_t, other_scores.T, returned)
+    )(place, logits_t, chosen_t, slots_t, other_scores.T, returned, in_hbm(total))
     return grad_hidden, grad_down, grad_logits.T
 
 

time: 138 us -> 141 us (1.022)
  waiting for transfers between devices: 19.7 us -> 23.2 us
    ppermute x9, waiting for transfers between devices: 4.66 us -> 8.24 us  [the longest x4 8.15 us: gathered(): first = in_hbm(lax.ppermute(first, ('y', 'core'), moves(1)))]
  transfers between devices with their start and end apart: 17 -> 17, of which waited for: 9 -> 10; matrix products, arithmetic and copies ran while one was open for 0% -> 0% of each run, Pallas kernels for 15% -> 14%
where the time goes in v7:
time: 141 us; the launch traced here: 140 us
  starting transfers between devices  88.9 us (63%)
  Pallas kernels  25.3 us (18%)
  waiting for transfers between devices  23.2 us (16%)
  local copies, waits for them, and re-layouts  1.45 us (1%)
    ppermute x5, starting transfers between devices, exchanged_by_bits(): came = lax.ppermute(pairs[:, 1], axis, [(i, i ^ step) for i in range(size)])  24.6 us
    ppermute x4, starting transfers between devices, gathered(): first = in_hbm(lax.ppermute(first, ('y', 'core'), moves(1)))  22.9 us
    all_to_all x1, starting transfers between devices, body(): lax.all_to_all(packed.reshape(window, 8, packed.shape[1]), EXPERT, split_...  20.6 us
    ppermute x5, waiting for transfers between devices, exchanged_by_bits(): came = lax.ppermute(pairs[:, 1], axis, [(i, i ^ step) for i in range(size)])  14.9 us
    ppermute x4, waiting for transfers between devices, gathered(): first = in_hbm(lax.ppermute(first, ('y', 'core'), moves(1)))  8.15 us
    pallas_call x2, Pallas kernels, half_product(): pl.pallas_call(functools.partial(product_kernel, half), in_specs=[SMEM, V...  6.8 us
    ppermute x3, starting transfers between devices, gathered(): second = in_hbm(lax.ppermute(second, ('y', 'core'), moves(-1)))  5.75 us
    all_to_all x1, starting transfers between devices, body(): lax.all_to_all(both.reshape(-1, shard, model), RING, split_axis=0, concat...  5.59 us
  transfers between devices with their start and end apart: 17, of which 10 were waited for; matrix products, arithmetic and copies ran while one was open for 0% of the time, Pallas kernels for 14%

profile of v7, /device:TPU:2, one launch (start us, length us, event | category | flops | bytes accessed | tf_op | source)
XLA Modules:
  0.0 140.0 jit_solution(1234052320243089881)
XLA Ops:
  0.6 5.2 %collective-permute-start = (bf16[24,2048]{1,0:T(8,128)(2,1)}, bf16[24,2048]{1,0:T(8,128)(2,1)S(1)}, u32[]{:S(2)}, u32[]{:S(2)}) collective-permute-start(bf16[24,2048]{1,0:T(8,128)(2,1)} %bitcast.68), channel_id=1, source_target_pairs={{0,2},{2,0},{1,3},{3,1},{4,6},{6,4},{5,7},{7,5},{8,10},{10,8},{9,1... | collective-permute-start | bytes 294920 | tf_op jit(solution)/shard_map/ppermute | solution.py:427
  6.8 2.6 %pack.1.array_ref = bf16[256,2560]{1,0:T(8,128)(2,1)} custom-call(bf16[256,128]{1,0:T(8,128)(2,1)S(1)} %get-tuple-element.15.place_ref, bf16[256,128]{1,0:T(8,128)(2,1)S(1)} %get-tuple-element.16.fold_ref, bf16[128,2048]{1,0:T(8,128)(2,1)} %rows_in.1), custom_call_target="tpu_custom_call" | custom-call | flops 335544320 | bytes 2621440 | tf_op jit(solution)/shard_map/pack/pallas_call | solution.py:445
  10.0 20.6 %all-to-all-start = ((bf16[32,8,2560]{2,1,0:T(8,128)(2,1)}), bf16[32,8,2560]{2,1,0:T(8,128)(2,1)S(1)}, u32[]{:S(2)}, u32[]{:S(2)}) async-start(bf16[32,8,2560]{2,1,0:T(8,128)(2,1)} %bitcast.65), calls=%async_computation | async-start | bytes 2621440 | tf_op jit(solution)/shard_map/all_to_all | solution.py:460
  31.6 6.2 %collective-permute-start.1 = (bf16[2,24,2048]{2,1,0:T(8,128)(2,1)S(1)}, bf16[2,24,2048]{2,1,0:T(8,128)(2,1)S(1)}, u32[]{:S(2)}, u32[]{:S(2)}) collective-permute-start(bf16[2,24,2048]{2,1,0:T(8,128)(2,1)S(1)} %paired.1.refs_0_), channel_id=1, source_target_pairs={{0,28},{1,5},{4,0},{5,9},{8,4},{9,13},{12,8},{13,17},{16,12},{17,2... | collective-permute-start | bytes 589832 | tf_op jit(solution)/shard_map/ppermute | solution.py:292
  39.7 3.3 %collective-permute-done.1.refs_1_ = bf16[2,24,2048]{2,1,0:T(8,128)(2,1)S(1)} collective-permute-done((bf16[2,24,2048]{2,1,0:T(8,128)(2,1)S(1)}, bf16[2,24,2048]{2,1,0:T(8,128)(2,1)S(1)}, u32[]{:S(2)}, u32[]{:S(2)}) %collective-permute-start.1) | collective-permute-done | bytes 196640 | tf_op jit(solution)/shard_map/ppermute | solution.py:292
  43.1 5.6 %collective-permute-start.2 = (bf16[2,24,2048]{2,1,0:T(8,128)(2,1)S(1)}, bf16[2,24,2048]{2,1,0:T(8,128)(2,1)S(1)}, u32[]{:S(2)}, u32[]{:S(2)}) collective-permute-start(bf16[2,24,2048]{2,1,0:T(8,128)(2,1)S(1)} %collective-permute-done.1.refs_1_), channel_id=1, source_target_pairs={{0,28},{1,5},{4,0},{5,9},{8,4},{9,13},{12,8},{13,17},{16,12},{17,2... | collective-permute-start | bytes 589832 | tf_op jit(solution)/shard_map/ppermute | solution.py:292
  50.6 2.4 %collective-permute-done.2.refs_2_ = bf16[2,24,2048]{2,1,0:T(8,128)(2,1)S(1)} collective-permute-done((bf16[2,24,2048]{2,1,0:T(8,128)(2,1)S(1)}, bf16[2,24,2048]{2,1,0:T(8,128)(2,1)S(1)}, u32[]{:S(2)}, u32[]{:S(2)}) %collective-permute-start.2) | collective-permute-done | bytes 196640 | tf_op jit(solution)/shard_map/ppermute | solution.py:292
  53.0 5.6 %collective-permute-start.3 = (bf16[2,24,2048]{2,1,0:T(8,128)(2,1)S(1)}, bf16[2,24,2048]{2,1,0:T(8,128)(2,1)S(1)}, u32[]{:S(2)}, u32[]{:S(2)}) collective-permute-start(bf16[2,24,2048]{2,1,0:T(8,128)(2,1)S(1)} %collective-permute-done.2.refs_2_), channel_id=1, source_target_pairs={{0,28},{1,5},{4,0},{5,9},{8,4},{9,13},{12,8},{13,17},{16,12},{17,2... | collective-permute-start | bytes 589832 | tf_op jit(solution)/shard_map/ppermute | solution.py:292
  62.2 5.6 %collective-permute-start.4 = (bf16[2,24,2048]{2,1,0:T(8,128)(2,1)S(1)}, bf16[2,24,2048]{2,1,0:T(8,128)(2,1)}, u32[]{:S(2)}, u32[]{:S(2)}) collective-permute-start(bf16[2,24,2048]{2,1,0:T(8,128)(2,1)S(1)} %collective-permute-done.3.refs_3_), channel_id=1, source_target_pairs={{0,28},{1,5},{4,0},{5,9},{8,4},{9,13},{12,8},{13,17},{16,12},{17,2... | collective-permute-start | bytes 589832 | tf_op jit(solution)/shard_map/ppermute | solution.py:292
  75.1 2.4 %half_sent.1 = bf16[384,2048]{1,0:T(8,128)(2,1)} custom-call(bf16[768,256]{1,0:T(8,128)(2,1)S(1)} %get-tuple-element.13.main_t_ref, bf16[768,64]{1,0:T(8,128)(2,1)S(1)} %get-tuple-element.14.extra_t_ref, bf16[256,2560]{1,0:T(8,128)(2,1)S(1)} %bitcast.48, bf16[8,128]{1,0:T(8,128)(2,1)S(1)} %slice.44.refs_0_), custom_call_target="tpu_custom_call" | custom-call | flops 503316480 | bytes 4718592 | tf_op jit(solution)/shard_map/half_sent/pallas_call | solution.py:159
  77.5 2.4 %collective-permute-start.9 = (bf16[384,2048]{1,0:T(8,128)(2,1)}, bf16[384,2048]{1,0:T(8,128)(2,1)S(1)}, u32[]{:S(2)}, u32[]{:S(2)}) collective-permute-start(bf16[384,2048]{1,0:T(8,128)(2,1)} %half_sent.1), channel_id=1, source_target_pairs={{0,1},{1,0},{2,3},{3,2},{4,5},{5,4},{6,7},{7,6},{8,9},{9,8},{10,11... | collective-permute-start | bytes 4718600 | tf_op jit(solution)/shard_map/ppermute | solution.py:483
  79.9 2.9 %product_of_own.1 = (bf16[384,256]{1,0:T(8,128)(2,1)S(1)}, bf16[384,64]{1,0:T(8,128)(2,1)S(1)}, f32[32,128]{1,0:T(8,128)S(1)}) custom-call(s32[4]{0:T(128)S(1)} %pad_add_fusion.place_ref, bf16[768,256]{1,0:T(8,128)(2,1)S(1)} %get-tuple-element.13.main_t_ref, bf16[768,64]{1,0:T(8,128)(2,1)S(1)} %get-tuple-element.14.extra_t_ref, ...), custom_call_target="tpu_custom_call" | custom-call | flops 503316480 | tf_op jit(solution)/shard_map/product_of_own/pallas_call | solution.py:221
  82.8 3.9 %product_of_other.1 = (bf16[384,256]{1,0:T(8,128)(2,1)S(1)}, bf16[384,64]{1,0:T(8,128)(2,1)S(1)}, f32[32,128]{1,0:T(8,128)S(1)}) custom-call(s32[4]{0:T(128)S(1)} %pad_add_fusion.place_ref, bf16[768,256]{1,0:T(8,128)(2,1)S(1)} %get-tuple-element.13.main_t_ref, bf16[768,64]{1,0:T(8,128)(2,1)S(1)} %get-tuple-element.14.extra_t_ref, ...), custom_call_target="tpu_custom_call" | custom-call | flops 503316480 | tf_op jit(solution)/shard_map/product_of_other/pallas_call | solution.py:221
  86.8 2.4 %half_kept.1 = bf16[384,2048]{1,0:T(8,128)(2,1)} custom-call(bf16[768,256]{1,0:T(8,128)(2,1)S(1)} %get-tuple-element.13.main_t_ref, bf16[768,64]{1,0:T(8,128)(2,1)S(1)} %get-tuple-element.14.extra_t_ref, bf16[256,2560]{1,0:T(8,128)(2,1)S(1)} %bitcast.51, bf16[384,2048]{1,0:T(8,128)(2,1)S(1)} %collective-permute-done.9.refs_0_, ...), custom_call_target="tpu_custom_call" | custom-call | flops 503316480 | bytes 4718592 | tf_op jit(solution)/shard_map/half_kept/pallas_call | solution.py:159
  89.2 5.6 %all-to-all-start.1 = ((bf16[16,24,2048]{2,1,0:T(8,128)(2,1)}), bf16[16,24,2048]{2,1,0:T(8,128)(2,1)S(1)}, u32[]{:S(2)}, u32[]{:S(2)}) async-start(bf16[16,24,2048]{2,1,0:T(8,128)(2,1)} %bitcast.66), calls=%async_computation.1 | async-start | bytes 3145728 | tf_op jit(solution)/shard_map/all_to_all | solution.py:487
  94.8 2.4 %collective-permute-start.10 = (f32[16,1,128]{2,0,1:T(8,128)S(1)}, f32[16,1,128]{2,0,1:T(8,128)S(1)}, u32[]{:S(2)}, u32[]{:S(2)}) collective-permute-start(f32[16,1,128]{2,0,1:T(8,128)S(1)} %bitcast.78), channel_id=1, source_target_pairs={{0,32},{32,0},{64,96},{96,64},{128,160},{160,128},{192,224},{224,1... | collective-permute-start | bytes 24584 | tf_op jit(solution)/shard_map/ppermute | solution.py:342
  97.2 3.2 %collective-permute-done.10 = f32[16,1,128]{2,0,1:T(8,128)S(1)} collective-permute-done((f32[16,1,128]{2,0,1:T(8,128)S(1)}, f32[16,1,128]{2,0,1:T(8,128)S(1)}, u32[]{:S(2)}, u32[]{:S(2)}) %collective-permute-start.10) | collective-permute-done | bytes 8224 | tf_op jit(solution)/shard_map/ppermute | solution.py:342
  100.4 4.3 %collective-permute-start.11 = (f32[8,2,128]{2,0,1:T(8,128)S(1)}, f32[8,2,128]{2,0,1:T(8,128)S(1)}, u32[]{:S(2)}, u32[]{:S(2)}) collective-permute-start(f32[8,2,128]{2,0,1:T(8,128)S(1)} %bitcast.77), channel_id=1, source_target_pairs={{0,64},{32,96},{64,0},{96,32},{128,192},{160,224},{192,128},{224,1... | collective-permute-start | bytes 24584 | tf_op jit(solution)/shard_map/ppermute | solution.py:342
  106.8 6.4 %collective-permute-start.12 = (f32[4,4,128]{2,0,1:T(4,128)S(1)}, f32[4,4,128]{2,0,1:T(4,128)S(1)}, u32[]{:S(2)}, u32[]{:S(2)}) collective-permute-start(f32[4,4,128]{2,0,1:T(4,128)S(1)} %bitcast.80), channel_id=1, source_target_pairs={{0,128},{32,160},{64,192},{96,224},{128,0},{160,32},{192,64},{224,... | collective-permute-start | bytes 24584 | tf_op jit(solution)/shard_map/ppermute | solution.py:342
  113.2 3.1 %collective-permute-done.12 = f32[4,4,128]{2,0,1:T(4,128)S(1)} collective-permute-done((f32[4,4,128]{2,0,1:T(4,128)S(1)}, f32[4,4,128]{2,0,1:T(4,128)S(1)}, u32[]{:S(2)}, u32[]{:S(2)}) %collective-permute-start.12) | collective-permute-done | bytes 8224 | tf_op jit(solution)/shard_map/ppermute | solution.py:342
  116.3 4.3 %collective-permute-start.13 = (f32[2,8,128]{2,1,0:T(8,128)S(1)}, f32[2,8,128]{2,1,0:T(8,128)S(1)}, u32[]{:S(2)}, u32[]{:S(2)}) collective-permute-start(f32[2,8,128]{2,1,0:T(8,128)S(1)} %get-tuple-element.26), channel_id=1, source_target_pairs={{0,256},{256,0},{512,768},{768,512},{1,257},{257,1},{513,769},{769... | collective-permute-start | bytes 24584 | tf_op jit(solution)/shard_map/ppermute | solution.py:342
  122.9 7.3 %collective-permute-start.14 = (f32[1,16,128]{2,1,0:T(8,128)S(1)}, f32[1,16,128]{2,1,0:T(8,128)S(1)}, u32[]{:S(2)}, u32[]{:S(2)}) collective-permute-start(f32[1,16,128]{2,1,0:T(8,128)S(1)} %get-tuple-element.24), channel_id=1, source_target_pairs={{0,512},{256,768},{512,0},{768,256},{1,513},{257,769},{513,1},{769... | collective-permute-start | bytes 24584 | tf_op jit(solution)/shard_map/ppermute | solution.py:342
  130.2 2.5 %order.1 = bf16[320,768]{1,0:T(8,128)(2,1)} custom-call(s32[4]{0:T(128)S(1)} %pad_add_fusion.place_ref, bf16[384,256]{1,0:T(8,128)(2,1)S(1)} %copy-done.7, bf16[384,64]{1,0:T(8,128)(2,1)S(1)} %copy-done.9, bf16[384,256]{1,0:T(8,128)(2,1)S(1)} %get-tuple-element.20.other_main, bf16[384,64]{1,0:T(8,128)(2,1)S(1)} %get-tuple-element.21.other_extra), custom_call_target="tpu_custom_call" | custom-call | flops 377487360 | bytes 983040 | tf_op jit(solution)/shard_map/order/pallas_call | solution.py:494
  132.8 4.2 %collective-permute-done.14 = f32[1,16,128]{2,1,0:T(8,128)S(1)} collective-permute-done((f32[1,16,128]{2,1,0:T(8,128)S(1)}, f32[1,16,128]{2,1,0:T(8,128)S(1)}, u32[]{:S(2)}, u32[]{:S(2)}) %collective-permute-start.14) | collective-permute-done | bytes 8224 | tf_op jit(solution)/shard_map/ppermute | solution.py:342
  (69 shorter events, 24.8 us)
Async XLA Ops:
  0.6 8.7 %collective-permute-start = (bf16[24,2048]{1,0:T(8,128)(2,1)}, bf16[24,2048]{1,0:T(8,128)(2,1)S(1)}, u32[]{:S(2)}, u32[]{:S(2)}) collective-permute-start(bf16[24,2048]{1,0:T(8,128)(2,1)} %bitcast.68), channel_id=1, source_target_pairs={{0,2},{2,0},{1,3},{3,1},{4,6},{6,4},{5,7},{7,5},{8,10},{10,8},{9,1... | collective-permute-start | bytes 294920 | tf_op jit(solution)/shard_map/ppermute | solution.py:427
  10.0 57.8 %copy-start.5 = (bf16[1,1,32,10,768]{4,2,3,1,0:T(8,128)(2,1)S(1)}, bf16[1,1,32,10,768]{4,2,3,1,0:T(8,128)(2,1)}, u32[]{:S(2)}) copy-start(bf16[1,1,32,10,768]{4,2,3,1,0:T(8,128)(2,1)} %param.12) | copy-start | bytes 1474564
  10.0 65.0 %all-to-all-start = ((bf16[32,8,2560]{2,1,0:T(8,128)(2,1)}), bf16[32,8,2560]{2,1,0:T(8,128)(2,1)S(1)}, u32[]{:S(2)}, u32[]{:S(2)}) async-start(bf16[32,8,2560]{2,1,0:T(8,128)(2,1)} %bitcast.65), calls=%async_computation | async-start | bytes 2621440 | tf_op jit(solution)/shard_map/all_to_all | solution.py:460
  31.6 11.4 %collective-permute-start.1 = (bf16[2,24,2048]{2,1,0:T(8,128)(2,1)S(1)}, bf16[2,24,2048]{2,1,0:T(8,128)(2,1)S(1)}, u32[]{:S(2)}, u32[]{:S(2)}) collective-permute-start(bf16[2,24,2048]{2,1,0:T(8,128)(2,1)S(1)} %paired.1.refs_0_), channel_id=1, source_target_pairs={{0,28},{1,5},{4,0},{5,9},{8,4},{9,13},{12,8},{13,17},{16,12},{17,2... | collective-permute-start | bytes 589832 | tf_op jit(solution)/shard_map/ppermute | solution.py:292
  37.8 10.8 %collective-permute-start.5 = (bf16[2,24,2048]{2,1,0:T(8,128)(2,1)S(1)}, bf16[2,24,2048]{2,1,0:T(8,128)(2,1)S(1)}, u32[]{:S(2)}, u32[]{:S(2)}) collective-permute-start(bf16[2,24,2048]{2,1,0:T(8,128)(2,1)S(1)} %paired.1.refs_0_), channel_id=1, source_target_pairs={{0,4},{1,29},{4,8},{5,1},{8,12},{9,5},{12,16},{13,9},{16,20},{17,1... | collective-permute-start | bytes 589832 | tf_op jit(solution)/shard_map/ppermute | solution.py:295
  43.1 10.0 %collective-permute-start.2 = (bf16[2,24,2048]{2,1,0:T(8,128)(2,1)S(1)}, bf16[2,24,2048]{2,1,0:T(8,128)(2,1)S(1)}, u32[]{:S(2)}, u32[]{:S(2)}) collective-permute-start(bf16[2,24,2048]{2,1,0:T(8,128)(2,1)S(1)} %collective-permute-done.1.refs_1_), channel_id=1, source_target_pairs={{0,28},{1,5},{4,0},{5,9},{8,4},{9,13},{12,8},{13,17},{16,12},{17,2... | collective-permute-start | bytes 589832 | tf_op jit(solution)/shard_map/ppermute | solution.py:292
  48.7 10.0 %collective-permute-start.6 = (bf16[2,24,2048]{2,1,0:T(8,128)(2,1)S(1)}, bf16[2,24,2048]{2,1,0:T(8,128)(2,1)S(1)}, u32[]{:S(2)}, u32[]{:S(2)}) collective-permute-start(bf16[2,24,2048]{2,1,0:T(8,128)(2,1)S(1)} %collective-permute-done.5.refs_7_), channel_id=1, source_target_pairs={{0,4},{1,29},{4,8},{5,1},{8,12},{9,5},{12,16},{13,9},{16,20},{17,1... | collective-permute-start | bytes 589832 | tf_op jit(solution)/shard_map/ppermute | solution.py:295
  53.0 9.1 %collective-permute-start.3 = (bf16[2,24,2048]{2,1,0:T(8,128)(2,1)S(1)}, bf16[2,24,2048]{2,1,0:T(8,128)(2,1)S(1)}, u32[]{:S(2)}, u32[]{:S(2)}) collective-permute-start(bf16[2,24,2048]{2,1,0:T(8,128)(2,1)S(1)} %collective-permute-done.2.refs_2_), channel_id=1, source_target_pairs={{0,28},{1,5},{4,0},{5,9},{8,4},{9,13},{12,8},{13,17},{16,12},{17,2... | collective-permute-start | bytes 589832 | tf_op jit(solution)/shard_map/ppermute | solution.py:292
  58.7 10.7 %copy-start.14 = (bf16[2,24,2048]{2,1,0:T(8,128)(2,1)}, bf16[2,24,2048]{2,1,0:T(8,128)(2,1)S(1)}, u32[]{:S(2)}) copy-start(bf16[2,24,2048]{2,1,0:T(8,128)(2,1)S(1)} %collective-permute-done.6.refs_6_) | copy-start | bytes 589828
  58.7 10.7 %collective-permute-start.7 = (bf16[2,24,2048]{2,1,0:T(8,128)(2,1)S(1)}, bf16[2,24,2048]{2,1,0:T(8,128)(2,1)S(1)}, u32[]{:S(2)}, u32[]{:S(2)}) collective-permute-start(bf16[2,24,2048]{2,1,0:T(8,128)(2,1)S(1)} %collective-permute-done.6.refs_6_), channel_id=1, source_target_pairs={{0,4},{1,29},{4,8},{5,1},{8,12},{9,5},{12,16},{13,9},{16,20},{17,1... | collective-permute-start | bytes 589832 | tf_op jit(solution)/shard_map/ppermute | solution.py:295
  62.2 8.8 %collective-permute-start.4 = (bf16[2,24,2048]{2,1,0:T(8,128)(2,1)S(1)}, bf16[2,24,2048]{2,1,0:T(8,128)(2,1)}, u32[]{:S(2)}, u32[]{:S(2)}) collective-permute-start(bf16[2,24,2048]{2,1,0:T(8,128)(2,1)S(1)} %collective-permute-done.3.refs_3_), channel_id=1, source_target_pairs={{0,28},{1,5},{4,0},{5,9},{8,4},{9,13},{12,8},{13,17},{16,12},{17,2... | collective-permute-start | bytes 589832 | tf_op jit(solution)/shard_map/ppermute | solution.py:292
  73.1 9.7 %collective-permute-start.8 = (bf16[384,2048]{1,0:T(8,128)(2,1)S(1)}, bf16[384,2048]{1,0:T(8,128)(2,1)}, u32[]{:S(2)}, u32[]{:S(2)}) collective-permute-start(bf16[384,2048]{1,0:T(8,128)(2,1)S(1)} %bitcast.52), channel_id=1, source_target_pairs={{0,1},{1,0},{2,3},{3,2},{4,5},{5,4},{6,7},{7,6},{8,9},{9,8},{10,11... | collective-permute-start | bytes 4718600 | tf_op jit(solution)/shard_map/ppermute | solution.py:466
  77.5 9.3 %collective-permute-start.9 = (bf16[384,2048]{1,0:T(8,128)(2,1)}, bf16[384,2048]{1,0:T(8,128)(2,1)S(1)}, u32[]{:S(2)}, u32[]{:S(2)}) collective-permute-start(bf16[384,2048]{1,0:T(8,128)(2,1)} %half_sent.1), channel_id=1, source_target_pairs={{0,1},{1,0},{2,3},{3,2},{4,5},{5,4},{6,7},{7,6},{8,9},{9,8},{10,11... | collective-permute-start | bytes 4718600 | tf_op jit(solution)/shard_map/ppermute | solution.py:483
  89.1 41.0 %copy-start.7 = (bf16[384,256]{1,0:T(8,128)(2,1)S(1)}, bf16[384,256]{1,0:T(8,128)(2,1)}, u32[]{:S(2)}) copy-start(bf16[384,256]{1,0:T(8,128)(2,1)} %copy-done.6) | copy-start | bytes 589828
  89.2 41.0 %copy-start.9 = (bf16[384,64]{1,0:T(8,128)(2,1)S(1)}, bf16[384,64]{1,0:T(8,128)(2,1)}, u32[]{:S(2)}) copy-start(bf16[384,64]{1,0:T(8,128)(2,1)} %copy-done.8) | copy-start | bytes 147460
  89.2 47.8 %all-to-all-start.1 = ((bf16[16,24,2048]{2,1,0:T(8,128)(2,1)}), bf16[16,24,2048]{2,1,0:T(8,128)(2,1)S(1)}, u32[]{:S(2)}, u32[]{:S(2)}) async-start(bf16[16,24,2048]{2,1,0:T(8,128)(2,1)} %bitcast.66), calls=%async_computation.1 | async-start | bytes 3145728 | tf_op jit(solution)/shard_map/all_to_all | solution.py:487
  94.8 5.5 %collective-permute-start.10 = (f32[16,1,128]{2,0,1:T(8,128)S(1)}, f32[16,1,128]{2,0,1:T(8,128)S(1)}, u32[]{:S(2)}, u32[]{:S(2)}) collective-permute-start(f32[16,1,128]{2,0,1:T(8,128)S(1)} %bitcast.78), channel_id=1, source_target_pairs={{0,32},{32,0},{64,96},{96,64},{128,160},{160,128},{192,224},{224,1... | collective-permute-start | bytes 24584 | tf_op jit(solution)/shard_map/ppermute | solution.py:342
  100.4 6.4 %collective-permute-start.11 = (f32[8,2,128]{2,0,1:T(8,128)S(1)}, f32[8,2,128]{2,0,1:T(8,128)S(1)}, u32[]{:S(2)}, u32[]{:S(2)}) collective-permute-start(f32[8,2,128]{2,0,1:T(8,128)S(1)} %bitcast.77), channel_id=1, source_target_pairs={{0,64},{32,96},{64,0},{96,32},{128,192},{160,224},{192,128},{224,1... | collective-permute-start | bytes 24584 | tf_op jit(solution)/shard_map/ppermute | solution.py:342
  106.8 9.5 %collective-permute-start.12 = (f32[4,4,128]{2,0,1:T(4,128)S(1)}, f32[4,4,128]{2,0,1:T(4,128)S(1)}, u32[]{:S(2)}, u32[]{:S(2)}) collective-permute-start(f32[4,4,128]{2,0,1:T(4,128)S(1)} %bitcast.80), channel_id=1, source_target_pairs={{0,128},{32,160},{64,192},{96,224},{128,0},{160,32},{192,64},{224,... | collective-permute-start | bytes 24584 | tf_op jit(solution)/shard_map/ppermute | solution.py:342
  116.3 6.6 %collective-permute-start.13 = (f32[2,8,128]{2,1,0:T(8,128)S(1)}, f32[2,8,128]{2,1,0:T(8,128)S(1)}, u32[]{:S(2)}, u32[]{:S(2)}) collective-permute-start(f32[2,8,128]{2,1,0:T(8,128)S(1)} %get-tuple-element.26), channel_id=1, source_target_pairs={{0,256},{256,0},{512,768},{768,512},{1,257},{257,1},{513,769},{769... | collective-permute-start | bytes 24584 | tf_op jit(solution)/shard_map/ppermute | solution.py:342
  122.9 14.1 %collective-permute-start.14 = (f32[1,16,128]{2,1,0:T(8,128)S(1)}, f32[1,16,128]{2,1,0:T(8,128)S(1)}, u32[]{:S(2)}, u32[]{:S(2)}) collective-permute-start(f32[1,16,128]{2,1,0:T(8,128)S(1)} %get-tuple-element.24), channel_id=1, source_target_pairs={{0,512},{256,768},{512,0},{768,256},{1,513},{257,769},{513,1},{769... | collective-permute-start | bytes 24584 | tf_op jit(solution)/shard_map/ppermute | solution.py:342
  130.2 8.3 %copy-start.1 = (f32[128,8]{0,1:T(8,128)S(1)}, f32[128,8]{0,1:T(8,128)}, u32[]{:S(2)}) copy-start(f32[128,8]{0,1:T(8,128)} %param.8) | copy-start | bytes 12292
  130.2 8.3 %copy-start.2 = (s32[128,8]{0,1:T(8,128)S(1)}, s32[128,8]{0,1:T(8,128)}, u32[]{:S(2)}) copy-start(s32[128,8]{0,1:T(8,128)} %param.9) | copy-start | bytes 12292
  130.2 8.3 %copy-start.3 = (s32[128,8]{0,1:T(8,128)S(1)}, s32[128,8]{0,1:T(8,128)}, u32[]{:S(2)}) copy-start(s32[128,8]{0,1:T(8,128)} %param.10) | copy-start | bytes 12292
  (10 other events, 46.6 us)

commit v8 on v6

--- a/solution.py
+++ b/solution.py
@@ -371,12 +371,12 @@
     chosen, slots = chosen_ref[...], slots_ref[...]
     topk, tokens = chosen.shape
     experts = score_ref.shape[0]
-    returned = score_ref[...]
+    returned = score_ref[:, :16]
     found = []
     here = chosen ^ place_ref[3]
     for k in range(topk):
         hit = jnp.where(iota((experts, tokens), 0) == here[k : k + 1, :], 1.0, 0.0)
-        by_slot = exact_dot(returned, hit, 0, 0)[:16, :]
+        by_slot = exact_dot(returned, hit, 0, 0)
         at_slot = iota((16, tokens), 0) == slots[k : k + 1, :]
         found.append(jnp.sum(jnp.where(at_slot, by_slot, 0.0), axis=0, keepdims=True))
     inside = jnp.concatenate(found, axis=0) / sent

time: 138 us -> 137 us (level)
  no operation moved by 1% of the time
where the time goes in v8:
time: 137 us; the launch traced here: 136 us
  starting transfers between devices  89.1 us (65%)
  Pallas kernels  25 us (18%)
  waiting for transfers between devices  19.7 us (14%)
  local copies, waits for them, and re-layouts  1.4 us (1%)
    ppermute x5, starting transfers between devices, exchanged_by_bits(): came = lax.ppermute(pairs[:, 1], axis, [(i, i ^ step) for i in range(size)])  24.4 us
    ppermute x4, starting transfers between devices, gathered(): above = in_hbm(lax.ppermute(above, 'y', down))  22.9 us
    all_to_all x1, starting transfers between devices, body(): lax.all_to_all(packed.reshape(window, 8, packed.shape[1]), EXPERT, split_...  20.6 us
    ppermute x5, waiting for transfers between devices, exchanged_by_bits(): came = lax.ppermute(pairs[:, 1], axis, [(i, i ^ step) for i in range(size)])  15.1 us
    pallas_call x2, Pallas kernels, half_product(): pl.pallas_call(functools.partial(product_kernel, half), in_specs=[SMEM] +...  6.76 us
    all_to_all x1, starting transfers between devices, body(): lax.all_to_all(both.reshape(-1, shard, model), RING, split_axis=0, concat...  5.87 us
    ppermute x3, starting transfers between devices, gathered(): below = in_hbm(lax.ppermute(below, 'y', up))  5.76 us
    ppermute x1, starting transfers between devices, body(): beside = lax.ppermute(weights, 'zl', swap)  5.19 us
  transfers between devices with their start and end apart: 17, of which 9 were waited for; matrix products, arithmetic and copies ran while one was open for 0% of the time, Pallas kernels for 15%

profile of v8, /device:TPU:2, one launch (start us, length us, event | category | flops | bytes accessed | tf_op | source)
XLA Modules:
  0.0 136.4 jit_solution(11128634072609010945)
XLA Ops:
  0.6 5.2 %collective-permute-start = (bf16[24,2048]{1,0:T(8,128)(2,1)}, bf16[24,2048]{1,0:T(8,128)(2,1)S(1)}, u32[]{:S(2)}, u32[]{:S(2)}) collective-permute-start(bf16[24,2048]{1,0:T(8,128)(2,1)} %bitcast.55), channel_id=1, source_target_pairs={{0,2},{2,0},{1,3},{3,1},{4,6},{6,4},{5,7},{7,5},{8,10},{10,8},{9,1... | collective-permute-start | bytes 294920 | tf_op jit(solution)/shard_map/ppermute | solution.py:399
  6.8 2.6 %pack.1.array_ref = bf16[256,2560]{1,0:T(8,128)(2,1)} custom-call(bf16[256,128]{1,0:T(8,128)(2,1)S(1)} %get-tuple-element.15.place_ref, bf16[256,128]{1,0:T(8,128)(2,1)S(1)} %get-tuple-element.16.fold_ref, bf16[128,2048]{1,0:T(8,128)(2,1)} %rows_in.1), custom_call_target="tpu_custom_call" | custom-call | flops 335544320 | bytes 2621440 | tf_op jit(solution)/shard_map/pack/pallas_call | solution.py:417
  10.7 20.6 %all-to-all-start = ((bf16[32,8,2560]{2,1,0:T(8,128)(2,1)}), bf16[32,8,2560]{2,1,0:T(8,128)(2,1)S(1)}, u32[]{:S(2)}, u32[]{:S(2)}) async-start(bf16[32,8,2560]{2,1,0:T(8,128)(2,1)} %bitcast.67), calls=%async_computation | async-start | bytes 2621440 | tf_op jit(solution)/shard_map/all_to_all | solution.py:432
  31.3 6.2 %collective-permute-start.1 = (bf16[2,24,2048]{2,1,0:T(8,128)(2,1)S(1)}, bf16[2,24,2048]{2,1,0:T(8,128)(2,1)S(1)}, u32[]{:S(2)}, u32[]{:S(2)}) collective-permute-start(bf16[2,24,2048]{2,1,0:T(8,128)(2,1)S(1)} %paired.1.refs_0_), channel_id=1, source_target_pairs={{0,28},{4,0},{8,4},{12,8},{16,12},{20,16},{24,20},{28,24},{1,29},{... | collective-permute-start | bytes 589832 | tf_op jit(solution)/shard_map/ppermute | solution.py:273
  40.8 5.6 %collective-permute-start.2 = (bf16[2,24,2048]{2,1,0:T(8,128)(2,1)S(1)}, bf16[2,24,2048]{2,1,0:T(8,128)(2,1)S(1)}, u32[]{:S(2)}, u32[]{:S(2)}) collective-permute-start(bf16[2,24,2048]{2,1,0:T(8,128)(2,1)S(1)} %collective-permute-done.1.refs_1_), channel_id=1, source_target_pairs={{0,28},{4,0},{8,4},{12,8},{16,12},{20,16},{24,20},{28,24},{1,29},{... | collective-permute-start | bytes 589832 | tf_op jit(solution)/shard_map/ppermute | solution.py:273
  49.6 5.6 %collective-permute-start.3 = (bf16[2,24,2048]{2,1,0:T(8,128)(2,1)S(1)}, bf16[2,24,2048]{2,1,0:T(8,128)(2,1)S(1)}, u32[]{:S(2)}, u32[]{:S(2)}) collective-permute-start(bf16[2,24,2048]{2,1,0:T(8,128)(2,1)S(1)} %collective-permute-done.2.refs_2_), channel_id=1, source_target_pairs={{0,28},{4,0},{8,4},{12,8},{16,12},{20,16},{24,20},{28,24},{1,29},{... | collective-permute-start | bytes 589832 | tf_op jit(solution)/shard_map/ppermute | solution.py:273
  58.3 5.6 %collective-permute-start.4 = (bf16[2,24,2048]{2,1,0:T(8,128)(2,1)S(1)}, bf16[2,24,2048]{2,1,0:T(8,128)(2,1)}, u32[]{:S(2)}, u32[]{:S(2)}) collective-permute-start(bf16[2,24,2048]{2,1,0:T(8,128)(2,1)S(1)} %collective-permute-done.3.refs_3_), channel_id=1, source_target_pairs={{0,28},{4,0},{8,4},{12,8},{16,12},{20,16},{24,20},{28,24},{1,29},{... | collective-permute-start | bytes 589832 | tf_op jit(solution)/shard_map/ppermute | solution.py:273
  67.1 2.1 %placed.1 = bf16[16,24,2048]{2,1,0:T(8,128)(2,1)S(1)} custom-call(s32[4]{0:T(128)S(1)} %pad_add_fusion.place_ref, bf16[2,24,2048]{2,1,0:T(8,128)(2,1)} %copy-done, bf16[2,24,2048]{2,1,0:T(8,128)(2,1)} %copy-done.11, bf16[2,24,2048]{2,1,0:T(8,128)(2,1)} %copy-done.13, bf16[2,24,2048]{2,1,0:T(8,128)(2,1)} %copy-done.15, ...), custom_call_target="tpu_custom_call" | custom-call | tf_op jit(solution)/shard_map/placed/pallas_call | solution.py:278
  71.2 2.4 %half_sent.1 = bf16[384,2048]{1,0:T(8,128)(2,1)} custom-call(bf16[768,256]{1,0:T(8,128)(2,1)S(1)} %get-tuple-element.13.main_t_ref, bf16[768,64]{1,0:T(8,128)(2,1)S(1)} %get-tuple-element.14.extra_t_ref, bf16[256,2560]{1,0:T(8,128)(2,1)S(1)} %bitcast.48, bf16[8,128]{1,0:T(8,128)(2,1)S(1)} %slice.49.refs_0_), custom_call_target="tpu_custom_call" | custom-call | flops 503316480 | bytes 4718592 | tf_op jit(solution)/shard_map/half_sent/pallas_call | solution.py:159
  73.6 2.4 %collective-permute-start.9 = (bf16[384,2048]{1,0:T(8,128)(2,1)}, bf16[384,2048]{1,0:T(8,128)(2,1)S(1)}, u32[]{:S(2)}, u32[]{:S(2)}) collective-permute-start(bf16[384,2048]{1,0:T(8,128)(2,1)} %half_sent.1), channel_id=1, source_target_pairs={{0,1},{1,0},{2,3},{3,2},{4,5},{5,4},{6,7},{7,6},{8,9},{9,8},{10,11... | collective-permute-start | bytes 4718600 | tf_op jit(solution)/shard_map/ppermute | solution.py:455
  76.0 2.9 %product_of_own.1 = (bf16[384,256]{1,0:T(8,128)(2,1)S(1)}, bf16[384,64]{1,0:T(8,128)(2,1)S(1)}, f32[32,128]{1,0:T(8,128)S(1)}) custom-call(s32[4]{0:T(128)S(1)} %pad_add_fusion.place_ref, bf16[768,256]{1,0:T(8,128)(2,1)S(1)} %get-tuple-element.13.main_t_ref, bf16[768,64]{1,0:T(8,128)(2,1)S(1)} %get-tuple-element.14.extra_t_ref, ...), custom_call_target="tpu_custom_call" | custom-call | flops 503316480 | tf_op jit(solution)/shard_map/product_of_own/pallas_call | solution.py:209
  79.0 3.9 %product_of_other.1 = (bf16[384,256]{1,0:T(8,128)(2,1)S(1)}, bf16[384,64]{1,0:T(8,128)(2,1)S(1)}, f32[32,128]{1,0:T(8,128)S(1)}) custom-call(s32[4]{0:T(128)S(1)} %pad_add_fusion.place_ref, bf16[768,256]{1,0:T(8,128)(2,1)S(1)} %get-tuple-element.13.main_t_ref, bf16[768,64]{1,0:T(8,128)(2,1)S(1)} %get-tuple-element.14.extra_t_ref, ...), custom_call_target="tpu_custom_call" | custom-call | flops 503316480 | tf_op jit(solution)/shard_map/product_of_other/pallas_call | solution.py:209
  82.8 2.4 %half_kept.1 = bf16[384,2048]{1,0:T(8,128)(2,1)} custom-call(bf16[768,256]{1,0:T(8,128)(2,1)S(1)} %get-tuple-element.13.main_t_ref, bf16[768,64]{1,0:T(8,128)(2,1)S(1)} %get-tuple-element.14.extra_t_ref, bf16[256,2560]{1,0:T(8,128)(2,1)S(1)} %bitcast.51, bf16[384,2048]{1,0:T(8,128)(2,1)S(1)} %collective-permute-done.9.refs_0_, ...), custom_call_target="tpu_custom_call" | custom-call | flops 503316480 | bytes 4718592 | tf_op jit(solution)/shard_map/half_kept/pallas_call | solution.py:159
  85.3 5.9 %all-to-all-start.1 = ((bf16[16,24,2048]{2,1,0:T(8,128)(2,1)}), bf16[16,24,2048]{2,1,0:T(8,128)(2,1)S(1)}, u32[]{:S(2)}, u32[]{:S(2)}) async-start(bf16[16,24,2048]{2,1,0:T(8,128)(2,1)} %bitcast.68), calls=%async_computation.1 | async-start | bytes 3145728 | tf_op jit(solution)/shard_map/all_to_all | solution.py:459
  93.4 3.4 %collective-permute-done.10 = f32[16,1,128]{2,0,1:T(8,128)S(1)} collective-permute-done((f32[16,1,128]{2,0,1:T(8,128)S(1)}, f32[16,1,128]{2,0,1:T(8,128)S(1)}, u32[]{:S(2)}, u32[]{:S(2)}) %collective-permute-start.10) | collective-permute-done | bytes 8224 | tf_op jit(solution)/shard_map/ppermute | solution.py:316
  96.8 4.3 %collective-permute-start.11 = (f32[8,2,128]{2,0,1:T(8,128)S(1)}, f32[8,2,128]{2,0,1:T(8,128)S(1)}, u32[]{:S(2)}, u32[]{:S(2)}) collective-permute-start(f32[8,2,128]{2,0,1:T(8,128)S(1)} %bitcast.77), channel_id=1, source_target_pairs={{0,64},{32,96},{64,0},{96,32},{128,192},{160,224},{192,128},{224,1... | collective-permute-start | bytes 24584 | tf_op jit(solution)/shard_map/ppermute | solution.py:316
  101.1 2.2 %collective-permute-done.11 = f32[8,2,128]{2,0,1:T(8,128)S(1)} collective-permute-done((f32[8,2,128]{2,0,1:T(8,128)S(1)}, f32[8,2,128]{2,0,1:T(8,128)S(1)}, u32[]{:S(2)}, u32[]{:S(2)}) %collective-permute-start.11) | collective-permute-done | bytes 8224 | tf_op jit(solution)/shard_map/ppermute | solution.py:316
  103.3 6.5 %collective-permute-start.12 = (f32[4,4,128]{2,0,1:T(4,128)S(1)}, f32[4,4,128]{2,0,1:T(4,128)S(1)}, u32[]{:S(2)}, u32[]{:S(2)}) collective-permute-start(f32[4,4,128]{2,0,1:T(4,128)S(1)} %bitcast.80), channel_id=1, source_target_pairs={{0,128},{32,160},{64,192},{96,224},{128,0},{160,32},{192,64},{224,... | collective-permute-start | bytes 24584 | tf_op jit(solution)/shard_map/ppermute | solution.py:316
  109.7 3.0 %collective-permute-done.12 = f32[4,4,128]{2,0,1:T(4,128)S(1)} collective-permute-done((f32[4,4,128]{2,0,1:T(4,128)S(1)}, f32[4,4,128]{2,0,1:T(4,128)S(1)}, u32[]{:S(2)}, u32[]{:S(2)}) %collective-permute-start.12) | collective-permute-done | bytes 8224 | tf_op jit(solution)/shard_map/ppermute | solution.py:316
  112.7 4.3 %collective-permute-start.13 = (f32[2,8,128]{2,1,0:T(8,128)S(1)}, f32[2,8,128]{2,1,0:T(8,128)S(1)}, u32[]{:S(2)}, u32[]{:S(2)}) collective-permute-start(f32[2,8,128]{2,1,0:T(8,128)S(1)} %get-tuple-element.26), channel_id=1, source_target_pairs={{0,256},{256,0},{512,768},{768,512},{1,257},{257,1},{513,769},{769... | collective-permute-start | bytes 24584 | tf_op jit(solution)/shard_map/ppermute | solution.py:316
  117.0 2.3 %collective-permute-done.13 = f32[2,8,128]{2,1,0:T(8,128)S(1)} collective-permute-done((f32[2,8,128]{2,1,0:T(8,128)S(1)}, f32[2,8,128]{2,1,0:T(8,128)S(1)}, u32[]{:S(2)}, u32[]{:S(2)}) %collective-permute-start.13) | collective-permute-done | bytes 8224 | tf_op jit(solution)/shard_map/ppermute | solution.py:316
  119.3 7.3 %collective-permute-start.14 = (f32[1,16,128]{2,1,0:T(8,128)S(1)}, f32[1,16,128]{2,1,0:T(8,128)S(1)}, u32[]{:S(2)}, u32[]{:S(2)}) collective-permute-start(f32[1,16,128]{2,1,0:T(8,128)S(1)} %get-tuple-element.24), channel_id=1, source_target_pairs={{0,512},{256,768},{512,0},{768,256},{1,513},{257,769},{513,1},{769... | collective-permute-start | bytes 24584 | tf_op jit(solution)/shard_map/ppermute | solution.py:316
  126.6 2.5 %order.1 = bf16[320,768]{1,0:T(8,128)(2,1)} custom-call(s32[4]{0:T(128)S(1)} %pad_add_fusion.place_ref, bf16[384,256]{1,0:T(8,128)(2,1)S(1)} %copy-done.8, bf16[384,64]{1,0:T(8,128)(2,1)S(1)} %copy-done.10, bf16[384,256]{1,0:T(8,128)(2,1)S(1)} %get-tuple-element.20.other_main, bf16[384,64]{1,0:T(8,128)(2,1)S(1)} %get-tuple-element.21.other_extra), custom_call_target="tpu_custom_call" | custom-call | flops 377487360 | bytes 983040 | tf_op jit(solution)/shard_map/order/pallas_call | solution.py:465
  129.2 4.2 %collective-permute-done.14 = f32[1,16,128]{2,1,0:T(8,128)S(1)} collective-permute-done((f32[1,16,128]{2,1,0:T(8,128)S(1)}, f32[1,16,128]{2,1,0:T(8,128)S(1)}, u32[]{:S(2)}, u32[]{:S(2)}) %collective-permute-start.14) | collective-permute-done | bytes 8224 | tf_op jit(solution)/shard_map/ppermute | solution.py:316
  (70 shorter events, 22.2 us)
Async XLA Ops:
  0.6 8.7 %collective-permute-start = (bf16[24,2048]{1,0:T(8,128)(2,1)}, bf16[24,2048]{1,0:T(8,128)(2,1)S(1)}, u32[]{:S(2)}, u32[]{:S(2)}) collective-permute-start(bf16[24,2048]{1,0:T(8,128)(2,1)} %bitcast.55), channel_id=1, source_target_pairs={{0,2},{2,0},{1,3},{3,1},{4,6},{6,4},{5,7},{7,5},{8,10},{10,8},{9,1... | collective-permute-start | bytes 294920 | tf_op jit(solution)/shard_map/ppermute | solution.py:399
  10.6 53.4 %copy-start.6 = (bf16[1,1,32,10,768]{4,2,3,1,0:T(8,128)(2,1)S(1)}, bf16[1,1,32,10,768]{4,2,3,1,0:T(8,128)(2,1)}, u32[]{:S(2)}) copy-start(bf16[1,1,32,10,768]{4,2,3,1,0:T(8,128)(2,1)} %param.12) | copy-start | bytes 1474564
  10.7 60.5 %all-to-all-start = ((bf16[32,8,2560]{2,1,0:T(8,128)(2,1)}), bf16[32,8,2560]{2,1,0:T(8,128)(2,1)S(1)}, u32[]{:S(2)}, u32[]{:S(2)}) async-start(bf16[32,8,2560]{2,1,0:T(8,128)(2,1)} %bitcast.67), calls=%async_computation | async-start | bytes 2621440 | tf_op jit(solution)/shard_map/all_to_all | solution.py:432
  31.3 9.5 %collective-permute-start.1 = (bf16[2,24,2048]{2,1,0:T(8,128)(2,1)S(1)}, bf16[2,24,2048]{2,1,0:T(8,128)(2,1)S(1)}, u32[]{:S(2)}, u32[]{:S(2)}) collective-permute-start(bf16[2,24,2048]{2,1,0:T(8,128)(2,1)S(1)} %paired.1.refs_0_), channel_id=1, source_target_pairs={{0,28},{4,0},{8,4},{12,8},{16,12},{20,16},{24,20},{28,24},{1,29},{... | collective-permute-start | bytes 589832 | tf_op jit(solution)/shard_map/ppermute | solution.py:273
  37.5 8.9 %collective-permute-start.5 = (bf16[2,24,2048]{2,1,0:T(8,128)(2,1)S(1)}, bf16[2,24,2048]{2,1,0:T(8,128)(2,1)S(1)}, u32[]{:S(2)}, u32[]{:S(2)}) collective-permute-start(bf16[2,24,2048]{2,1,0:T(8,128)(2,1)S(1)} %paired.1.refs_0_), channel_id=1, source_target_pairs={{0,4},{4,8},{8,12},{12,16},{16,20},{20,24},{24,28},{28,0},{1,5},{5... | collective-permute-start | bytes 589832 | tf_op jit(solution)/shard_map/ppermute | solution.py:276
  40.8 8.8 %collective-permute-start.2 = (bf16[2,24,2048]{2,1,0:T(8,128)(2,1)S(1)}, bf16[2,24,2048]{2,1,0:T(8,128)(2,1)S(1)}, u32[]{:S(2)}, u32[]{:S(2)}) collective-permute-start(bf16[2,24,2048]{2,1,0:T(8,128)(2,1)S(1)} %collective-permute-done.1.refs_1_), channel_id=1, source_target_pairs={{0,28},{4,0},{8,4},{12,8},{16,12},{20,16},{24,20},{28,24},{1,29},{... | collective-permute-start | bytes 589832 | tf_op jit(solution)/shard_map/ppermute | solution.py:273
  46.4 8.8 %collective-permute-start.6 = (bf16[2,24,2048]{2,1,0:T(8,128)(2,1)S(1)}, bf16[2,24,2048]{2,1,0:T(8,128)(2,1)S(1)}, u32[]{:S(2)}, u32[]{:S(2)}) collective-permute-start(bf16[2,24,2048]{2,1,0:T(8,128)(2,1)S(1)} %collective-permute-done.5.refs_7_), channel_id=1, source_target_pairs={{0,4},{4,8},{8,12},{12,16},{16,20},{20,24},{24,28},{28,0},{1,5},{5... | collective-permute-start | bytes 589832 | tf_op jit(solution)/shard_map/ppermute | solution.py:276
  49.6 8.8 %collective-permute-start.3 = (bf16[2,24,2048]{2,1,0:T(8,128)(2,1)S(1)}, bf16[2,24,2048]{2,1,0:T(8,128)(2,1)S(1)}, u32[]{:S(2)}, u32[]{:S(2)}) collective-permute-start(bf16[2,24,2048]{2,1,0:T(8,128)(2,1)S(1)} %collective-permute-done.2.refs_2_), channel_id=1, source_target_pairs={{0,28},{4,0},{8,4},{12,8},{16,12},{20,16},{24,20},{28,24},{1,29},{... | collective-permute-start | bytes 589832 | tf_op jit(solution)/shard_map/ppermute | solution.py:273
  55.2 10.3 %collective-permute-start.7 = (bf16[2,24,2048]{2,1,0:T(8,128)(2,1)S(1)}, bf16[2,24,2048]{2,1,0:T(8,128)(2,1)S(1)}, u32[]{:S(2)}, u32[]{:S(2)}) collective-permute-start(bf16[2,24,2048]{2,1,0:T(8,128)(2,1)S(1)} %collective-permute-done.6.refs_6_), channel_id=1, source_target_pairs={{0,4},{4,8},{8,12},{12,16},{16,20},{20,24},{24,28},{28,0},{1,5},{5... | collective-permute-start | bytes 589832 | tf_op jit(solution)/shard_map/ppermute | solution.py:276
  58.3 8.8 %collective-permute-start.4 = (bf16[2,24,2048]{2,1,0:T(8,128)(2,1)S(1)}, bf16[2,24,2048]{2,1,0:T(8,128)(2,1)}, u32[]{:S(2)}, u32[]{:S(2)}) collective-permute-start(bf16[2,24,2048]{2,1,0:T(8,128)(2,1)S(1)} %collective-permute-done.3.refs_3_), channel_id=1, source_target_pairs={{0,28},{4,0},{8,4},{12,8},{16,12},{20,16},{24,20},{28,24},{1,29},{... | collective-permute-start | bytes 589832 | tf_op jit(solution)/shard_map/ppermute | solution.py:273
  69.2 9.7 %collective-permute-start.8 = (bf16[384,2048]{1,0:T(8,128)(2,1)S(1)}, bf16[384,2048]{1,0:T(8,128)(2,1)}, u32[]{:S(2)}, u32[]{:S(2)}) collective-permute-start(bf16[384,2048]{1,0:T(8,128)(2,1)S(1)} %bitcast.52), channel_id=1, source_target_pairs={{0,1},{1,0},{2,3},{3,2},{4,5},{5,4},{6,7},{7,6},{8,9},{9,8},{10,11... | collective-permute-start | bytes 4718600 | tf_op jit(solution)/shard_map/ppermute | solution.py:438
  73.6 9.2 %collective-permute-start.9 = (bf16[384,2048]{1,0:T(8,128)(2,1)}, bf16[384,2048]{1,0:T(8,128)(2,1)S(1)}, u32[]{:S(2)}, u32[]{:S(2)}) collective-permute-start(bf16[384,2048]{1,0:T(8,128)(2,1)} %half_sent.1), channel_id=1, source_target_pairs={{0,1},{1,0},{2,3},{3,2},{4,5},{5,4},{6,7},{7,6},{8,9},{9,8},{10,11... | collective-permute-start | bytes 4718600 | tf_op jit(solution)/shard_map/ppermute | solution.py:455
  85.2 41.4 %copy-start.8 = (bf16[384,256]{1,0:T(8,128)(2,1)S(1)}, bf16[384,256]{1,0:T(8,128)(2,1)}, u32[]{:S(2)}) copy-start(bf16[384,256]{1,0:T(8,128)(2,1)} %copy-done.7) | copy-start | bytes 589828
  85.3 41.4 %copy-start.10 = (bf16[384,64]{1,0:T(8,128)(2,1)S(1)}, bf16[384,64]{1,0:T(8,128)(2,1)}, u32[]{:S(2)}) copy-start(bf16[384,64]{1,0:T(8,128)(2,1)} %copy-done.9) | copy-start | bytes 147460
  85.3 49.6 %all-to-all-start.1 = ((bf16[16,24,2048]{2,1,0:T(8,128)(2,1)}), bf16[16,24,2048]{2,1,0:T(8,128)(2,1)S(1)}, u32[]{:S(2)}, u32[]{:S(2)}) async-start(bf16[16,24,2048]{2,1,0:T(8,128)(2,1)} %bitcast.68), calls=%async_computation.1 | async-start | bytes 3145728 | tf_op jit(solution)/shard_map/all_to_all | solution.py:459
  91.2 42.2 %copy-start.2 = (f32[128,8]{0,1:T(8,128)S(1)}, f32[128,8]{0,1:T(8,128)}, u32[]{:S(2)}) copy-start(f32[128,8]{0,1:T(8,128)} %param.8) | copy-start | bytes 12292
  91.2 42.2 %copy-start.3 = (s32[128,8]{0,1:T(8,128)S(1)}, s32[128,8]{0,1:T(8,128)}, u32[]{:S(2)}) copy-start(s32[128,8]{0,1:T(8,128)} %param.9) | copy-start | bytes 12292
  91.2 42.2 %copy-start.4 = (s32[128,8]{0,1:T(8,128)S(1)}, s32[128,8]{0,1:T(8,128)}, u32[]{:S(2)}) copy-start(s32[128,8]{0,1:T(8,128)} %param.10) | copy-start | bytes 12292
  91.2 42.2 %copy-start.5 = (f32[128,8]{0,1:T(8,128)S(1)}, f32[128,8]{0,1:T(8,128)}, u32[]{:S(2)}) copy-start(f32[128,8]{0,1:T(8,128)} %param.11) | copy-start | bytes 12292
  91.2 5.5 %collective-permute-start.10 = (f32[16,1,128]{2,0,1:T(8,128)S(1)}, f32[16,1,128]{2,0,1:T(8,128)S(1)}, u32[]{:S(2)}, u32[]{:S(2)}) collective-permute-start(f32[16,1,128]{2,0,1:T(8,128)S(1)} %bitcast.78), channel_id=1, source_target_pairs={{0,32},{32,0},{64,96},{96,64},{128,160},{160,128},{192,224},{224,1... | collective-permute-start | bytes 24584 | tf_op jit(solution)/shard_map/ppermute | solution.py:316
  96.8 6.4 %collective-permute-start.11 = (f32[8,2,128]{2,0,1:T(8,128)S(1)}, f32[8,2,128]{2,0,1:T(8,128)S(1)}, u32[]{:S(2)}, u32[]{:S(2)}) collective-permute-start(f32[8,2,128]{2,0,1:T(8,128)S(1)} %bitcast.77), channel_id=1, source_target_pairs={{0,64},{32,96},{64,0},{96,32},{128,192},{160,224},{192,128},{224,1... | collective-permute-start | bytes 24584 | tf_op jit(solution)/shard_map/ppermute | solution.py:316
  103.3 9.5 %collective-permute-start.12 = (f32[4,4,128]{2,0,1:T(4,128)S(1)}, f32[4,4,128]{2,0,1:T(4,128)S(1)}, u32[]{:S(2)}, u32[]{:S(2)}) collective-permute-start(f32[4,4,128]{2,0,1:T(4,128)S(1)} %bitcast.80), channel_id=1, source_target_pairs={{0,128},{32,160},{64,192},{96,224},{128,0},{160,32},{192,64},{224,... | collective-permute-start | bytes 24584 | tf_op jit(solution)/shard_map/ppermute | solution.py:316
  112.7 6.6 %collective-permute-start.13 = (f32[2,8,128]{2,1,0:T(8,128)S(1)}, f32[2,8,128]{2,1,0:T(8,128)S(1)}, u32[]{:S(2)}, u32[]{:S(2)}) collective-permute-start(f32[2,8,128]{2,1,0:T(8,128)S(1)} %get-tuple-element.26), channel_id=1, source_target_pairs={{0,256},{256,0},{512,768},{768,512},{1,257},{257,1},{513,769},{769... | collective-permute-start | bytes 24584 | tf_op jit(solution)/shard_map/ppermute | solution.py:316
  119.3 14.1 %collective-permute-start.14 = (f32[1,16,128]{2,1,0:T(8,128)S(1)}, f32[1,16,128]{2,1,0:T(8,128)S(1)}, u32[]{:S(2)}, u32[]{:S(2)}) collective-permute-start(f32[1,16,128]{2,1,0:T(8,128)S(1)} %get-tuple-element.24), channel_id=1, source_target_pairs={{0,512},{256,768},{512,0},{768,256},{1,513},{257,769},{513,1},{769... | collective-permute-start | bytes 24584 | tf_op jit(solution)/shard_map/ppermute | solution.py:316
  (10 other events, 86.4 us)
